TPU v7x, 256 devices: a whole 4x4x8 slice. The times are simulated.
256 devices in a mesh: segment: 4 (over z_hi, core), expert: 64 (over y, x, z_lo).
Axes of the slice: x: 4, y: 4, z: 8 (z_hi: 2, z_lo: 4; z = z_hi * 4 + z_lo), core: 2. Of those that a mesh axis runs over, the one named last changes fastest.
Arguments:
- x_fwd: bfloat16 [512, 7168], P(('segment', 'expert')), may hold values from -6 to 6
- ids_fwd: int32 [512, 4], P('segment'), may hold values from 0 to 7, all different within a row; in each aligned block of 2 rows (0 to 1, 2 to 3, ...) at most 2 rows name the same one
- probs_fwd: bfloat16 [512, 4], P('segment'), may hold values from 0.049804688 to 0.44921875
- x_bwd: bfloat16 [512, 7168], P(('segment', 'expert')), may hold values from -6 to 6
- ids_bwd: int32 [512, 4], P('segment'), may hold values from 0 to 7, all different within a row; in each aligned block of 2 rows (0 to 1, 2 to 3, ...) at most 2 rows name the same one
- probs_bwd: bfloat16 [512, 4], P('segment'), may hold values from 0.049804688 to 0.44921875
- grad_out: bfloat16 [512, 7168], P(('segment', 'expert')), may hold values from -6 to 6
- w_gate: bfloat16 [4, 7168, 16384], P('segment', None, 'expert'), may hold values from -0.0625 to 0.0625
- w_up: bfloat16 [4, 7168, 16384], P('segment', None, 'expert'), may hold values from -0.0625 to 0.0625
- w_down: bfloat16 [4, 16384, 7168], P('segment', 'expert'), may hold values from -0.125 to 0.125
Outputs:
- fwd_next: bfloat16 [512, 7168], P(('segment', 'expert'))
- bwd_next: bfloat16 [512, 7168], P(('segment', 'expert'))
- dprob: float32 [512, 4], P(('segment', 'expert'))
Inputs may be any that keep to these rules, and one draw needn't show every extreme that they name: `ids_fwd`: in each aligned block of 2 rows (the tokens of one device) a row names 4 distinct experts and no expert is named by more than 2 rows; some block reaches 2. The same holds for ids_bwd. `ids_bwd`: as for ids_fwd.
All inputs are finite; a program needn't handle non-finite values.
Results may differ from a plain program's by a relative error of at most 0.0038.
Values may be sent and summed in bfloat16 or wider, within the bound.
No kernel may reach another device: no remote copies, remote signals or barrier semaphores. Data moves between devices by JAX's collectives and lax.ppermute only.
A program may use at most 128 MiB of HBM per device.

v0:
```python
import jax
import jax.numpy as jnp
from jax import lax
from jax.sharding import PartitionSpec as P

EXP_WIN = 8
TOPK_WIN = 4


def passed_along(value, axis, by):
    length = lax.axis_size(axis)
    return lax.ppermute(value, axis, [(i, (i + by) % length) for i in range(length)])


def contract_last(left, right):
    return lax.dot_general(
        left, right, (((1,), (1,)), ((), ())), preferred_element_type=jnp.float32
    )


def expert_forward(picked, w_g, w_u, w_d):
    gate_act = jnp.dot(picked, w_g, preferred_element_type=jnp.float32)
    up_act = jnp.dot(picked, w_u, preferred_element_type=jnp.float32)
    hidden = (jax.nn.silu(gate_act) * up_act).astype(jnp.bfloat16)
    return jnp.dot(hidden, w_d, preferred_element_type=jnp.float32)


def expert_backward(picked, grad_rows, grad_plain, w_g, w_u, w_d):
    gate_act = jnp.dot(picked, w_g, preferred_element_type=jnp.float32)
    up_act = jnp.dot(picked, w_u, preferred_element_type=jnp.float32)
    silu_gate = jax.nn.silu(gate_act)
    hidden = (silu_gate * up_act).astype(jnp.bfloat16)
    expert_out = jnp.dot(hidden, w_d, preferred_element_type=jnp.float32)
    inner = jnp.sum(grad_plain.astype(jnp.float32) * expert_out, axis=-1)
    grad_hidden = contract_last(grad_rows, w_d)
    sig = jax.nn.sigmoid(gate_act)
    dsilu = sig * (1.0 + gate_act * (1.0 - sig))
    grad_gate = (grad_hidden * up_act * dsilu).astype(jnp.bfloat16)
    grad_up = (grad_hidden * silu_gate).astype(jnp.bfloat16)
    grad_input = contract_last(grad_gate, w_g) + contract_last(grad_up, w_u)
    return (grad_input, inner)


def route_ranks(ids, tok_rows):
    all_rows, routes = ids.shape
    one_hot = (ids[:, :, None] == jnp.arange(EXP_WIN, dtype=jnp.int32)).astype(jnp.int32)
    grouped = one_hot.reshape(all_rows // tok_rows, tok_rows * routes, EXP_WIN)
    before = jnp.cumsum(grouped, axis=1) - grouped
    return jnp.sum((before * grouped).reshape(all_rows, routes, EXP_WIN), axis=-1)


def slot_tables(ids, probs, expert_id, tok_rows, capacity):
    all_rows = ids.shape[0]
    route_rank = route_ranks(ids, tok_rows)
    is_mine = ids == expert_id
    routed = jnp.any(is_mine, axis=-1)
    weight = jnp.sum(jnp.where(is_mine, probs.astype(jnp.float32), 0.0), axis=-1)
    rank_tok = jnp.sum(jnp.where(is_mine, route_rank, 0), axis=-1)
    source = jnp.arange(all_rows, dtype=jnp.int32) // tok_rows
    slot_tok = source * capacity + rank_tok
    slot_count = all_rows // tok_rows * capacity
    matches = (slot_tok[None, :] == jnp.arange(slot_count, dtype=jnp.int32)[:, None]) & routed[
        None, :
    ]
    token_ids = jnp.sum(
        jnp.where(matches, jnp.arange(all_rows, dtype=jnp.int32)[None, :], 0), axis=-1
    )
    filled = jnp.any(matches, axis=-1)
    return (is_mine, slot_tok, routed, weight, token_ids, filled)


def pick_rows(source_rows, token_ids, filled):
    taken = jnp.take(source_rows, token_ids, axis=0)
    return jnp.where(filled[:, None], taken, jnp.zeros((), source_rows.dtype))


def body(x_fwd, ids_fwd, probs_fwd, x_bwd, ids_bwd, probs_bwd, grad_out, w_gate, w_up, w_down):
    tok_rows = x_fwd.shape[0]
    slices = lax.axis_size("expert") // EXP_WIN
    capacity = max(2, 3 * tok_rows * TOPK_WIN // (2 * EXP_WIN))
    w_g = w_gate[0]
    w_u = w_up[0]
    w_d = w_down[0]
    expert_id = lax.axis_index("expert") // slices
    xf_all, xb_all, grad_all = (
        lax.all_gather(x_fwd, "expert", axis=0, tiled=True),
        lax.all_gather(x_bwd, "expert", axis=0, tiled=True),
        lax.all_gather(grad_out, "expert", axis=0, tiled=True),
    )
    mine_f, slot_f, routed_f, weight_f, token_f, filled_f = slot_tables(
        ids_fwd, probs_fwd, expert_id, tok_rows, capacity
    )
    mine_b, slot_b, routed_b, weight_b, token_b, filled_b = slot_tables(
        ids_bwd, probs_bwd, expert_id, tok_rows, capacity
    )
    partial_value = expert_forward(pick_rows(xf_all, token_f, filled_f), w_g, w_u, w_d)
    moe_fwd = lax.psum_scatter(
        weight_f[:, None] * jnp.take(partial_value, slot_f, axis=0),
        "expert",
        scatter_dimension=0,
        tiled=True,
    )
    picked_b = pick_rows(xb_all, token_b, filled_b)
    grad_picked = pick_rows(grad_all, token_b, filled_b)
    slot_weight = jnp.where(filled_b, jnp.take(weight_b, token_b), 0.0)
    grad_rows = (slot_weight[:, None] * grad_picked.astype(jnp.float32)).astype(jnp.bfloat16)
    grad_input, inner = expert_backward(picked_b, grad_rows, grad_picked, w_g, w_u, w_d)
    grad_term = jnp.where(routed_b[:, None], jnp.take(grad_input, slot_b, axis=0), 0.0)
    dprob_term = jnp.where(mine_b, jnp.take(inner, slot_b)[:, None], 0.0)
    moe_bwd, dprob = (
        lax.psum_scatter(grad_term, "expert", scatter_dimension=0, tiled=True),
        lax.psum_scatter(dprob_term, "expert", scatter_dimension=0, tiled=True),
    )
    layer_out = (x_fwd.astype(jnp.float32) + moe_fwd).astype(jnp.bfloat16)
    fwd_next = passed_along(layer_out, "segment", 1)
    input_grad = (grad_out.astype(jnp.float32) + moe_bwd).astype(jnp.bfloat16)
    bwd_next = passed_along(input_grad, "segment", -1)
    return (fwd_next, bwd_next, dprob)


def solution(mesh):
    return jax.shard_map(
        body,
        mesh=mesh,
        in_specs=(
            P(("segment", "expert"), None),
            P("segment", None),
            P("segment", None),
            P(("segment", "expert"), None),
            P("segment", None),
            P("segment", None),
            P(("segment", "expert"), None),
            P("segment", None, "expert"),
            P("segment", None, "expert"),
            P("segment", "expert", None),
        ),
        out_specs=(
            P(("segment", "expert"), None),
            P(("segment", "expert"), None),
            P(("segment", "expert"), None),
        ),
        check_vma=False,
    )
```

profile of v0, /device:TPU:1, one launch (start us, length us, event | category | flops | bytes accessed | tf_op | source)
XLA Modules:
  0.0 1887.9 jit_solution(7634872450114210314)
XLA Ops:
  15.7 303.1 %all-gather.11.cloned.1.call-done = bf16[64,2,7168]{2,1,0:T(2,128)(2,1)} async-done(((bf16[1,2,7168]{2,1,0:T(2,128)(2,1)}), bf16[64,2,7168]{2,1,0:T(2,128)(2,1)}) %all-gather.11.cloned.1.call-update) | async-done | bytes 1835024 | tf_op jit(solution)/shard_map/all_gather | solution.py:87
  318.9 4.1 reshape.141
  322.9 3.0 gather_fusion.4
  325.9 341.8 %all-gather.9.cloned.1.call-done = bf16[64,2,7168]{2,1,0:T(2,128)(2,1)} async-done(((bf16[1,2,7168]{2,1,0:T(2,128)(2,1)}), bf16[64,2,7168]{2,1,0:T(2,128)(2,1)}) %all-gather.9.cloned.1.call-update) | async-done | bytes 1835024 | tf_op jit(solution)/shard_map/all_gather | solution.py:88
  667.7 4.1 reshape.139
  671.7 2.9 gather_fusion.3
  674.7 3.4 fusion.13
  679.6 336.9 %all-gather.7.cloned.1.call-done = bf16[64,2,7168]{2,1,0:T(2,128)(2,1)} async-done(((bf16[1,2,7168]{2,1,0:T(2,128)(2,1)}), bf16[64,2,7168]{2,1,0:T(2,128)(2,1)}) %all-gather.7.cloned.1.call-update) | async-done | bytes 1835024 | tf_op jit(solution)/shard_map/all_gather | solution.py:86
  1016.5 4.2 reshape.137
  1020.7 3.0 gather_fusion
  1023.7 3.4 fusion.15
  1027.1 7.2 fusion.4
  1034.4 4.1 fusion.2
  1038.5 1.3 fusion.11
  1040.5 3.2 convolution_add_fusion
  1043.7 7.0 gather_fusion.1
  1050.7 7.1 gather_fusion.5
  1057.9 4.9 select_select_fusion
  1062.8 2.4 select_multiply_fusion
  1067.1 3.4 fusion.19
  1071.8 317.8 %all-reduce.2 = f32[128,4]{1,0:T(8,128)S(1)} all-reduce(f32[128,4]{1,0:T(8,128)S(1)} %broadcast_select_fusion), channel_id=4, replica_groups=mesh['segment'=4,'expert'=64] {'expert'}, use_global_device_ids=true, to_apply=%region_17.21.clone | all-reduce | flops 512 | bytes 4096
  1389.6 440.5 %all-reduce.6.cloned.1.call-done = (f32[128,7168]{1,0:T(8,128)}, f32[128,7168]{1,0:T(8,128)}) async-done(((f32[128,7168]{1,0:T(8,128)}, f32[128,7168]{1,0:T(8,128)}), (f32[128,7168]{1,0:T(8,128)}, f32[128,7168]{1,0:T(8,128)})) %all-reduce.6.cloned.1.call-update) | async-done | bytes 7340048
  1832.1 41.4 %collective-permute-start.1 = (bf16[2,7168]{1,0:T(2,128)(2,1)S(1)}, bf16[2,7168]{1,0:T(2,128)(2,1)S(1)}, u32[]{:S(2)}, u32[]{:S(2)}) collective-permute-start(bf16[2,7168]{1,0:T(2,128)(2,1)S(1)} %fusion.44), channel_id=1, source_target_pairs={{0,192},{64,0},{128,64},{192,128},{1,193},{65,1},{129,65},{193,129... | collective-permute-start | bytes 86024 | tf_op jit(solution)/shard_map/ppermute | solution.py:12
  1873.5 4.9 collective-permute-start
  (76 shorter events, 18.1 us)
Async XLA Ops:
  7.2 311.7 %all-gather.11.cloned.1.call-start = ((), (), s32[]{:S(2)}) async-start(), calls=%async_computation.2 | async-start | bytes 1863680 | tf_op jit(solution)/shard_map/all_gather | solution.py:87
  7.9 659.8 %all-gather.9.cloned.1.call-start = ((), (), s32[]{:S(2)}) async-start(), calls=%async_computation.1 | async-start | bytes 1863680 | tf_op jit(solution)/shard_map/all_gather | solution.py:88
  8.7 1007.8 %all-gather.7.cloned.1.call-start = ((), (), s32[]{:S(2)}) async-start(), calls=%async_computation | async-start | bytes 1863680 | tf_op jit(solution)/shard_map/all_gather | solution.py:86
  9.4 1820.7 %all-reduce.6.cloned.1.call-start = ((), (), s32[]{:S(2)}) async-start(), calls=%async_computation.3 | async-start | bytes 14680064
  674.7 3.7 copy-start.1
  674.7 4.2 copy-start.6
  1023.7 3.4 copy-start.3
  1034.4 4.1 copy-start.4
  1038.5 2.0 copy-start.2
  1057.9 4.9 copy-start
  1065.1 0.7 copy-start.9
  1065.1 1.9 copy-start.5
  1067.1 763.0 %copy-start.7 = (bf16[2,7168]{1,0:T(2,128)(2,1)S(1)}, bf16[2,7168]{1,0:T(2,128)(2,1)}, u32[]{:S(2)}) copy-start(bf16[2,7168]{1,0:T(2,128)(2,1)} %param.16) | copy-start | bytes 86020
  1067.1 764.0 %copy-start.8 = (bf16[2,7168]{1,0:T(2,128)(2,1)S(1)}, bf16[2,7168]{1,0:T(2,128)(2,1)}, u32[]{:S(2)}) copy-start(bf16[2,7168]{1,0:T(2,128)(2,1)} %param.22) | copy-start | bytes 86020
  1832.1 48.1 %collective-permute-start.1 = (bf16[2,7168]{1,0:T(2,128)(2,1)S(1)}, bf16[2,7168]{1,0:T(2,128)(2,1)S(1)}, u32[]{:S(2)}, u32[]{:S(2)}) collective-permute-start(bf16[2,7168]{1,0:T(2,128)(2,1)S(1)} %fusion.44), channel_id=1, source_target_pairs={{0,192},{64,0},{128,64},{192,128},{1,193},{65,1},{129,65},{193,129... | collective-permute-start | bytes 86024 | tf_op jit(solution)/shard_map/ppermute | solution.py:12
  1873.5 6.7 collective-permute-start
Sparse Core Ops, SparseCore 0:
  9.8 309.0 all-gather.10
  320.6 346.9 all-gather.8
  669.5 346.9 all-gather.6
  1065.3 764.7 all-reduce.5
where the time goes:
time: 1890 us
  waiting for transfers between devices  1430 us (76%)
  blocking collectives  318 us (17%)
  starting transfers between devices  46.4 us (2%)
  local copies, waits for them, and re-layouts  46.2 us (2%)
  matrix products  26.8 us (1%)
    unnamed x5, waiting for transfers between devices  443 us
    all_gather x1, waiting for transfers between devices, body(): lax.all_gather(grad_out, 'expert', axis=0, tiled=True)  342 us
    all_gather x1, waiting for transfers between devices, body(): lax.all_gather(x_fwd, 'expert', axis=0, tiled=True)  337 us
    unnamed x1, blocking collectives  318 us
    all_gather x1, waiting for transfers between devices, body(): lax.all_gather(x_bwd, 'expert', axis=0, tiled=True)  303 us
    ppermute x2, starting transfers between devices, passed_along(): lax.ppermute(value, axis, [(i, (i + by) % length) for i in range(length)])  46.3 us
  transfers between devices with their start and end apart: 6, of which 5 were waited for; matrix products, arithmetic and copies ran while one was open for 2% of the time, Pallas kernels for 0%

commit v1 on v0

v1 whole, which is shorter than its diff:
```python
import jax
import jax.numpy as jnp
from jax import lax
from jax.experimental import pallas as pl
from jax.experimental.pallas import tpu as pltpu
from jax.sharding import PartitionSpec as P

EXP_WIN = 8
SIDE = 4
LANES = 128
CHUNKS = 4
STRIDE = {"z": 1, "x": 4, "y": 16}
F32 = jnp.float32
BF16 = jnp.bfloat16


def swap(value, along, by):
    length = lax.axis_size("expert")
    return lax.ppermute(
        value, "expert", [(i, i ^ (by * STRIDE[along])) for i in range(length)]
    )


def passed_along(value, axis, by):
    length = lax.axis_size(axis)
    return lax.ppermute(value, axis, [(i, (i + by) % length) for i in range(length)])


def handed_on(forth, back):
    length = lax.axis_size("segment")
    even = lax.axis_index("segment") % 2 == 0
    near = [(i, i ^ 1) for i in range(length)]
    far = [(i, (i - 1 if i % 2 == 0 else i + 1) % length) for i in range(length)]
    got_far = lax.ppermute(jnp.where(even, back, forth), "segment", far)
    got_near = lax.ppermute(jnp.where(even, forth, back), "segment", near)
    return jnp.where(even, got_far, got_near), jnp.where(even, got_near, got_far)


def gathered(value, along):
    return jnp.concatenate([value] + [swap(value, along, j) for j in range(1, SIDE)], axis=0)


def relayed(value, along):
    one, three = swap(value, along, 1), swap(value, along, 3)
    low, high = halves(three, one)
    return [value, one, swap(low, along, 1), swap(high, along, 3), three]


def scattered(own, others, along):
    for j, block in enumerate(others, 1):
        own = own + swap(block, along, j).astype(F32)
    return own


def cut(value, sent_as):
    blocks = value.reshape(SIDE, value.shape[0] // SIDE, value.shape[1])
    return blocks[0], [blocks[j].astype(sent_as) for j in range(1, SIDE)]


def to_other_order(value):
    rows, width = value.shape
    parts = value.reshape(SIDE, SIDE, rows // SIDE // SIDE, width)
    return parts.transpose(1, 0, 2, 3).reshape(rows, width)


def blocks_swapped(value):
    size = value.shape[0] // SIDE // SIDE
    return jnp.concatenate(
        [
            value[(b * SIDE + a) * size : (b * SIDE + a + 1) * size]
            for a in range(SIDE)
            for b in range(SIDE)
        ],
        axis=0,
    )


def contract_last(left, right):
    return lax.dot_general(
        left, right, (((1,), (1,)), ((), ())), preferred_element_type=F32
    )


def dot(left, right):
    return jnp.dot(left, right, preferred_element_type=F32)


def columns(pieces, first, step):
    return jnp.concatenate([ref[:, first : first + step] for ref in pieces], axis=0)


def halves_kernel(*refs):
    count = (len(refs) - 1) // 2
    sems = refs[-1]
    copies = []
    for i, (ref, out) in enumerate(zip(refs[:count], refs[count:-1])):
        half = out.shape[0]
        first = 0 if i % 2 == 0 else half
        copies.append(pltpu.make_async_copy(ref.at[pl.ds(first, half), :], out, sems.at[i]))
    for copy in copies:
        copy.start()
    for copy in copies:
        copy.wait()


def halves(*pieces):
    vmem = pl.BlockSpec(memory_space=pltpu.VMEM)
    shapes = [jax.ShapeDtypeStruct((p.shape[0] // 2, p.shape[1]), p.dtype) for p in pieces]
    return pl.pallas_call(
        halves_kernel,
        out_shape=shapes,
        in_specs=[vmem] * len(pieces),
        out_specs=[vmem] * len(pieces),
        scratch_shapes=[pltpu.SemaphoreType.DMA((len(pieces),))],
        compiler_params=pltpu.CompilerParams(vmem_limit_bytes=16 * 2**20),
    )(*pieces)


def forward_kernel(*refs):
    parts, tab_ref, hbm = refs[:5], refs[5], refs[6:9]
    wg, wu, wd, gate_b, up_b = refs[9:14]
    own, one_lo, one_hi, two_lo, two_hi, three_lo, three_hi, sems = refs[14:]
    width = wg.shape[0]
    step = width // CHUNKS
    rows = parts[0].shape[0]
    count, half = SIDE * rows, rows // 2

    def copies(c):
        part = pl.ds(c * step, step)
        return (
            pltpu.make_async_copy(hbm[0].at[part, :], wg.at[part, :], sems.at[0, c]),
            pltpu.make_async_copy(hbm[1].at[part, :], wu.at[part, :], sems.at[1, c]),
        )

    last = pltpu.make_async_copy(hbm[2], wd, sems.at[2, 0])
    for c in range(CHUNKS):
        for copy in copies(c):
            copy.start()
    last.start()
    gate = up = gate_back = up_back = 0.0
    for c in range(CHUNKS):
        for copy in copies(c):
            copy.wait()
        at = c * step
        w_g, w_u = wg[at : at + step, :], wu[at : at + step, :]
        x = columns(parts, at, step)
        gate, up = gate + dot(x, w_g), up + dot(x, w_u)
        if c * 2 < CHUNKS:
            x = columns(parts, width + at, step)
            gate_back, up_back = gate_back + dot(x, w_g), up_back + dot(x, w_u)
    gate_b[...] = blocks_swapped(gate_back)
    up_b[...] = blocks_swapped(up_back)

    hidden = (gate / (1.0 + jnp.exp(-gate)) * up).astype(BF16)
    weight = tab_ref[0][:, :1]
    last.wait()
    for c in range(CHUNKS):
        part = slice(c * step, (c + 1) * step)
        out = weight * dot(hidden, wd[:, part])
        own[:, part] = out[:rows]
        sent = out.astype(BF16)
        one_lo[:, part] = sent[rows : rows + half]
        one_hi[:, part] = out[rows + half : 2 * rows]
        two_lo[:, part] = sent[2 * rows : 2 * rows + half]
        two_hi[:, part] = sent[2 * rows + half : 3 * rows]
        three_lo[:, part] = out[3 * rows : 3 * rows + half]
        three_hi[:, part] = sent[3 * rows + half :]


def forward(parts, table, w_g, w_u, w_d):
    width, hidden = w_g.shape
    rows = parts[0].shape[0]
    half, count = rows // 2, SIDE * rows
    vmem = pl.BlockSpec(memory_space=pltpu.VMEM)
    out = jax.ShapeDtypeStruct
    return pl.pallas_call(
        forward_kernel,
        out_shape=(
            out(w_g.shape, BF16),
            out(w_u.shape, BF16),
            out(w_d.shape, BF16),
            out((count, hidden), F32),
            out((count, hidden), F32),
            out((rows, width), F32),
            out((half, width), BF16),
            out((half, width), F32),
            out((half, width), BF16),
            out((half, width), BF16),
            out((half, width), F32),
            out((half, width), BF16),
        ),
        in_specs=[vmem] * 6 + [pl.BlockSpec(memory_space=pl.ANY)] * 3,
        out_specs=(vmem,) * 12,
        scratch_shapes=[pltpu.SemaphoreType.DMA((3, CHUNKS))],
        compiler_params=pltpu.CompilerParams(vmem_limit_bytes=36 * 2**20),
        cost_estimate=pl.CostEstimate(
            flops=2 * count * width * hidden * 4, bytes_accessed=6 * width * hidden, transcendentals=0
        ),
    )(*parts, table, w_g, w_u, w_d)


def backward_kernel(*refs):
    parts, (gate_b, up_b, tab_ref, wg, wu, wd) = refs[:5], refs[5:11]
    own, one, two, three, p_own = refs[11:]
    width = wg.shape[0]
    half_width, step = width // 2, width // CHUNKS
    rows = parts[0].shape[0]
    gate, up, back = gate_b[...], up_b[...], 0.0
    for c in range(CHUNKS):
        at = c * step
        back = back + contract_last(columns(parts, at, step), wd[:, at : at + step])
        if c * 2 >= CHUNKS:
            x = columns(parts, at + half_width, step)
            gate = gate + dot(x, wg[at : at + step, :])
            up = up + dot(x, wu[at : at + step, :])

    sig = 1.0 / (1.0 + jnp.exp(-gate))
    silu = gate * sig
    hidden = (silu * up).astype(BF16)
    inner = jnp.sum(hidden.astype(F32) * back, axis=-1, keepdims=True)
    grad_hidden = tab_ref[1][:, :1] * back
    dsilu = sig * (1.0 + gate * (1.0 - sig))
    grad_gate = (grad_hidden * up * dsilu).astype(BF16)
    grad_up = (grad_hidden * silu).astype(BF16)

    prob = tab_ref[2] * inner
    p_own[...] = prob[:rows]
    top = prob.astype(BF16).astype(F32)
    lane = lax.broadcasted_iota(jnp.int32, prob.shape, 1)
    coded = jnp.where(lane < 4, top, jnp.where(lane < 8, prob - top, 0.0)).astype(BF16)
    for j, ref in enumerate((one, two, three), 1):
        ref[:, width:] = coded[j * rows : (j + 1) * rows]
    for c in range(CHUNKS):
        part = slice(c * step, (c + 1) * step)
        out = contract_last(grad_gate, wg[part, :]) + contract_last(grad_up, wu[part, :])
        own[:, part] = out[:rows]
        sent = out.astype(BF16)
        for j, ref in enumerate((one, two, three), 1):
            ref[:, part] = sent[j * rows : (j + 1) * rows]


def backward(parts, gate_b, up_b, table, w_g, w_u, w_d):
    width, hidden = w_g.shape
    rows = parts[0].shape[0]
    vmem = pl.BlockSpec(memory_space=pltpu.VMEM)
    out = jax.ShapeDtypeStruct
    sent = out((rows, width + LANES), BF16)
    return pl.pallas_call(
        backward_kernel,
        out_shape=(out((rows, width), F32), sent, sent, sent, out((rows, LANES), F32)),
        in_specs=[vmem] * 11,
        out_specs=(vmem,) * 5,
        compiler_params=pltpu.CompilerParams(vmem_limit_bytes=24 * 2**20),
    )(*parts, gate_b, up_b, table, w_g, w_u, w_d)


def own_weight(ids, probs, expert_id):
    return jnp.sum(jnp.where(ids == expert_id, probs.astype(F32), 0.0), axis=-1)


def reordered(table, order):
    hit = order[:, None] == jnp.arange(table.shape[0], dtype=jnp.int32)[None, :]
    return jnp.sum(jnp.where(hit[:, :, None], table[None, :, :], 0.0), axis=1)


def body(x_fwd, ids_fwd, probs_fwd, x_bwd, ids_bwd, probs_bwd, grad_out, w_gate, w_up, w_down):
    width = x_fwd.shape[1]
    half = width // 2
    me = lax.axis_index("expert")
    expert_id = me // (lax.axis_size("expert") // EXP_WIN)

    spot = jnp.arange(SIDE**3 * 2, dtype=jnp.int32)
    order_a = ((spot // 2) ^ me) * 2 + spot % 2
    order_b = to_other_order(order_a[:, None])[:, 0]
    weight_f = own_weight(ids_fwd, probs_fwd, expert_id)
    weight_b = own_weight(ids_bwd, probs_bwd, expert_id)
    mine_b = (ids_bwd == expert_id).astype(F32)
    tab_f = reordered(weight_f[:, None], order_a)
    tab_b = reordered(jnp.concatenate([weight_b[:, None], mine_b], axis=1), order_b)
    spread = lambda v: jnp.broadcast_to(v, (v.shape[0], LANES))
    table = jnp.stack(
        [spread(tab_f), spread(tab_b[:, :1]), jnp.tile(tab_b[:, 1:], (1, LANES // 4))]
    )

    first = jnp.concatenate([x_fwd, x_bwd[:, :half], grad_out, x_bwd[:, half:]], axis=1)
    lines = gathered(first, "z")
    a_part, b_part = lines[:, : width + half], lines[:, width + half :]
    a_parts = relayed(gathered(a_part, "x"), "y")
    b_parts = relayed(gathered(b_part, "y"), "x")

    (
        w_g, w_u, w_d, gate_b, up_b,
        f_own, f_one_lo, f_one_hi, f_two_lo, f_two_hi, f_three_lo, f_three_hi,
    ) = forward(a_parts, table, w_gate[0], w_up[0], w_down[0])
    b_own, b_one, b_two, b_three, p_own = backward(b_parts, gate_b, up_b, table, w_g, w_u, w_d)

    f_three_lo = (f_three_lo + swap(f_two_lo, "y", 1).astype(F32)).astype(BF16)
    f_one_hi = (f_one_hi + swap(f_two_hi, "y", 3).astype(F32)).astype(BF16)
    sum_f = (
        f_own
        + swap(jnp.concatenate([f_one_lo, f_one_hi], axis=0), "y", 1).astype(F32)
        + swap(jnp.concatenate([f_three_lo, f_three_hi], axis=0), "y", 3).astype(F32)
    )
    sum_b, sum_p = b_own, p_own[:, :4]
    for j, block in enumerate((b_one, b_two, b_three), 1):
        got = swap(block, "x", j).astype(F32)
        sum_b = sum_b + got[:, :width]
        sum_p = sum_p + got[:, width : width + 4] + got[:, width + 4 : width + 8]

    sum_f = scattered(*cut(sum_f, BF16), "x")
    top = lax.reduce_precision(sum_p, 8, 7)
    coded = jnp.pad(jnp.concatenate([top, sum_p - top], axis=1), ((0, 0), (0, LANES - 8)))
    both = scattered(*cut(jnp.concatenate([sum_b, coded], axis=1), BF16), "y")
    sum_b, coded = both[:, :width], both[:, width:]
    last = scattered(*cut(jnp.concatenate([sum_f, sum_b, coded], axis=1), F32), "z")

    layer_out = (x_fwd.astype(F32) + last[:, :width]).astype(BF16)
    input_grad = (grad_out.astype(F32) + last[:, width : 2 * width]).astype(BF16)
    fwd_next, bwd_next = handed_on(layer_out, input_grad)
    dprob = last[:, 2 * width : 2 * width + 4] + last[:, 2 * width + 4 : 2 * width + 8]
    return (fwd_next, bwd_next, dprob)


def solution(mesh):
    return jax.shard_map(
        body,
        mesh=mesh,
        in_specs=(
            P(("segment", "expert"), None),
            P("segment", None),
            P("segment", None),
            P(("segment", "expert"), None),
            P("segment", None),
            P("segment", None),
            P(("segment", "expert"), None),
            P("segment", None, "expert"),
            P("segment", None, "expert"),
            P("segment", "expert", None),
        ),
        out_specs=(
            P(("segment", "expert"), None),
            P(("segment", "expert"), None),
            P(("segment", "expert"), None),
        ),
        check_vma=False,
    )
```

time: 1890 us -> 130 us (0.07)
  waiting for transfers between devices: 1430 us -> 46.8 us
  blocking collectives: 318 us -> 0 us
  local copies, waits for them, and re-layouts: 46.2 us -> 2.72 us
  matrix products: 26.8 us -> 0 us
    all_gather x3 -> x0, waiting for transfers between devices: 982 us -> none  [the longest x1 342 us: body(): lax.all_gather(grad_out, 'expert', axis=0, tiled=True)]
    unnamed x5 -> x0, waiting for transfers between devices: 443 us -> none
    unnamed x1 -> x0, blocking collectives: 318 us -> none
    ppermute x2 -> x35, waiting for transfers between devices: 1.23 us -> 46.8 us  [the longest x33 45.2 us: swap(): lax.ppermute(value, 'expert', [(i, i ^ by * STRIDE[along]) for i in range...]
    dot_general x8 -> x0, matrix products: 26.8 us -> none  [the longest x3 8.61 us: contract_last(): lax.dot_general(left, right, (((1,), (1,)), ((), ())), preferred_element_...]
    gather x7 -> x0, local copies, waits for them, and re-layouts: 25.5 us -> none  [the longest x3 8.86 us: pick_rows(): taken = jnp.take(source_rows, token_ids, axis=0)]
    ppermute x2 -> x35, starting transfers between devices: 46.3 us -> 60.8 us  [the longest x33 48.4 us: swap(): lax.ppermute(value, 'expert', [(i, i ^ by * STRIDE[along]) for i in range...]
  transfers between devices with their start and end apart: 6 -> 35, of which waited for: 5 -> 16; matrix products, arithmetic and copies ran while one was open for 2% -> 3% of each run, Pallas kernels for 0% -> 9%
where the time goes in v1:
time: 130 us
  starting transfers between devices  60.8 us (47%)
  waiting for transfers between devices  46.8 us (36%)
  Pallas kernels  12.3 us (9%)
  other arithmetic  6.21 us (5%)
  local copies, waits for them, and re-layouts  2.72 us (2%)
    ppermute x33, starting transfers between devices, swap(): lax.ppermute(value, 'expert', [(i, i ^ by * STRIDE[along]) for i in range...  48.4 us
    ppermute x33, waiting for transfers between devices, swap(): lax.ppermute(value, 'expert', [(i, i ^ by * STRIDE[along]) for i in range...  45.2 us
    ppermute x1, starting transfers between devices, handed_on(): got_far = lax.ppermute(jnp.where(even, back, forth), 'segment', far)  12.4 us
    pallas_call x1, Pallas kernels, forward(): pl.pallas_call(forward_kernel, out_shape=(out(w_g.shape, BF16), out(w_u.s...  6.08 us
    pallas_call x1, Pallas kernels, backward(): pl.pallas_call(backward_kernel, out_shape=(out((rows, width), F32), sent,...  4.8 us
  transfers between devices with their start and end apart: 35, of which 16 were waited for; matrix products, arithmetic and copies ran while one was open for 3% of the time, Pallas kernels for 9%

profile of v1, /device:TPU:1, one launch (start us, length us, event | category | flops | bytes accessed | tf_op | source)
XLA Modules:
  0.0 129.9 jit_solution(13518733386070044645)
XLA Ops:
  2.3 2.6 %collective-permute-start = (bf16[2,21504]{1,0:T(2,128)(2,1)S(1)}, bf16[2,21504]{1,0:T(2,128)(2,1)S(1)}, u32[]{:S(2)}, u32[]{:S(2)}) collective-permute-start(bf16[2,21504]{1,0:T(2,128)(2,1)S(1)} %pad_maximum_fusion.8), channel_id=1, source_target_pairs={{0,1},{1,0},{2,3},{3,2},{4,5},{5,4},{6,7},{7,6},{8,9},{9,8},{10,11... | collective-permute-start | bytes 258056 | tf_op jit(solution)/shard_map/ppermute | solution.py:19
  4.9 3.0 %collective-permute-start.1 = (bf16[2,21504]{1,0:T(2,128)(2,1)S(1)}, bf16[2,21504]{1,0:T(2,128)(2,1)S(1)}, u32[]{:S(2)}, u32[]{:S(2)}) collective-permute-start(bf16[2,21504]{1,0:T(2,128)(2,1)S(1)} %pad_maximum_fusion.8), channel_id=1, source_target_pairs={{0,2},{1,3},{2,0},{3,1},{4,6},{5,7},{6,4},{7,5},{8,10},{9,11},{10,... | collective-permute-start | bytes 258056 | tf_op jit(solution)/shard_map/ppermute | solution.py:19
  8.1 2.3 %collective-permute-done.1 = bf16[2,21504]{1,0:T(2,128)(2,1)S(1)} collective-permute-done((bf16[2,21504]{1,0:T(2,128)(2,1)S(1)}, bf16[2,21504]{1,0:T(2,128)(2,1)S(1)}, u32[]{:S(2)}, u32[]{:S(2)}) %collective-permute-start.1) | collective-permute-done | bytes 86048 | tf_op jit(solution)/shard_map/ppermute | solution.py:19
  10.4 2.7 %collective-permute-done.2 = bf16[2,21504]{1,0:T(2,128)(2,1)S(1)} collective-permute-done((bf16[2,21504]{1,0:T(2,128)(2,1)S(1)}, bf16[2,21504]{1,0:T(2,128)(2,1)S(1)}, u32[]{:S(2)}, u32[]{:S(2)}) %collective-permute-start.2) | collective-permute-done | bytes 86048 | tf_op jit(solution)/shard_map/ppermute | solution.py:19
  15.6 2.5 %collective-permute-start.4 = (bf16[8,10752]{1,0:T(8,128)(2,1)S(1)}, bf16[8,10752]{1,0:T(8,128)(2,1)S(1)}, u32[]{:S(2)}, u32[]{:S(2)}) collective-permute-start(bf16[8,10752]{1,0:T(8,128)(2,1)S(1)} %get-tuple-element.60), channel_id=1, source_target_pairs={{0,8},{1,9},{2,10},{3,11},{4,12},{5,13},{6,14},{7,15},{8,0},{9,1},... | collective-permute-start | bytes 516104 | tf_op jit(solution)/shard_map/ppermute | solution.py:19
  19.7 2.6 %collective-permute-start.18 = (bf16[8,10752]{1,0:T(8,128)(2,1)S(1)}, bf16[8,10752]{1,0:T(8,128)(2,1)S(1)}, u32[]{:S(2)}, u32[]{:S(2)}) collective-permute-start(bf16[8,10752]{1,0:T(8,128)(2,1)S(1)} %get-tuple-element.61), channel_id=1, source_target_pairs={{0,32},{1,33},{2,34},{3,35},{4,36},{5,37},{6,38},{7,39},{8,40},{9,... | collective-permute-start | bytes 516104 | tf_op jit(solution)/shard_map/ppermute | solution.py:19
  26.0 1.9 %collective-permute-start.7 = (bf16[32,10752]{1,0:T(8,128)(2,1)S(1)}, bf16[32,10752]{1,0:T(8,128)(2,1)S(1)}, u32[]{:S(2)}, u32[]{:S(2)}) collective-permute-start(bf16[32,10752]{1,0:T(8,128)(2,1)S(1)} %pad_maximum_fusion.1.refs_0_), channel_id=1, source_target_pairs={{0,48},{1,49},{2,50},{3,51},{4,52},{5,53},{6,54},{7,55},{8,56},{9,... | collective-permute-start | bytes 2064392 | tf_op jit(solution)/shard_map/ppermute | solution.py:19
  28.9 2.6 %collective-permute-start.21 = (bf16[32,10752]{1,0:T(8,128)(2,1)S(1)}, bf16[32,10752]{1,0:T(8,128)(2,1)S(1)}, u32[]{:S(2)}, u32[]{:S(2)}) collective-permute-start(bf16[32,10752]{1,0:T(8,128)(2,1)S(1)} %pad_maximum_fusion.2.refs_0_), channel_id=1, source_target_pairs={{0,12},{1,13},{2,14},{3,15},{4,8},{5,9},{6,10},{7,11},{8,4},{9,5},... | collective-permute-start | bytes 2064392 | tf_op jit(solution)/shard_map/ppermute | solution.py:19
  31.7 9.2 %collective-permute-done.6.refs_1_ = bf16[32,10752]{1,0:T(8,128)(2,1)S(1)} collective-permute-done((bf16[32,10752]{1,0:T(8,128)(2,1)S(1)}, bf16[32,10752]{1,0:T(8,128)(2,1)S(1)}, u32[]{:S(2)}, u32[]{:S(2)}) %collective-permute-start.6) | collective-permute-done | bytes 688160 | tf_op jit(solution)/shard_map/ppermute | solution.py:19
  40.9 4.7 %collective-permute-done.7.refs_0_.refs_4_ = bf16[32,10752]{1,0:T(8,128)(2,1)S(1)} collective-permute-done((bf16[32,10752]{1,0:T(8,128)(2,1)S(1)}, bf16[32,10752]{1,0:T(8,128)(2,1)S(1)}, u32[]{:S(2)}, u32[]{:S(2)}) %collective-permute-start.7) | collective-permute-done | bytes 688160 | tf_op jit(solution)/shard_map/ppermute | solution.py:19
  50.3 1.9 %collective-permute-start.22 = (bf16[16,10752]{1,0:T(8,128)(2,1)S(1)}, bf16[16,10752]{1,0:T(8,128)(2,1)S(1)}, u32[]{:S(2)}, u32[]{:S(2)}) collective-permute-start(bf16[16,10752]{1,0:T(8,128)(2,1)S(1)} %get-tuple-element.33), channel_id=1, source_target_pairs={{0,4},{1,5},{2,6},{3,7},{4,0},{5,1},{6,2},{7,3},{8,12},{9,13},{10,... | collective-permute-start | bytes 1032200 | tf_op jit(solution)/shard_map/ppermute | solution.py:19
  56.5 6.1 %shard_map.122 = (bf16[7168,256]{1,0:T(8,128)(2,1)S(1)}, bf16[7168,256]{1,0:T(8,128)(2,1)S(1)}, bf16[256,7168]{1,0:T(8,128)(2,1)S(1)}, f32[128,256]{1,0:T(8,128)...) custom-call(bf16[32,10752]{1,0:T(8,128)(2,1)S(1)} %pad_maximum_fusio, ...), custom_call_target="tpu_custom_call" | custom-call | flops 1879048192 | bytes 11010048 | tf_op jit(solution)/shard_map/pallas_call | solution.py:176
  62.8 4.8 %shard_map.124 = (f32[32,7168]{1,0:T(8,128)S(1)}, bf16[32,7296]{1,0:T(8,128)(2,1)S(1)}, bf16[32,7296]{1,0:T(8,128)(2,1)S(1)}, bf16[32,7296]{1,0:T(8,128)(2,1)S(1)}, f32[32,128]{1,0:T(8,128)S(1)}) custom-call(bf16[32,10752]{1,0:T(8,128)(2,1)S(1)} %pad_maximum_fusion.2.refs_0_, bf16[32,10752]{1,0:T(8,128)(2,1)S(1)} %collective-permute-done.20.refs_1_, ...), custom_call_target="tpu_custom_call" | custom-call | tf_op jit(solution)/shard_map/pallas_call | solution.py:248
  67.6 2.0 %collective-permute-start.24 = (bf16[32,7296]{1,0:T(8,128)(2,1)S(1)}, bf16[32,7296]{1,0:T(8,128)(2,1)S(1)}, u32[]{:S(2)}, u32[]{:S(2)}) collective-permute-start(bf16[32,7296]{1,0:T(8,128)(2,1)S(1)} %get-tuple-element.41), channel_id=1, source_target_pairs={{0,4},{1,5},{2,6},{3,7},{4,0},{5,1},{6,2},{7,3},{8,12},{9,13},{10,... | collective-permute-start | bytes 1400840 | tf_op jit(solution)/shard_map/ppermute | solution.py:19
  69.9 2.2 %collective-permute-start.26 = (bf16[32,7296]{1,0:T(8,128)(2,1)S(1)}, bf16[32,7296]{1,0:T(8,128)(2,1)S(1)}, u32[]{:S(2)}, u32[]{:S(2)}) collective-permute-start(bf16[32,7296]{1,0:T(8,128)(2,1)S(1)} %get-tuple-element.43), channel_id=1, source_target_pairs={{0,12},{1,13},{2,14},{3,15},{4,8},{5,9},{6,10},{7,11},{8,4},{9,5},... | collective-permute-start | bytes 1400840 | tf_op jit(solution)/shard_map/ppermute | solution.py:19
  73.8 2.1 %collective-permute-start.13 = (bf16[32,7168]{1,0:T(8,128)(2,1)S(1)}, bf16[32,7168]{1,0:T(8,128)(2,1)S(1)}, u32[]{:S(2)}, u32[]{:S(2)}) collective-permute-start(bf16[32,7168]{1,0:T(8,128)(2,1)S(1)} %pad_maximum_fusion.4), channel_id=1, source_target_pairs={{0,48},{1,49},{2,50},{3,51},{4,52},{5,53},{6,54},{7,55},{8,56},{9,... | collective-permute-start | bytes 1376264 | tf_op jit(solution)/shard_map/ppermute | solution.py:19
  77.0 9.1 %collective-permute-done.25 = bf16[32,7296]{1,0:T(8,128)(2,1)S(1)} collective-permute-done((bf16[32,7296]{1,0:T(8,128)(2,1)S(1)}, bf16[32,7296]{1,0:T(8,128)(2,1)S(1)}, u32[]{:S(2)}, u32[]{:S(2)}) %collective-permute-start.25) | collective-permute-done | bytes 466976 | tf_op jit(solution)/shard_map/ppermute | solution.py:19
  88.5 2.1 %collective-permute-start.29 = (bf16[8,7296]{1,0:T(8,128)(2,1)S(1)}, bf16[8,7296]{1,0:T(8,128)(2,1)S(1)}, u32[]{:S(2)}, u32[]{:S(2)}) collective-permute-start(bf16[8,7296]{1,0:T(8,128)(2,1)S(1)} %get-tuple-element.52), channel_id=1, source_target_pairs={{0,48},{1,49},{2,50},{3,51},{4,52},{5,53},{6,54},{7,55},{8,56},{9,... | collective-permute-start | bytes 350216 | tf_op jit(solution)/shard_map/ppermute | solution.py:19
  92.5 3.1 %collective-permute-start.15 = (bf16[8,7168]{1,0:T(8,128)(2,1)S(1)}, bf16[8,7168]{1,0:T(8,128)(2,1)S(1)}, u32[]{:S(2)}, u32[]{:S(2)}) collective-permute-start(bf16[8,7168]{1,0:T(8,128)(2,1)S(1)} %get-tuple-element.59), channel_id=1, source_target_pairs={{0,8},{1,9},{2,10},{3,11},{4,12},{5,13},{6,14},{7,15},{8,0},{9,1},... | collective-permute-start | bytes 344072 | tf_op jit(solution)/shard_map/ppermute | solution.py:19
  95.8 3.3 %collective-permute-done.15 = bf16[8,7168]{1,0:T(8,128)(2,1)S(1)} collective-permute-done((bf16[8,7168]{1,0:T(8,128)(2,1)S(1)}, bf16[8,7168]{1,0:T(8,128)(2,1)S(1)}, u32[]{:S(2)}, u32[]{:S(2)}) %collective-permute-start.15) | collective-permute-done | bytes 114720 | tf_op jit(solution)/shard_map/ppermute | solution.py:19
  100.7 5.8 %collective-permute-start.30 = (f32[2,14464]{1,0:T(2,128)S(1)}, f32[2,14464]{1,0:T(2,128)S(1)}, u32[]{:S(2)}, u32[]{:S(2)}) collective-permute-start(f32[2,14464]{1,0:T(2,128)S(1)} %get-tuple-element.54), channel_id=1, source_target_pairs={{0,1},{1,0},{2,3},{3,2},{4,5},{5,4},{6,7},{7,6},{8,9},{9,8},{10,11... | collective-permute-start | bytes 347144 | tf_op jit(solution)/shard_map/ppermute | solution.py:19
  106.6 1.9 %collective-permute-start.31 = (f32[2,14464]{1,0:T(2,128)S(1)}, f32[2,14464]{1,0:T(2,128)S(1)}, u32[]{:S(2)}, u32[]{:S(2)}) collective-permute-start(f32[2,14464]{1,0:T(2,128)S(1)} %get-tuple-element.56), channel_id=1, source_target_pairs={{0,2},{1,3},{2,0},{3,1},{4,6},{5,7},{6,4},{7,5},{8,10},{9,11},{10,... | collective-permute-start | bytes 347144 | tf_op jit(solution)/shard_map/ppermute | solution.py:19
  111.1 3.2 %collective-permute-done.32 = f32[2,14464]{1,0:T(2,128)S(1)} collective-permute-done((f32[2,14464]{1,0:T(2,128)S(1)}, f32[2,14464]{1,0:T(2,128)S(1)}, u32[]{:S(2)}, u32[]{:S(2)}) %collective-permute-start.32) | collective-permute-done | bytes 115744 | tf_op jit(solution)/shard_map/ppermute | solution.py:19
  114.5 12.4 %collective-permute-start.33 = (bf16[2,7168]{1,0:T(2,128)(2,1)S(1)}, bf16[2,7168]{1,0:T(2,128)(2,1)S(1)}, u32[]{:S(2)}, u32[]{:S(2)}) collective-permute-start(bf16[2,7168]{1,0:T(2,128)(2,1)S(1)} %get-tuple-element.63), channel_id=1, source_target_pairs={{0,192},{64,128},{128,64},{192,0},{1,193},{65,129},{129,65},{193,1... | collective-permute-start | bytes 86024 | tf_op jit(solution)/shard_map/ppermute | solution.py:34
  (110 shorter events, 34.8 us)
Async XLA Ops:
  14.3 8.0 %collective-permute-start.3 = (bf16[8,10752]{1,0:T(8,128)(2,1)S(1)}, bf16[8,10752]{1,0:T(8,128)(2,1)S(1)}, u32[]{:S(2)}, u32[]{:S(2)}) collective-permute-start(bf16[8,10752]{1,0:T(8,128)(2,1)S(1)} %get-tuple-element.60), channel_id=1, source_target_pairs={{0,4},{1,5},{2,6},{3,7},{4,0},{5,1},{6,2},{7,3},{8,12},{9,13},{10,... | collective-permute-start | bytes 516104 | tf_op jit(solution)/shard_map/ppermute | solution.py:19
  15.6 7.5 %collective-permute-start.4 = (bf16[8,10752]{1,0:T(8,128)(2,1)S(1)}, bf16[8,10752]{1,0:T(8,128)(2,1)S(1)}, u32[]{:S(2)}, u32[]{:S(2)}) collective-permute-start(bf16[8,10752]{1,0:T(8,128)(2,1)S(1)} %get-tuple-element.60), channel_id=1, source_target_pairs={{0,8},{1,9},{2,10},{3,11},{4,12},{5,13},{6,14},{7,15},{8,0},{9,1},... | collective-permute-start | bytes 516104 | tf_op jit(solution)/shard_map/ppermute | solution.py:19
  18.3 9.6 %collective-permute-start.17 = (bf16[8,10752]{1,0:T(8,128)(2,1)S(1)}, bf16[8,10752]{1,0:T(8,128)(2,1)S(1)}, u32[]{:S(2)}, u32[]{:S(2)}) collective-permute-start(bf16[8,10752]{1,0:T(8,128)(2,1)S(1)} %get-tuple-element.61), channel_id=1, source_target_pairs={{0,16},{1,17},{2,18},{3,19},{4,20},{5,21},{6,22},{7,23},{8,24},{9,... | collective-permute-start | bytes 516104 | tf_op jit(solution)/shard_map/ppermute | solution.py:19
  19.7 8.2 %collective-permute-start.18 = (bf16[8,10752]{1,0:T(8,128)(2,1)S(1)}, bf16[8,10752]{1,0:T(8,128)(2,1)S(1)}, u32[]{:S(2)}, u32[]{:S(2)}) collective-permute-start(bf16[8,10752]{1,0:T(8,128)(2,1)S(1)} %get-tuple-element.61), channel_id=1, source_target_pairs={{0,32},{1,33},{2,34},{3,35},{4,36},{5,37},{6,38},{7,39},{8,40},{9,... | collective-permute-start | bytes 516104 | tf_op jit(solution)/shard_map/ppermute | solution.py:19
  24.6 16.3 %collective-permute-start.6 = (bf16[32,10752]{1,0:T(8,128)(2,1)S(1)}, bf16[32,10752]{1,0:T(8,128)(2,1)S(1)}, u32[]{:S(2)}, u32[]{:S(2)}) collective-permute-start(bf16[32,10752]{1,0:T(8,128)(2,1)S(1)} %pad_maximum_fusion.1.refs_0_), channel_id=1, source_target_pairs={{0,16},{1,17},{2,18},{3,19},{4,20},{5,21},{6,22},{7,23},{8,24},{9,... | collective-permute-start | bytes 2064392 | tf_op jit(solution)/shard_map/ppermute | solution.py:19
  26.0 19.6 %collective-permute-start.7 = (bf16[32,10752]{1,0:T(8,128)(2,1)S(1)}, bf16[32,10752]{1,0:T(8,128)(2,1)S(1)}, u32[]{:S(2)}, u32[]{:S(2)}) collective-permute-start(bf16[32,10752]{1,0:T(8,128)(2,1)S(1)} %pad_maximum_fusion.1.refs_0_), channel_id=1, source_target_pairs={{0,48},{1,49},{2,50},{3,51},{4,52},{5,53},{6,54},{7,55},{8,56},{9,... | collective-permute-start | bytes 2064392 | tf_op jit(solution)/shard_map/ppermute | solution.py:19
  28.8 21.2 %collective-permute-start.20 = (bf16[32,10752]{1,0:T(8,128)(2,1)S(1)}, bf16[32,10752]{1,0:T(8,128)(2,1)S(1)}, u32[]{:S(2)}, u32[]{:S(2)}) collective-permute-start(bf16[32,10752]{1,0:T(8,128)(2,1)S(1)} %pad_maximum_fusion.2.refs_0_), channel_id=1, source_target_pairs={{0,4},{1,5},{2,6},{3,7},{4,0},{5,1},{6,2},{7,3},{8,12},{9,13},{10,... | collective-permute-start | bytes 2064392 | tf_op jit(solution)/shard_map/ppermute | solution.py:19
  28.9 21.1 %collective-permute-start.21 = (bf16[32,10752]{1,0:T(8,128)(2,1)S(1)}, bf16[32,10752]{1,0:T(8,128)(2,1)S(1)}, u32[]{:S(2)}, u32[]{:S(2)}) collective-permute-start(bf16[32,10752]{1,0:T(8,128)(2,1)S(1)} %pad_maximum_fusion.2.refs_0_), channel_id=1, source_target_pairs={{0,12},{1,13},{2,14},{3,15},{4,8},{5,9},{6,10},{7,11},{8,4},{9,5},... | collective-permute-start | bytes 2064392 | tf_op jit(solution)/shard_map/ppermute | solution.py:19
  47.6 7.2 %collective-permute-start.8 = (bf16[16,10752]{1,0:T(8,128)(2,1)}, bf16[16,10752]{1,0:T(8,128)(2,1)}, u32[]{:S(2)}, u32[]{:S(2)}) collective-permute-start(bf16[16,10752]{1,0:T(8,128)(2,1)} %get-tuple-element.24), channel_id=1, source_target_pairs={{0,16},{1,17},{2,18},{3,19},{4,20},{5,21},{6,22},{7,23},{8,24},{9,... | collective-permute-start | bytes 1032200 | tf_op jit(solution)/shard_map/ppermute | solution.py:19
  47.9 8.6 %collective-permute-start.9 = (bf16[16,10752]{1,0:T(8,128)(2,1)}, bf16[16,10752]{1,0:T(8,128)(2,1)}, u32[]{:S(2)}, u32[]{:S(2)}) collective-permute-start(bf16[16,10752]{1,0:T(8,128)(2,1)} %get-tuple-element.25), channel_id=1, source_target_pairs={{0,48},{1,49},{2,50},{3,51},{4,52},{5,53},{6,54},{7,55},{8,56},{9,... | collective-permute-start | bytes 1032200 | tf_op jit(solution)/shard_map/ppermute | solution.py:19
  50.3 12.4 %collective-permute-start.22 = (bf16[16,10752]{1,0:T(8,128)(2,1)S(1)}, bf16[16,10752]{1,0:T(8,128)(2,1)S(1)}, u32[]{:S(2)}, u32[]{:S(2)}) collective-permute-start(bf16[16,10752]{1,0:T(8,128)(2,1)S(1)} %get-tuple-element.33), channel_id=1, source_target_pairs={{0,4},{1,5},{2,6},{3,7},{4,0},{5,1},{6,2},{7,3},{8,12},{9,13},{10,... | collective-permute-start | bytes 1032200 | tf_op jit(solution)/shard_map/ppermute | solution.py:19
  52.3 10.5 %collective-permute-start.23 = (bf16[16,10752]{1,0:T(8,128)(2,1)S(1)}, bf16[16,10752]{1,0:T(8,128)(2,1)S(1)}, u32[]{:S(2)}, u32[]{:S(2)}) collective-permute-start(bf16[16,10752]{1,0:T(8,128)(2,1)S(1)} %get-tuple-element.34), channel_id=1, source_target_pairs={{0,12},{1,13},{2,14},{3,15},{4,8},{5,9},{6,10},{7,11},{8,4},{9,5},... | collective-permute-start | bytes 1032200 | tf_op jit(solution)/shard_map/ppermute | solution.py:19
  62.6 9.6 %collective-permute-start.10 = (bf16[16,7168]{1,0:T(8,128)(2,1)S(1)}, bf16[16,7168]{1,0:T(8,128)(2,1)S(1)}, u32[]{:S(2)}, u32[]{:S(2)}) collective-permute-start(bf16[16,7168]{1,0:T(8,128)(2,1)S(1)} %get-tuple-element.29), channel_id=1, source_target_pairs={{0,48},{1,49},{2,50},{3,51},{4,52},{5,53},{6,54},{7,55},{8,56},{9,... | collective-permute-start | bytes 688136 | tf_op jit(solution)/shard_map/ppermute | solution.py:19
  62.7 11.1 %collective-permute-start.12 = (bf16[16,7168]{1,0:T(8,128)(2,1)S(1)}, bf16[16,7168]{1,0:T(8,128)(2,1)S(1)}, u32[]{:S(2)}, u32[]{:S(2)}) collective-permute-start(bf16[16,7168]{1,0:T(8,128)(2,1)S(1)} %get-tuple-element.31), channel_id=1, source_target_pairs={{0,16},{1,17},{2,18},{3,19},{4,20},{5,21},{6,22},{7,23},{8,24},{9,... | collective-permute-start | bytes 688136 | tf_op jit(solution)/shard_map/ppermute | solution.py:19
  67.6 9.3 %collective-permute-start.24 = (bf16[32,7296]{1,0:T(8,128)(2,1)S(1)}, bf16[32,7296]{1,0:T(8,128)(2,1)S(1)}, u32[]{:S(2)}, u32[]{:S(2)}) collective-permute-start(bf16[32,7296]{1,0:T(8,128)(2,1)S(1)} %get-tuple-element.41), channel_id=1, source_target_pairs={{0,4},{1,5},{2,6},{3,7},{4,0},{5,1},{6,2},{7,3},{8,12},{9,13},{10,... | collective-permute-start | bytes 1400840 | tf_op jit(solution)/shard_map/ppermute | solution.py:19
  69.6 16.4 %collective-permute-start.25 = (bf16[32,7296]{1,0:T(8,128)(2,1)S(1)}, bf16[32,7296]{1,0:T(8,128)(2,1)S(1)}, u32[]{:S(2)}, u32[]{:S(2)}) collective-permute-start(bf16[32,7296]{1,0:T(8,128)(2,1)S(1)} %get-tuple-element.42), channel_id=1, source_target_pairs={{0,8},{1,9},{2,10},{3,11},{4,12},{5,13},{6,14},{7,15},{8,0},{9,1},... | collective-permute-start | bytes 1400840 | tf_op jit(solution)/shard_map/ppermute | solution.py:19
  69.9 16.2 %collective-permute-start.26 = (bf16[32,7296]{1,0:T(8,128)(2,1)S(1)}, bf16[32,7296]{1,0:T(8,128)(2,1)S(1)}, u32[]{:S(2)}, u32[]{:S(2)}) collective-permute-start(bf16[32,7296]{1,0:T(8,128)(2,1)S(1)} %get-tuple-element.43), channel_id=1, source_target_pairs={{0,12},{1,13},{2,14},{3,15},{4,8},{5,9},{6,10},{7,11},{8,4},{9,5},... | collective-permute-start | bytes 1400840 | tf_op jit(solution)/shard_map/ppermute | solution.py:19
  72.2 18.4 %collective-permute-start.11 = (bf16[32,7168]{1,0:T(8,128)(2,1)S(1)}, bf16[32,7168]{1,0:T(8,128)(2,1)S(1)}, u32[]{:S(2)}, u32[]{:S(2)}) collective-permute-start(bf16[32,7168]{1,0:T(8,128)(2,1)S(1)} %pad_maximum_fusion.3), channel_id=1, source_target_pairs={{0,16},{1,17},{2,18},{3,19},{4,20},{5,21},{6,22},{7,23},{8,24},{9,... | collective-permute-start | bytes 1376264 | tf_op jit(solution)/shard_map/ppermute | solution.py:19
  73.8 16.8 %collective-permute-start.13 = (bf16[32,7168]{1,0:T(8,128)(2,1)S(1)}, bf16[32,7168]{1,0:T(8,128)(2,1)S(1)}, u32[]{:S(2)}, u32[]{:S(2)}) collective-permute-start(bf16[32,7168]{1,0:T(8,128)(2,1)S(1)} %pad_maximum_fusion.4), channel_id=1, source_target_pairs={{0,48},{1,49},{2,50},{3,51},{4,52},{5,53},{6,54},{7,55},{8,56},{9,... | collective-permute-start | bytes 1376264 | tf_op jit(solution)/shard_map/ppermute | solution.py:19
  86.7 9.0 %collective-permute-start.27 = (bf16[8,7296]{1,0:T(8,128)(2,1)S(1)}, bf16[8,7296]{1,0:T(8,128)(2,1)S(1)}, u32[]{:S(2)}, u32[]{:S(2)}) collective-permute-start(bf16[8,7296]{1,0:T(8,128)(2,1)S(1)} %get-tuple-element.51), channel_id=1, source_target_pairs={{0,16},{1,17},{2,18},{3,19},{4,20},{5,21},{6,22},{7,23},{8,24},{9,... | collective-permute-start | bytes 350216 | tf_op jit(solution)/shard_map/ppermute | solution.py:19
  88.0 7.7 %collective-permute-start.28 = (bf16[8,7296]{1,0:T(8,128)(2,1)S(1)}, bf16[8,7296]{1,0:T(8,128)(2,1)S(1)}, u32[]{:S(2)}, u32[]{:S(2)}) collective-permute-start(bf16[8,7296]{1,0:T(8,128)(2,1)S(1)} %get-tuple-element.53), channel_id=1, source_target_pairs={{0,32},{1,33},{2,34},{3,35},{4,36},{5,37},{6,38},{7,39},{8,40},{9,... | collective-permute-start | bytes 350216 | tf_op jit(solution)/shard_map/ppermute | solution.py:19
  88.5 7.2 %collective-permute-start.29 = (bf16[8,7296]{1,0:T(8,128)(2,1)S(1)}, bf16[8,7296]{1,0:T(8,128)(2,1)S(1)}, u32[]{:S(2)}, u32[]{:S(2)}) collective-permute-start(bf16[8,7296]{1,0:T(8,128)(2,1)S(1)} %get-tuple-element.52), channel_id=1, source_target_pairs={{0,48},{1,49},{2,50},{3,51},{4,52},{5,53},{6,54},{7,55},{8,56},{9,... | collective-permute-start | bytes 350216 | tf_op jit(solution)/shard_map/ppermute | solution.py:19
  100.7 8.8 %collective-permute-start.30 = (f32[2,14464]{1,0:T(2,128)S(1)}, f32[2,14464]{1,0:T(2,128)S(1)}, u32[]{:S(2)}, u32[]{:S(2)}) collective-permute-start(f32[2,14464]{1,0:T(2,128)S(1)} %get-tuple-element.54), channel_id=1, source_target_pairs={{0,1},{1,0},{2,3},{3,2},{4,5},{5,4},{6,7},{7,6},{8,9},{9,8},{10,11... | collective-permute-start | bytes 347144 | tf_op jit(solution)/shard_map/ppermute | solution.py:19
  114.5 14.7 %collective-permute-start.33 = (bf16[2,7168]{1,0:T(2,128)(2,1)S(1)}, bf16[2,7168]{1,0:T(2,128)(2,1)S(1)}, u32[]{:S(2)}, u32[]{:S(2)}) collective-permute-start(bf16[2,7168]{1,0:T(2,128)(2,1)S(1)} %get-tuple-element.63), channel_id=1, source_target_pairs={{0,192},{64,128},{128,64},{192,0},{1,193},{65,129},{129,65},{193,1... | collective-permute-start | bytes 86024 | tf_op jit(solution)/shard_map/ppermute | solution.py:34
  (19 other events, 174.7 us)

commit v2 on v1

--- a/solution.py
+++ b/solution.py
@@ -8,7 +8,10 @@
 EXP_WIN = 8
 SIDE = 4
 LANES = 128
-CHUNKS = 4
+CHUNKS = 2
+LOAD_CHUNKS = 4
+LOADS = [(kind, c) for c in range(LOAD_CHUNKS) for kind in (0, 1)]
+LOADS = LOADS + [(2, c) for c in range(LOAD_CHUNKS)]
 STRIDE = {"z": 1, "x": 4, "y": 16}
 F32 = jnp.float32
 BF16 = jnp.bfloat16
@@ -36,13 +39,26 @@
     return jnp.where(even, got_far, got_near), jnp.where(even, got_near, got_far)
 
 
+def coded(value):
+    top = lax.reduce_precision(value, 8, 7)
+    return jnp.pad(jnp.concatenate([top, value - top], axis=1), ((0, 0), (0, LANES - 8)))
+
+
+def decoded(columns_of):
+    return columns_of[:, :4] + columns_of[:, 4:8]
+
+
+def after(value, *earlier):
+    return lax.optimization_barrier((value,) + earlier)[0]
+
+
 def gathered(value, along):
     return jnp.concatenate([value] + [swap(value, along, j) for j in range(1, SIDE)], axis=0)
 
 
-def relayed(value, along):
+def relayed(value, along, earlier):
     one, three = swap(value, along, 1), swap(value, along, 3)
-    low, high = halves(three, one)
+    low, high = halves(three, one, earlier)
     return [value, one, swap(low, along, 1), swap(high, along, 3), three]
 
 
@@ -89,31 +105,31 @@
     return jnp.concatenate([ref[:, first : first + step] for ref in pieces], axis=0)
 
 
-def halves_kernel(*refs):
-    count = (len(refs) - 1) // 2
-    sems = refs[-1]
-    copies = []
-    for i, (ref, out) in enumerate(zip(refs[:count], refs[count:-1])):
-        half = out.shape[0]
-        first = 0 if i % 2 == 0 else half
-        copies.append(pltpu.make_async_copy(ref.at[pl.ds(first, half), :], out, sems.at[i]))
+def halves_kernel(three, one, _, __, low, high, sems):
+    half = low.shape[0]
+    copies = (
+        pltpu.make_async_copy(three.at[pl.ds(0, half), :], low, sems.at[0]),
+        pltpu.make_async_copy(one.at[pl.ds(half, half), :], high, sems.at[1]),
+    )
     for copy in copies:
         copy.start()
     for copy in copies:
         copy.wait()
 
 
-def halves(*pieces):
-    vmem = pl.BlockSpec(memory_space=pltpu.VMEM)
-    shapes = [jax.ShapeDtypeStruct((p.shape[0] // 2, p.shape[1]), p.dtype) for p in pieces]
+def halves(three, one, earlier):
+    vmem, there = pl.BlockSpec(memory_space=pltpu.VMEM), pl.BlockSpec(memory_space=pl.ANY)
+    rows, width = one.shape
+    out = jax.ShapeDtypeStruct((rows // 2, width), one.dtype)
     return pl.pallas_call(
         halves_kernel,
-        out_shape=shapes,
-        in_specs=[vmem] * len(pieces),
-        out_specs=[vmem] * len(pieces),
-        scratch_shapes=[pltpu.SemaphoreType.DMA((len(pieces),))],
+        out_shape=(out, out),
+        in_specs=[vmem, vmem, there, there],
+        out_specs=(vmem, vmem),
+        cost_estimate=pl.CostEstimate(flops=1, bytes_accessed=10**6, transcendentals=0),
+        scratch_shapes=[pltpu.SemaphoreType.DMA((2,))],
         compiler_params=pltpu.CompilerParams(vmem_limit_bytes=16 * 2**20),
-    )(*pieces)
+    )(three, one, *earlier)
 
 
 def forward_kernel(*refs):
@@ -121,40 +137,36 @@
     wg, wu, wd, gate_b, up_b = refs[9:14]
     own, one_lo, one_hi, two_lo, two_hi, three_lo, three_hi, sems = refs[14:]
     width = wg.shape[0]
-    step = width // CHUNKS
+    step = width // LOAD_CHUNKS
     rows = parts[0].shape[0]
     count, half = SIDE * rows, rows // 2
 
-    def copies(c):
+    def load(kind, c):
         part = pl.ds(c * step, step)
-        return (
-            pltpu.make_async_copy(hbm[0].at[part, :], wg.at[part, :], sems.at[0, c]),
-            pltpu.make_async_copy(hbm[1].at[part, :], wu.at[part, :], sems.at[1, c]),
-        )
-
-    last = pltpu.make_async_copy(hbm[2], wd, sems.at[2, 0])
-    for c in range(CHUNKS):
-        for copy in copies(c):
-            copy.start()
-    last.start()
+        at = (slice(None), part) if kind == 2 else (part, slice(None))
+        held = (wg, wu, wd)[kind]
+        return pltpu.make_async_copy(hbm[kind].at[at], held.at[at], sems.at[kind, c])
+
+    for kind, c in LOADS:
+        load(kind, c).start()
     gate = up = gate_back = up_back = 0.0
-    for c in range(CHUNKS):
-        for copy in copies(c):
-            copy.wait()
+    for c in range(LOAD_CHUNKS):
         at = c * step
+        load(0, c).wait()
+        load(1, c).wait()
         w_g, w_u = wg[at : at + step, :], wu[at : at + step, :]
         x = columns(parts, at, step)
         gate, up = gate + dot(x, w_g), up + dot(x, w_u)
-        if c * 2 < CHUNKS:
+        if c * 2 < LOAD_CHUNKS:
             x = columns(parts, width + at, step)
             gate_back, up_back = gate_back + dot(x, w_g), up_back + dot(x, w_u)
     gate_b[...] = blocks_swapped(gate_back)
     up_b[...] = blocks_swapped(up_back)
 
     hidden = (gate / (1.0 + jnp.exp(-gate)) * up).astype(BF16)
-    weight = tab_ref[0][:, :1]
-    last.wait()
-    for c in range(CHUNKS):
+    weight = tab_ref[...]
+    for c in range(LOAD_CHUNKS):
+        load(2, c).wait()
         part = slice(c * step, (c + 1) * step)
         out = weight * dot(hidden, wd[:, part])
         own[:, part] = out[:rows]
@@ -191,11 +203,9 @@
         ),
         in_specs=[vmem] * 6 + [pl.BlockSpec(memory_space=pl.ANY)] * 3,
         out_specs=(vmem,) * 12,
-        scratch_shapes=[pltpu.SemaphoreType.DMA((3, CHUNKS))],
+        scratch_shapes=[pltpu.SemaphoreType.DMA((3, LOAD_CHUNKS))],
         compiler_params=pltpu.CompilerParams(vmem_limit_bytes=36 * 2**20),
-        cost_estimate=pl.CostEstimate(
-            flops=2 * count * width * hidden * 4, bytes_accessed=6 * width * hidden, transcendentals=0
-        ),
+        cost_estimate=pl.CostEstimate(flops=10**10, bytes_accessed=10**7, transcendentals=0),
     )(*parts, table, w_g, w_u, w_d)
 
 
@@ -218,18 +228,19 @@
     silu = gate * sig
     hidden = (silu * up).astype(BF16)
     inner = jnp.sum(hidden.astype(F32) * back, axis=-1, keepdims=True)
-    grad_hidden = tab_ref[1][:, :1] * back
+    grad_hidden = tab_ref[:, 8:9] * back
     dsilu = sig * (1.0 + gate * (1.0 - sig))
     grad_gate = (grad_hidden * up * dsilu).astype(BF16)
     grad_up = (grad_hidden * silu).astype(BF16)
 
-    prob = tab_ref[2] * inner
+    prob = tab_ref[:, :8] * inner
     p_own[...] = prob[:rows]
     top = prob.astype(BF16).astype(F32)
     lane = lax.broadcasted_iota(jnp.int32, prob.shape, 1)
-    coded = jnp.where(lane < 4, top, jnp.where(lane < 8, prob - top, 0.0)).astype(BF16)
+    parts_of = jnp.where(lane < 4, top, prob - top).astype(BF16)
     for j, ref in enumerate((one, two, three), 1):
-        ref[:, width:] = coded[j * rows : (j + 1) * rows]
+        ref[:, width:] = jnp.zeros((rows, LANES), BF16)
+        ref[:, width : width + 8] = parts_of[j * rows : (j + 1) * rows]
     for c in range(CHUNKS):
         part = slice(c * step, (c + 1) * step)
         out = contract_last(grad_gate, wg[part, :]) + contract_last(grad_up, wu[part, :])
@@ -247,9 +258,10 @@
     sent = out((rows, width + LANES), BF16)
     return pl.pallas_call(
         backward_kernel,
-        out_shape=(out((rows, width), F32), sent, sent, sent, out((rows, LANES), F32)),
+        out_shape=(out((rows, width), F32), sent, sent, sent, out((rows, 8), F32)),
         in_specs=[vmem] * 11,
         out_specs=(vmem,) * 5,
+        cost_estimate=pl.CostEstimate(flops=10**10, bytes_accessed=10**7, transcendentals=0),
         compiler_params=pltpu.CompilerParams(vmem_limit_bytes=24 * 2**20),
     )(*parts, gate_b, up_b, table, w_g, w_u, w_d)
 
@@ -276,23 +288,22 @@
     weight_b = own_weight(ids_bwd, probs_bwd, expert_id)
     mine_b = (ids_bwd == expert_id).astype(F32)
     tab_f = reordered(weight_f[:, None], order_a)
-    tab_b = reordered(jnp.concatenate([weight_b[:, None], mine_b], axis=1), order_b)
-    spread = lambda v: jnp.broadcast_to(v, (v.shape[0], LANES))
-    table = jnp.stack(
-        [spread(tab_f), spread(tab_b[:, :1]), jnp.tile(tab_b[:, 1:], (1, LANES // 4))]
-    )
+    tab_b = reordered(jnp.concatenate([mine_b, mine_b, weight_b[:, None]], axis=1), order_b)
+    tables = tab_f, tab_b
 
     first = jnp.concatenate([x_fwd, x_bwd[:, :half], grad_out, x_bwd[:, half:]], axis=1)
     lines = gathered(first, "z")
     a_part, b_part = lines[:, : width + half], lines[:, width + half :]
-    a_parts = relayed(gathered(a_part, "x"), "y")
-    b_parts = relayed(gathered(b_part, "y"), "x")
+    a_parts = relayed(gathered(a_part, "x"), "y", tables)
+    b_parts = relayed(gathered(b_part, "y"), "x", tables)
 
     (
         w_g, w_u, w_d, gate_b, up_b,
         f_own, f_one_lo, f_one_hi, f_two_lo, f_two_hi, f_three_lo, f_three_hi,
-    ) = forward(a_parts, table, w_gate[0], w_up[0], w_down[0])
-    b_own, b_one, b_two, b_three, p_own = backward(b_parts, gate_b, up_b, table, w_g, w_u, w_d)
+    ) = forward(a_parts, tab_f, w_gate[0], w_up[0], w_down[0])
+    b_own, b_one, b_two, b_three, p_own = backward(b_parts, gate_b, up_b, tab_b, w_g, w_u, w_d)
+
+    f_two_lo, f_two_hi = after(f_two_lo, b_own), after(f_two_hi, b_own)
 
     f_three_lo = (f_three_lo + swap(f_two_lo, "y", 1).astype(F32)).astype(BF16)
     f_one_hi = (f_one_hi + swap(f_two_hi, "y", 3).astype(F32)).astype(BF16)
@@ -301,18 +312,16 @@
         + swap(jnp.concatenate([f_one_lo, f_one_hi], axis=0), "y", 1).astype(F32)
         + swap(jnp.concatenate([f_three_lo, f_three_hi], axis=0), "y", 3).astype(F32)
     )
-    sum_b, sum_p = b_own, p_own[:, :4]
+    sum_b, sum_p = after(b_own, sum_f), p_own[:, :4]
     for j, block in enumerate((b_one, b_two, b_three), 1):
         got = swap(block, "x", j).astype(F32)
         sum_b = sum_b + got[:, :width]
         sum_p = sum_p + got[:, width : width + 4] + got[:, width + 4 : width + 8]
 
     sum_f = scattered(*cut(sum_f, BF16), "x")
-    top = lax.reduce_precision(sum_p, 8, 7)
-    coded = jnp.pad(jnp.concatenate([top, sum_p - top], axis=1), ((0, 0), (0, LANES - 8)))
-    both = scattered(*cut(jnp.concatenate([sum_b, coded], axis=1), BF16), "y")
-    sum_b, coded = both[:, :width], both[:, width:]
-    last = scattered(*cut(jnp.concatenate([sum_f, sum_b, coded], axis=1), F32), "z")
+    both = scattered(*cut(jnp.concatenate([sum_b, coded(sum_p)], axis=1), BF16), "y")
+    sum_b, sum_p = both[:, :width], decoded(both[:, width:])
+    last = scattered(*cut(jnp.concatenate([sum_f, sum_b, coded(sum_p)], axis=1), F32), "z")
 
     layer_out = (x_fwd.astype(F32) + last[:, :width]).astype(BF16)
     input_grad = (grad_out.astype(F32) + last[:, width : 2 * width]).astype(BF16)

time: 130 us -> 131 us (level)
  waiting for transfers between devices: 46.8 us -> 45.4 us
    ppermute x1, starting transfers between devices: 12.4 us -> 15 us  [handed_on(): got_far = lax.ppermute(jnp.where(even, back, forth), 'segment', far)]
    ppermute x33, starting transfers between devices: 48.4 us -> 46.9 us  [swap(): lax.ppermute(value, 'expert', [(i, i ^ by * STRIDE[along]) for i in range...]
  transfers between devices with their start and end apart: 35 -> 35, of which waited for: 16 -> 18; matrix products, arithmetic and copies ran while one was open for 3% -> 3% of each run, Pallas kernels for 9% -> 5%
where the time goes in v2:
time: 131 us; the launch traced here: 130 us
  starting transfers between devices  61.9 us (47%)
  waiting for transfers between devices  45.4 us (35%)
  Pallas kernels  12 us (9%)
  other arithmetic  6.7 us (5%)
  local copies, waits for them, and re-layouts  2.8 us (2%)
    ppermute x33, starting transfers between devices, swap(): lax.ppermute(value, 'expert', [(i, i ^ by * STRIDE[along]) for i in range...  46.9 us
    ppermute x33, waiting for transfers between devices, swap(): lax.ppermute(value, 'expert', [(i, i ^ by * STRIDE[along]) for i in range...  44.4 us
    ppermute x1, starting transfers between devices, handed_on(): got_far = lax.ppermute(jnp.where(even, back, forth), 'segment', far)  15 us
    pallas_call x1, Pallas kernels, forward(): pl.pallas_call(forward_kernel, out_shape=(out(w_g.shape, BF16), out(w_u.s...  5.23 us
    pallas_call x1, Pallas kernels, backward(): pl.pallas_call(backward_kernel, out_shape=(out((rows, width), F32), sent,...  5.15 us
  transfers between devices with their start and end apart: 35, of which 18 were waited for; matrix products, arithmetic and copies ran while one was open for 3% of the time, Pallas kernels for 5%

profile of v2, /device:TPU:1, one launch (start us, length us, event | category | flops | bytes accessed | tf_op | source)
XLA Modules:
  0.0 129.8 jit_solution(11194353026922571353)
XLA Ops:
  2.2 2.6 %collective-permute-start = (bf16[2,21504]{1,0:T(2,128)(2,1)S(1)}, bf16[2,21504]{1,0:T(2,128)(2,1)S(1)}, u32[]{:S(2)}, u32[]{:S(2)}) collective-permute-start(bf16[2,21504]{1,0:T(2,128)(2,1)S(1)} %pad_maximum_fusion.7), channel_id=1, source_target_pairs={{0,1},{1,0},{2,3},{3,2},{4,5},{5,4},{6,7},{7,6},{8,9},{9,8},{10,11... | collective-permute-start | bytes 258056 | tf_op jit(solution)/shard_map/ppermute | solution.py:22
  4.8 3.0 %collective-permute-start.1 = (bf16[2,21504]{1,0:T(2,128)(2,1)S(1)}, bf16[2,21504]{1,0:T(2,128)(2,1)S(1)}, u32[]{:S(2)}, u32[]{:S(2)}) collective-permute-start(bf16[2,21504]{1,0:T(2,128)(2,1)S(1)} %pad_maximum_fusion.7), channel_id=1, source_target_pairs={{0,2},{1,3},{2,0},{3,1},{4,6},{5,7},{6,4},{7,5},{8,10},{9,11},{10,... | collective-permute-start | bytes 258056 | tf_op jit(solution)/shard_map/ppermute | solution.py:22
  10.3 2.7 %collective-permute-done.2 = bf16[2,21504]{1,0:T(2,128)(2,1)S(1)} collective-permute-done((bf16[2,21504]{1,0:T(2,128)(2,1)S(1)}, bf16[2,21504]{1,0:T(2,128)(2,1)S(1)}, u32[]{:S(2)}, u32[]{:S(2)}) %collective-permute-start.2) | collective-permute-done | bytes 86048 | tf_op jit(solution)/shard_map/ppermute | solution.py:22
  15.6 2.5 %collective-permute-start.4 = (bf16[8,10752]{1,0:T(8,128)(2,1)S(1)}, bf16[8,10752]{1,0:T(8,128)(2,1)S(1)}, u32[]{:S(2)}, u32[]{:S(2)}) collective-permute-start(bf16[8,10752]{1,0:T(8,128)(2,1)S(1)} %get-tuple-element.66), channel_id=1, source_target_pairs={{0,8},{1,9},{2,10},{3,11},{4,12},{5,13},{6,14},{7,15},{8,0},{9,1},... | collective-permute-start | bytes 516104 | tf_op jit(solution)/shard_map/ppermute | solution.py:22
  19.7 2.6 %collective-permute-start.11 = (bf16[8,10752]{1,0:T(8,128)(2,1)S(1)}, bf16[8,10752]{1,0:T(8,128)(2,1)S(1)}, u32[]{:S(2)}, u32[]{:S(2)}) collective-permute-start(bf16[8,10752]{1,0:T(8,128)(2,1)S(1)} %get-tuple-element.67), channel_id=1, source_target_pairs={{0,32},{1,33},{2,34},{3,35},{4,36},{5,37},{6,38},{7,39},{8,40},{9,... | collective-permute-start | bytes 516104 | tf_op jit(solution)/shard_map/ppermute | solution.py:22
  25.9 1.9 %collective-permute-start.7 = (bf16[32,10752]{1,0:T(8,128)(2,1)S(1)}, bf16[32,10752]{1,0:T(8,128)(2,1)S(1)}, u32[]{:S(2)}, u32[]{:S(2)}) collective-permute-start(bf16[32,10752]{1,0:T(8,128)(2,1)S(1)} %pad_maximum_fusion.1.refs_0_), channel_id=1, source_target_pairs={{0,48},{1,49},{2,50},{3,51},{4,52},{5,53},{6,54},{7,55},{8,56},{9,... | collective-permute-start | bytes 2064392 | tf_op jit(solution)/shard_map/ppermute | solution.py:22
  28.9 2.6 %collective-permute-start.14 = (bf16[32,10752]{1,0:T(8,128)(2,1)S(1)}, bf16[32,10752]{1,0:T(8,128)(2,1)}, u32[]{:S(2)}, u32[]{:S(2)}) collective-permute-start(bf16[32,10752]{1,0:T(8,128)(2,1)S(1)} %pad_maximum_fusion.2.refs_0_), channel_id=1, source_target_pairs={{0,12},{1,13},{2,14},{3,15},{4,8},{5,9},{6,10},{7,11},{8,4},{9,5},... | collective-permute-start | bytes 2064392 | tf_op jit(solution)/shard_map/ppermute | solution.py:22
  32.8 8.0 %collective-permute-done.6.one.refs_1_ = bf16[32,10752]{1,0:T(8,128)(2,1)S(1)} collective-permute-done((bf16[32,10752]{1,0:T(8,128)(2,1)S(1)}, bf16[32,10752]{1,0:T(8,128)(2,1)S(1)}, u32[]{:S(2)}, u32[]{:S(2)}) %collective-permute-start.6) | collective-permute-done | bytes 688160 | tf_op jit(solution)/shard_map/ppermute | solution.py:22
  40.9 4.8 %collective-permute-done.7.three.refs_4_ = bf16[32,10752]{1,0:T(8,128)(2,1)S(1)} collective-permute-done((bf16[32,10752]{1,0:T(8,128)(2,1)S(1)}, bf16[32,10752]{1,0:T(8,128)(2,1)S(1)}, u32[]{:S(2)}, u32[]{:S(2)}) %collective-permute-start.7) | collective-permute-done | bytes 688160 | tf_op jit(solution)/shard_map/ppermute | solution.py:22
  48.9 1.7 %collective-permute-start.15 = (bf16[16,10752]{1,0:T(8,128)(2,1)S(1)}, bf16[16,10752]{1,0:T(8,128)(2,1)S(1)}, u32[]{:S(2)}, u32[]{:S(2)}) collective-permute-start(bf16[16,10752]{1,0:T(8,128)(2,1)S(1)} %get-tuple-element.33), channel_id=1, source_target_pairs={{0,4},{1,5},{2,6},{3,7},{4,0},{5,1},{6,2},{7,3},{8,12},{9,13},{10,... | collective-permute-start | bytes 1032200 | tf_op jit(solution)/shard_map/ppermute | solution.py:22
  51.3 2.4 %collective-permute-done.8.refs_2_ = bf16[16,10752]{1,0:T(8,128)(2,1)S(1)} collective-permute-done((bf16[16,10752]{1,0:T(8,128)(2,1)S(1)}, bf16[16,10752]{1,0:T(8,128)(2,1)S(1)}, u32[]{:S(2)}, u32[]{:S(2)}) %collective-permute-start.8) | collective-permute-done | bytes 344096 | tf_op jit(solution)/shard_map/ppermute | solution.py:22
  53.7 1.8 %collective-permute-done.9.refs_3_ = bf16[16,10752]{1,0:T(8,128)(2,1)S(1)} collective-permute-done((bf16[16,10752]{1,0:T(8,128)(2,1)S(1)}, bf16[16,10752]{1,0:T(8,128)(2,1)S(1)}, u32[]{:S(2)}, u32[]{:S(2)}) %collective-permute-start.9) | collective-permute-done | bytes 344096 | tf_op jit(solution)/shard_map/ppermute | solution.py:22
  55.6 5.2 %shard_map.122 = (bf16[7168,256]{1,0:T(8,128)(2,1)S(1)}, bf16[7168,256]{1,0:T(8,128)(2,1)S(1)}, bf16[256,7168]{1,0:T(8,128)(2,1)S(1)}, f32[128,256]{1,0:T(8,128)...) custom-call(bf16[32,10752]{1,0:T(8,128)(2,1)S(1)} %pad_maximum_fusio, ...), custom_call_target="tpu_custom_call" | custom-call | flops 10000000000 | bytes 10000000 | tf_op jit(solution)/shard_map/pallas_call | solution.py:188
  60.8 5.1 %shard_map.124 = (f32[32,7168]{1,0:T(8,128)S(1)}, bf16[32,7296]{1,0:T(8,128)(2,1)S(1)}, bf16[32,7296]{1,0:T(8,128)(2,1)S(1)}, bf16[32,7296]{1,0:T(8,128)(2,1)S(1)}, f32[32,8]{1,0:T(8,128)S(1)}) custom-call(bf16[32,10752]{1,0:T(8,128)(2,1)S(1)} %pad_maximum_fusion.2.refs_0_, bf16[32,10752]{1,0:T(8,128)(2,1)S(1)} %collective-permute-done.13.one.refs_1_, ...), custom_call_target="tpu_custom_call" | custom-call | flops 10000000000 | bytes 10000000 | tf_op jit(solution)/shard_map/pallas_call | solution.py:259
  66.2 2.0 %collective-permute-start.24 = (bf16[32,7296]{1,0:T(8,128)(2,1)S(1)}, bf16[32,7296]{1,0:T(8,128)(2,1)S(1)}, u32[]{:S(2)}, u32[]{:S(2)}) collective-permute-start(bf16[32,7296]{1,0:T(8,128)(2,1)S(1)} %get-tuple-element.47), channel_id=1, source_target_pairs={{0,4},{1,5},{2,6},{3,7},{4,0},{5,1},{6,2},{7,3},{8,12},{9,13},{10,... | collective-permute-start | bytes 1400840 | tf_op jit(solution)/shard_map/ppermute | solution.py:22
  68.2 2.3 %collective-permute-start.26 = (bf16[32,7296]{1,0:T(8,128)(2,1)S(1)}, bf16[32,7296]{1,0:T(8,128)(2,1)S(1)}, u32[]{:S(2)}, u32[]{:S(2)}) collective-permute-start(bf16[32,7296]{1,0:T(8,128)(2,1)S(1)} %get-tuple-element.49), channel_id=1, source_target_pairs={{0,12},{1,13},{2,14},{3,15},{4,8},{5,9},{6,10},{7,11},{8,4},{9,5},... | collective-permute-start | bytes 1400840 | tf_op jit(solution)/shard_map/ppermute | solution.py:22
  72.5 2.0 %collective-permute-start.20 = (bf16[32,7168]{1,0:T(8,128)(2,1)S(1)}, bf16[32,7168]{1,0:T(8,128)(2,1)S(1)}, u32[]{:S(2)}, u32[]{:S(2)}) collective-permute-start(bf16[32,7168]{1,0:T(8,128)(2,1)S(1)} %pad_maximum_fusion.5), channel_id=1, source_target_pairs={{0,48},{1,49},{2,50},{3,51},{4,52},{5,53},{6,54},{7,55},{8,56},{9,... | collective-permute-start | bytes 1376264 | tf_op jit(solution)/shard_map/ppermute | solution.py:22
  75.6 9.1 %collective-permute-done.25 = bf16[32,7296]{1,0:T(8,128)(2,1)S(1)} collective-permute-done((bf16[32,7296]{1,0:T(8,128)(2,1)S(1)}, bf16[32,7296]{1,0:T(8,128)(2,1)S(1)}, u32[]{:S(2)}, u32[]{:S(2)}) %collective-permute-start.25) | collective-permute-done | bytes 466976 | tf_op jit(solution)/shard_map/ppermute | solution.py:22
  86.6 3.2 %collective-permute-start.22 = (bf16[8,7168]{1,0:T(8,128)(2,1)S(1)}, bf16[8,7168]{1,0:T(8,128)(2,1)S(1)}, u32[]{:S(2)}, u32[]{:S(2)}) collective-permute-start(bf16[8,7168]{1,0:T(8,128)(2,1)S(1)} %get-tuple-element.65), channel_id=1, source_target_pairs={{0,8},{1,9},{2,10},{3,11},{4,12},{5,13},{6,14},{7,15},{8,0},{9,1},... | collective-permute-start | bytes 344072 | tf_op jit(solution)/shard_map/ppermute | solution.py:22
  91.5 1.8 %collective-permute-start.28 = (bf16[8,7296]{1,0:T(8,128)(2,1)S(1)}, bf16[8,7296]{1,0:T(8,128)(2,1)S(1)}, u32[]{:S(2)}, u32[]{:S(2)}) collective-permute-start(bf16[8,7296]{1,0:T(8,128)(2,1)S(1)} %get-tuple-element.59), channel_id=1, source_target_pairs={{0,32},{1,33},{2,34},{3,35},{4,36},{5,37},{6,38},{7,39},{8,40},{9,... | collective-permute-start | bytes 350216 | tf_op jit(solution)/shard_map/ppermute | solution.py:22
  94.7 2.0 %collective-permute-done.28 = bf16[8,7296]{1,0:T(8,128)(2,1)S(1)} collective-permute-done((bf16[8,7296]{1,0:T(8,128)(2,1)S(1)}, bf16[8,7296]{1,0:T(8,128)(2,1)S(1)}, u32[]{:S(2)}, u32[]{:S(2)}) %collective-permute-start.28) | collective-permute-done | bytes 116768 | tf_op jit(solution)/shard_map/ppermute | solution.py:22
  98.6 6.6 %collective-permute-start.30 = (f32[2,14464]{1,0:T(2,128)S(1)}, f32[2,14464]{1,0:T(2,128)S(1)}, u32[]{:S(2)}, u32[]{:S(2)}) collective-permute-start(f32[2,14464]{1,0:T(2,128)S(1)} %get-tuple-element.60), channel_id=1, source_target_pairs={{0,1},{1,0},{2,3},{3,2},{4,5},{5,4},{6,7},{7,6},{8,9},{9,8},{10,11... | collective-permute-start | bytes 347144 | tf_op jit(solution)/shard_map/ppermute | solution.py:22
  107.7 4.5 %collective-permute-done.31 = f32[2,14464]{1,0:T(2,128)S(1)} collective-permute-done((f32[2,14464]{1,0:T(2,128)S(1)}, f32[2,14464]{1,0:T(2,128)S(1)}, u32[]{:S(2)}, u32[]{:S(2)}) %collective-permute-start.31) | collective-permute-done | bytes 115744 | tf_op jit(solution)/shard_map/ppermute | solution.py:22
  112.5 15.0 %collective-permute-start.33 = (bf16[2,7168]{1,0:T(2,128)(2,1)S(1)}, bf16[2,7168]{1,0:T(2,128)(2,1)S(1)}, u32[]{:S(2)}, u32[]{:S(2)}) collective-permute-start(bf16[2,7168]{1,0:T(2,128)(2,1)S(1)} %get-tuple-element.71), channel_id=1, source_target_pairs={{0,192},{64,128},{128,64},{192,0},{1,193},{65,129},{129,65},{193,1... | collective-permute-start | bytes 86024 | tf_op jit(solution)/shard_map/ppermute | solution.py:37
  (106 shorter events, 33.4 us)
Async XLA Ops:
  2.2 7.1 %collective-permute-start = (bf16[2,21504]{1,0:T(2,128)(2,1)S(1)}, bf16[2,21504]{1,0:T(2,128)(2,1)S(1)}, u32[]{:S(2)}, u32[]{:S(2)}) collective-permute-start(bf16[2,21504]{1,0:T(2,128)(2,1)S(1)} %pad_maximum_fusion.7), channel_id=1, source_target_pairs={{0,1},{1,0},{2,3},{3,2},{4,5},{5,4},{6,7},{7,6},{8,9},{9,8},{10,11... | collective-permute-start | bytes 258056 | tf_op jit(solution)/shard_map/ppermute | solution.py:22
  14.3 8.1 %collective-permute-start.3 = (bf16[8,10752]{1,0:T(8,128)(2,1)S(1)}, bf16[8,10752]{1,0:T(8,128)(2,1)S(1)}, u32[]{:S(2)}, u32[]{:S(2)}) collective-permute-start(bf16[8,10752]{1,0:T(8,128)(2,1)S(1)} %get-tuple-element.66), channel_id=1, source_target_pairs={{0,4},{1,5},{2,6},{3,7},{4,0},{5,1},{6,2},{7,3},{8,12},{9,13},{10,... | collective-permute-start | bytes 516104 | tf_op jit(solution)/shard_map/ppermute | solution.py:22
  15.6 7.5 %collective-permute-start.4 = (bf16[8,10752]{1,0:T(8,128)(2,1)S(1)}, bf16[8,10752]{1,0:T(8,128)(2,1)S(1)}, u32[]{:S(2)}, u32[]{:S(2)}) collective-permute-start(bf16[8,10752]{1,0:T(8,128)(2,1)S(1)} %get-tuple-element.66), channel_id=1, source_target_pairs={{0,8},{1,9},{2,10},{3,11},{4,12},{5,13},{6,14},{7,15},{8,0},{9,1},... | collective-permute-start | bytes 516104 | tf_op jit(solution)/shard_map/ppermute | solution.py:22
  18.0 6.5 %collective-permute-start.5 = (bf16[8,10752]{1,0:T(8,128)(2,1)S(1)}, bf16[8,10752]{1,0:T(8,128)(2,1)S(1)}, u32[]{:S(2)}, u32[]{:S(2)}) collective-permute-start(bf16[8,10752]{1,0:T(8,128)(2,1)S(1)} %get-tuple-element.66), channel_id=1, source_target_pairs={{0,12},{1,13},{2,14},{3,15},{4,8},{5,9},{6,10},{7,11},{8,4},{9,5},... | collective-permute-start | bytes 516104 | tf_op jit(solution)/shard_map/ppermute | solution.py:22
  18.3 9.5 %collective-permute-start.10 = (bf16[8,10752]{1,0:T(8,128)(2,1)S(1)}, bf16[8,10752]{1,0:T(8,128)(2,1)S(1)}, u32[]{:S(2)}, u32[]{:S(2)}) collective-permute-start(bf16[8,10752]{1,0:T(8,128)(2,1)S(1)} %get-tuple-element.67), channel_id=1, source_target_pairs={{0,16},{1,17},{2,18},{3,19},{4,20},{5,21},{6,22},{7,23},{8,24},{9,... | collective-permute-start | bytes 516104 | tf_op jit(solution)/shard_map/ppermute | solution.py:22
  19.7 8.1 %collective-permute-start.11 = (bf16[8,10752]{1,0:T(8,128)(2,1)S(1)}, bf16[8,10752]{1,0:T(8,128)(2,1)S(1)}, u32[]{:S(2)}, u32[]{:S(2)}) collective-permute-start(bf16[8,10752]{1,0:T(8,128)(2,1)S(1)} %get-tuple-element.67), channel_id=1, source_target_pairs={{0,32},{1,33},{2,34},{3,35},{4,36},{5,37},{6,38},{7,39},{8,40},{9,... | collective-permute-start | bytes 516104 | tf_op jit(solution)/shard_map/ppermute | solution.py:22
  24.5 16.3 %collective-permute-start.6 = (bf16[32,10752]{1,0:T(8,128)(2,1)S(1)}, bf16[32,10752]{1,0:T(8,128)(2,1)S(1)}, u32[]{:S(2)}, u32[]{:S(2)}) collective-permute-start(bf16[32,10752]{1,0:T(8,128)(2,1)S(1)} %pad_maximum_fusion.1.refs_0_), channel_id=1, source_target_pairs={{0,16},{1,17},{2,18},{3,19},{4,20},{5,21},{6,22},{7,23},{8,24},{9,... | collective-permute-start | bytes 2064392 | tf_op jit(solution)/shard_map/ppermute | solution.py:22
  25.9 19.7 %collective-permute-start.7 = (bf16[32,10752]{1,0:T(8,128)(2,1)S(1)}, bf16[32,10752]{1,0:T(8,128)(2,1)S(1)}, u32[]{:S(2)}, u32[]{:S(2)}) collective-permute-start(bf16[32,10752]{1,0:T(8,128)(2,1)S(1)} %pad_maximum_fusion.1.refs_0_), channel_id=1, source_target_pairs={{0,48},{1,49},{2,50},{3,51},{4,52},{5,53},{6,54},{7,55},{8,56},{9,... | collective-permute-start | bytes 2064392 | tf_op jit(solution)/shard_map/ppermute | solution.py:22
  28.8 18.7 %collective-permute-start.13 = (bf16[32,10752]{1,0:T(8,128)(2,1)S(1)}, bf16[32,10752]{1,0:T(8,128)(2,1)S(1)}, u32[]{:S(2)}, u32[]{:S(2)}) collective-permute-start(bf16[32,10752]{1,0:T(8,128)(2,1)S(1)} %pad_maximum_fusion.2.refs_0_), channel_id=1, source_target_pairs={{0,4},{1,5},{2,6},{3,7},{4,0},{5,1},{6,2},{7,3},{8,12},{9,13},{10,... | collective-permute-start | bytes 2064392 | tf_op jit(solution)/shard_map/ppermute | solution.py:22
  28.9 18.6 %collective-permute-start.14 = (bf16[32,10752]{1,0:T(8,128)(2,1)S(1)}, bf16[32,10752]{1,0:T(8,128)(2,1)}, u32[]{:S(2)}, u32[]{:S(2)}) collective-permute-start(bf16[32,10752]{1,0:T(8,128)(2,1)S(1)} %pad_maximum_fusion.2.refs_0_), channel_id=1, source_target_pairs={{0,12},{1,13},{2,14},{3,15},{4,8},{5,9},{6,10},{7,11},{8,4},{9,5},... | collective-permute-start | bytes 2064392 | tf_op jit(solution)/shard_map/ppermute | solution.py:22
  46.8 7.0 %collective-permute-start.8 = (bf16[16,10752]{1,0:T(8,128)(2,1)S(1)}, bf16[16,10752]{1,0:T(8,128)(2,1)S(1)}, u32[]{:S(2)}, u32[]{:S(2)}) collective-permute-start(bf16[16,10752]{1,0:T(8,128)(2,1)S(1)} %get-tuple-element.27), channel_id=1, source_target_pairs={{0,16},{1,17},{2,18},{3,19},{4,20},{5,21},{6,22},{7,23},{8,24},{9,... | collective-permute-start | bytes 1032200 | tf_op jit(solution)/shard_map/ppermute | solution.py:22
  47.2 8.3 %collective-permute-start.9 = (bf16[16,10752]{1,0:T(8,128)(2,1)S(1)}, bf16[16,10752]{1,0:T(8,128)(2,1)S(1)}, u32[]{:S(2)}, u32[]{:S(2)}) collective-permute-start(bf16[16,10752]{1,0:T(8,128)(2,1)S(1)} %get-tuple-element.28), channel_id=1, source_target_pairs={{0,48},{1,49},{2,50},{3,51},{4,52},{5,53},{6,54},{7,55},{8,56},{9,... | collective-permute-start | bytes 1032200 | tf_op jit(solution)/shard_map/ppermute | solution.py:22
  48.9 11.9 %collective-permute-start.15 = (bf16[16,10752]{1,0:T(8,128)(2,1)S(1)}, bf16[16,10752]{1,0:T(8,128)(2,1)S(1)}, u32[]{:S(2)}, u32[]{:S(2)}) collective-permute-start(bf16[16,10752]{1,0:T(8,128)(2,1)S(1)} %get-tuple-element.33), channel_id=1, source_target_pairs={{0,4},{1,5},{2,6},{3,7},{4,0},{5,1},{6,2},{7,3},{8,12},{9,13},{10,... | collective-permute-start | bytes 1032200 | tf_op jit(solution)/shard_map/ppermute | solution.py:22
  50.6 10.2 %collective-permute-start.16 = (bf16[16,10752]{1,0:T(8,128)(2,1)S(1)}, bf16[16,10752]{1,0:T(8,128)(2,1)S(1)}, u32[]{:S(2)}, u32[]{:S(2)}) collective-permute-start(bf16[16,10752]{1,0:T(8,128)(2,1)S(1)} %get-tuple-element.34), channel_id=1, source_target_pairs={{0,12},{1,13},{2,14},{3,15},{4,8},{5,9},{6,10},{7,11},{8,4},{9,5},... | collective-permute-start | bytes 1032200 | tf_op jit(solution)/shard_map/ppermute | solution.py:22
  66.2 9.4 %collective-permute-start.24 = (bf16[32,7296]{1,0:T(8,128)(2,1)S(1)}, bf16[32,7296]{1,0:T(8,128)(2,1)S(1)}, u32[]{:S(2)}, u32[]{:S(2)}) collective-permute-start(bf16[32,7296]{1,0:T(8,128)(2,1)S(1)} %get-tuple-element.47), channel_id=1, source_target_pairs={{0,4},{1,5},{2,6},{3,7},{4,0},{5,1},{6,2},{7,3},{8,12},{9,13},{10,... | collective-permute-start | bytes 1400840 | tf_op jit(solution)/shard_map/ppermute | solution.py:22
  68.1 16.5 %collective-permute-start.25 = (bf16[32,7296]{1,0:T(8,128)(2,1)S(1)}, bf16[32,7296]{1,0:T(8,128)(2,1)S(1)}, u32[]{:S(2)}, u32[]{:S(2)}) collective-permute-start(bf16[32,7296]{1,0:T(8,128)(2,1)S(1)} %get-tuple-element.48), channel_id=1, source_target_pairs={{0,8},{1,9},{2,10},{3,11},{4,12},{5,13},{6,14},{7,15},{8,0},{9,1},... | collective-permute-start | bytes 1400840 | tf_op jit(solution)/shard_map/ppermute | solution.py:22
  68.2 16.5 %collective-permute-start.26 = (bf16[32,7296]{1,0:T(8,128)(2,1)S(1)}, bf16[32,7296]{1,0:T(8,128)(2,1)S(1)}, u32[]{:S(2)}, u32[]{:S(2)}) collective-permute-start(bf16[32,7296]{1,0:T(8,128)(2,1)S(1)} %get-tuple-element.49), channel_id=1, source_target_pairs={{0,12},{1,13},{2,14},{3,15},{4,8},{5,9},{6,10},{7,11},{8,4},{9,5},... | collective-permute-start | bytes 1400840 | tf_op jit(solution)/shard_map/ppermute | solution.py:22
  72.3 12.8 %collective-permute-start.18 = (bf16[32,7168]{1,0:T(8,128)(2,1)S(1)}, bf16[32,7168]{1,0:T(8,128)(2,1)S(1)}, u32[]{:S(2)}, u32[]{:S(2)}) collective-permute-start(bf16[32,7168]{1,0:T(8,128)(2,1)S(1)} %pad_maximum_fusion.4), channel_id=1, source_target_pairs={{0,16},{1,17},{2,18},{3,19},{4,20},{5,21},{6,22},{7,23},{8,24},{9,... | collective-permute-start | bytes 1376264 | tf_op jit(solution)/shard_map/ppermute | solution.py:22
  72.5 12.6 %collective-permute-start.20 = (bf16[32,7168]{1,0:T(8,128)(2,1)S(1)}, bf16[32,7168]{1,0:T(8,128)(2,1)S(1)}, u32[]{:S(2)}, u32[]{:S(2)}) collective-permute-start(bf16[32,7168]{1,0:T(8,128)(2,1)S(1)} %pad_maximum_fusion.5), channel_id=1, source_target_pairs={{0,48},{1,49},{2,50},{3,51},{4,52},{5,53},{6,54},{7,55},{8,56},{9,... | collective-permute-start | bytes 1376264 | tf_op jit(solution)/shard_map/ppermute | solution.py:22
  85.2 8.1 %collective-permute-start.21 = (bf16[8,7168]{1,0:T(8,128)(2,1)S(1)}, bf16[8,7168]{1,0:T(8,128)(2,1)S(1)}, u32[]{:S(2)}, u32[]{:S(2)}) collective-permute-start(bf16[8,7168]{1,0:T(8,128)(2,1)S(1)} %get-tuple-element.63), channel_id=1, source_target_pairs={{0,4},{1,5},{2,6},{3,7},{4,0},{5,1},{6,2},{7,3},{8,12},{9,13},{10,... | collective-permute-start | bytes 344072 | tf_op jit(solution)/shard_map/ppermute | solution.py:22
  86.6 7.6 %collective-permute-start.22 = (bf16[8,7168]{1,0:T(8,128)(2,1)S(1)}, bf16[8,7168]{1,0:T(8,128)(2,1)S(1)}, u32[]{:S(2)}, u32[]{:S(2)}) collective-permute-start(bf16[8,7168]{1,0:T(8,128)(2,1)S(1)} %get-tuple-element.65), channel_id=1, source_target_pairs={{0,8},{1,9},{2,10},{3,11},{4,12},{5,13},{6,14},{7,15},{8,0},{9,1},... | collective-permute-start | bytes 344072 | tf_op jit(solution)/shard_map/ppermute | solution.py:22
  98.6 9.1 %collective-permute-start.30 = (f32[2,14464]{1,0:T(2,128)S(1)}, f32[2,14464]{1,0:T(2,128)S(1)}, u32[]{:S(2)}, u32[]{:S(2)}) collective-permute-start(f32[2,14464]{1,0:T(2,128)S(1)} %get-tuple-element.60), channel_id=1, source_target_pairs={{0,1},{1,0},{2,3},{3,2},{4,5},{5,4},{6,7},{7,6},{8,9},{9,8},{10,11... | collective-permute-start | bytes 347144 | tf_op jit(solution)/shard_map/ppermute | solution.py:22
  105.3 7.0 %collective-permute-start.31 = (f32[2,14464]{1,0:T(2,128)S(1)}, f32[2,14464]{1,0:T(2,128)S(1)}, u32[]{:S(2)}, u32[]{:S(2)}) collective-permute-start(f32[2,14464]{1,0:T(2,128)S(1)} %get-tuple-element.62), channel_id=1, source_target_pairs={{0,2},{1,3},{2,0},{3,1},{4,6},{5,7},{6,4},{7,5},{8,10},{9,11},{10,... | collective-permute-start | bytes 347144 | tf_op jit(solution)/shard_map/ppermute | solution.py:22
  112.5 16.7 %collective-permute-start.33 = (bf16[2,7168]{1,0:T(2,128)(2,1)S(1)}, bf16[2,7168]{1,0:T(2,128)(2,1)S(1)}, u32[]{:S(2)}, u32[]{:S(2)}) collective-permute-start(bf16[2,7168]{1,0:T(2,128)(2,1)S(1)} %get-tuple-element.71), channel_id=1, source_target_pairs={{0,192},{64,128},{128,64},{192,0},{1,193},{65,129},{129,65},{193,1... | collective-permute-start | bytes 86024 | tf_op jit(solution)/shard_map/ppermute | solution.py:37
  (17 other events, 114.2 us)

commit v3 on v2

--- a/solution.py
+++ b/solution.py
@@ -135,11 +135,10 @@
 def forward_kernel(*refs):
     parts, tab_ref, hbm = refs[:5], refs[5], refs[6:9]
     wg, wu, wd, gate_b, up_b = refs[9:14]
-    own, one_lo, one_hi, two_lo, two_hi, three_lo, three_hi, sems = refs[14:]
+    own, one, two, three, sems = refs[14:]
     width = wg.shape[0]
     step = width // LOAD_CHUNKS
     rows = parts[0].shape[0]
-    count, half = SIDE * rows, rows // 2
 
     def load(kind, c):
         part = pl.ds(c * step, step)
@@ -171,18 +170,14 @@
         out = weight * dot(hidden, wd[:, part])
         own[:, part] = out[:rows]
         sent = out.astype(BF16)
-        one_lo[:, part] = sent[rows : rows + half]
-        one_hi[:, part] = out[rows + half : 2 * rows]
-        two_lo[:, part] = sent[2 * rows : 2 * rows + half]
-        two_hi[:, part] = sent[2 * rows + half : 3 * rows]
-        three_lo[:, part] = out[3 * rows : 3 * rows + half]
-        three_hi[:, part] = sent[3 * rows + half :]
+        for j, ref in enumerate((one, two, three), 1):
+            ref[:, part] = sent[j * rows : (j + 1) * rows]
 
 
 def forward(parts, table, w_g, w_u, w_d):
     width, hidden = w_g.shape
     rows = parts[0].shape[0]
-    half, count = rows // 2, SIDE * rows
+    count = SIDE * rows
     vmem = pl.BlockSpec(memory_space=pltpu.VMEM)
     out = jax.ShapeDtypeStruct
     return pl.pallas_call(
@@ -194,15 +189,12 @@
             out((count, hidden), F32),
             out((count, hidden), F32),
             out((rows, width), F32),
-            out((half, width), BF16),
-            out((half, width), F32),
-            out((half, width), BF16),
-            out((half, width), BF16),
-            out((half, width), F32),
-            out((half, width), BF16),
+            out((rows, width), BF16),
+            out((rows, width), BF16),
+            out((rows, width), BF16),
         ),
         in_specs=[vmem] * 6 + [pl.BlockSpec(memory_space=pl.ANY)] * 3,
-        out_specs=(vmem,) * 12,
+        out_specs=(vmem,) * 9,
         scratch_shapes=[pltpu.SemaphoreType.DMA((3, LOAD_CHUNKS))],
         compiler_params=pltpu.CompilerParams(vmem_limit_bytes=36 * 2**20),
         cost_estimate=pl.CostEstimate(flops=10**10, bytes_accessed=10**7, transcendentals=0),
@@ -211,7 +203,8 @@
 
 def backward_kernel(*refs):
     parts, (gate_b, up_b, tab_ref, wg, wu, wd) = refs[:5], refs[5:11]
-    own, one, two, three, p_own = refs[11:]
+    own, one_lo, one_hi, two_lo, two_hi, three_lo, three_hi, p_own = refs[11:]
+    blocks = (one_lo, one_hi, two_lo, two_hi, three_lo, three_hi)
     width = wg.shape[0]
     half_width, step = width // 2, width // CHUNKS
     rows = parts[0].shape[0]
@@ -238,16 +231,16 @@
     top = prob.astype(BF16).astype(F32)
     lane = lax.broadcasted_iota(jnp.int32, prob.shape, 1)
     parts_of = jnp.where(lane < 4, top, prob - top).astype(BF16)
-    for j, ref in enumerate((one, two, three), 1):
-        ref[:, width:] = jnp.zeros((rows, LANES), BF16)
-        ref[:, width : width + 8] = parts_of[j * rows : (j + 1) * rows]
+    half = rows // 2
+    for i, ref in enumerate(blocks, 2):
+        ref[:, width:] = jnp.zeros((half, LANES), ref.dtype)
+        ref[:, width : width + 8] = parts_of[i * half : (i + 1) * half].astype(ref.dtype)
     for c in range(CHUNKS):
         part = slice(c * step, (c + 1) * step)
         out = contract_last(grad_gate, wg[part, :]) + contract_last(grad_up, wu[part, :])
         own[:, part] = out[:rows]
-        sent = out.astype(BF16)
-        for j, ref in enumerate((one, two, three), 1):
-            ref[:, part] = sent[j * rows : (j + 1) * rows]
+        for i, ref in enumerate(blocks, 2):
+            ref[:, part] = out[i * half : (i + 1) * half].astype(ref.dtype)
 
 
 def backward(parts, gate_b, up_b, table, w_g, w_u, w_d):
@@ -255,12 +248,15 @@
     rows = parts[0].shape[0]
     vmem = pl.BlockSpec(memory_space=pltpu.VMEM)
     out = jax.ShapeDtypeStruct
-    sent = out((rows, width + LANES), BF16)
+    sent = out((rows // 2, width + LANES), BF16)
+    added = out((rows // 2, width + LANES), F32)
     return pl.pallas_call(
         backward_kernel,
-        out_shape=(out((rows, width), F32), sent, sent, sent, out((rows, 8), F32)),
+        out_shape=(
+            out((rows, width), F32), sent, added, sent, sent, added, sent, out((rows, 8), F32)
+        ),
         in_specs=[vmem] * 11,
-        out_specs=(vmem,) * 5,
+        out_specs=(vmem,) * 8,
         cost_estimate=pl.CostEstimate(flops=10**10, bytes_accessed=10**7, transcendentals=0),
         compiler_params=pltpu.CompilerParams(vmem_limit_bytes=24 * 2**20),
     )(*parts, gate_b, up_b, table, w_g, w_u, w_d)
@@ -297,26 +293,25 @@
     a_parts = relayed(gathered(a_part, "x"), "y", tables)
     b_parts = relayed(gathered(b_part, "y"), "x", tables)
 
-    (
-        w_g, w_u, w_d, gate_b, up_b,
-        f_own, f_one_lo, f_one_hi, f_two_lo, f_two_hi, f_three_lo, f_three_hi,
-    ) = forward(a_parts, tab_f, w_gate[0], w_up[0], w_down[0])
-    b_own, b_one, b_two, b_three, p_own = backward(b_parts, gate_b, up_b, tab_b, w_g, w_u, w_d)
-
-    f_two_lo, f_two_hi = after(f_two_lo, b_own), after(f_two_hi, b_own)
-
-    f_three_lo = (f_three_lo + swap(f_two_lo, "y", 1).astype(F32)).astype(BF16)
-    f_one_hi = (f_one_hi + swap(f_two_hi, "y", 3).astype(F32)).astype(BF16)
-    sum_f = (
-        f_own
-        + swap(jnp.concatenate([f_one_lo, f_one_hi], axis=0), "y", 1).astype(F32)
-        + swap(jnp.concatenate([f_three_lo, f_three_hi], axis=0), "y", 3).astype(F32)
-    )
-    sum_b, sum_p = after(b_own, sum_f), p_own[:, :4]
-    for j, block in enumerate((b_one, b_two, b_three), 1):
-        got = swap(block, "x", j).astype(F32)
-        sum_b = sum_b + got[:, :width]
-        sum_p = sum_p + got[:, width : width + 4] + got[:, width + 4 : width + 8]
+    w_g, w_u, w_d, gate_b, up_b, f_own, f_one, f_two, f_three = forward(
+        a_parts, tab_f, w_gate[0], w_up[0], w_down[0]
+    )
+    b_own, b_one_lo, b_one_hi, b_two_lo, b_two_hi, b_three_lo, b_three_hi, p_own = backward(
+        b_parts, gate_b, up_b, tab_b, w_g, w_u, w_d
+    )
+
+    sum_f = scattered(f_own, (f_one, f_two, f_three), "y")
+    def merged(one, two):
+        rest = coded(decoded(one[:, width:]) + decoded(two[:, width:].astype(F32)))
+        body_of = one[:, :width] + two[:, :width].astype(F32)
+        return jnp.concatenate([body_of.astype(BF16), rest.astype(BF16)], axis=1)
+
+    b_three_lo = merged(b_three_lo, swap(b_two_lo, "x", 1))
+    b_one_hi = merged(b_one_hi, swap(b_two_hi, "x", 3))
+    got_one = swap(jnp.concatenate([b_one_lo, b_one_hi], axis=0), "x", 1).astype(F32)
+    got_three = swap(jnp.concatenate([b_three_lo, b_three_hi], axis=0), "x", 3).astype(F32)
+    sum_b = b_own + got_one[:, :width] + got_three[:, :width]
+    sum_p = p_own[:, :4] + decoded(got_one[:, width:]) + decoded(got_three[:, width:])
 
     sum_f = scattered(*cut(sum_f, BF16), "x")
     both = scattered(*cut(jnp.concatenate([sum_b, coded(sum_p)], axis=1), BF16), "y")

time: 131 us -> 132 us (level)
  starting transfers between devices: 61.9 us -> 63.9 us
    ppermute x33, waiting for transfers between devices: 44.4 us -> 42.9 us  [swap(): lax.ppermute(value, 'expert', [(i, i ^ by * STRIDE[along]) for i in range...]
    ppermute x33, starting transfers between devices: 46.9 us -> 48.3 us  [swap(): lax.ppermute(value, 'expert', [(i, i ^ by * STRIDE[along]) for i in range...]
  transfers between devices with their start and end apart: 35 -> 35, of which waited for: 18 -> 18; matrix products, arithmetic and copies ran while one was open for 3% -> 4% of each run, Pallas kernels for 5% -> 6%
where the time goes in v3:
time: 132 us; the launch traced here: 131 us
  starting transfers between devices  63.9 us (48%)
  waiting for transfers between devices  44.6 us (34%)
  Pallas kernels  12 us (9%)
  other arithmetic  7.08 us (5%)
  local copies, waits for them, and re-layouts  2.8 us (2%)
    ppermute x33, starting transfers between devices, swap(): lax.ppermute(value, 'expert', [(i, i ^ by * STRIDE[along]) for i in range...  48.3 us
    ppermute x33, waiting for transfers between devices, swap(): lax.ppermute(value, 'expert', [(i, i ^ by * STRIDE[along]) for i in range...  42.9 us
    ppermute x1, starting transfers between devices, handed_on(): got_far = lax.ppermute(jnp.where(even, back, forth), 'segment', far)  15.6 us
    pallas_call x1, Pallas kernels, forward(): pl.pallas_call(forward_kernel, out_shape=(out(w_g.shape, BF16), out(w_u.s...  6.32 us
    pallas_call x1, Pallas kernels, backward(): pl.pallas_call(backward_kernel, out_shape=(out((rows, width), F32), sent,...  4.06 us
  transfers between devices with their start and end apart: 35, of which 18 were waited for; matrix products, arithmetic and copies ran while one was open for 4% of the time, Pallas kernels for 6%

profile of v3, /device:TPU:1, one launch (start us, length us, event | category | flops | bytes accessed | tf_op | source)
XLA Modules:
  0.0 131.4 jit_solution(14920487723344344207)
XLA Ops:
  2.2 2.6 %collective-permute-start = (bf16[2,21504]{1,0:T(2,128)(2,1)S(1)}, bf16[2,21504]{1,0:T(2,128)(2,1)S(1)}, u32[]{:S(2)}, u32[]{:S(2)}) collective-permute-start(bf16[2,21504]{1,0:T(2,128)(2,1)S(1)} %pad_maximum_fusion.6), channel_id=1, source_target_pairs={{0,1},{1,0},{2,3},{3,2},{4,5},{5,4},{6,7},{7,6},{8,9},{9,8},{10,11... | collective-permute-start | bytes 258056 | tf_op jit(solution)/shard_map/ppermute | solution.py:22
  4.8 3.0 %collective-permute-start.1 = (bf16[2,21504]{1,0:T(2,128)(2,1)S(1)}, bf16[2,21504]{1,0:T(2,128)(2,1)S(1)}, u32[]{:S(2)}, u32[]{:S(2)}) collective-permute-start(bf16[2,21504]{1,0:T(2,128)(2,1)S(1)} %pad_maximum_fusion.6), channel_id=1, source_target_pairs={{0,2},{1,3},{2,0},{3,1},{4,6},{5,7},{6,4},{7,5},{8,10},{9,11},{10,... | collective-permute-start | bytes 258056 | tf_op jit(solution)/shard_map/ppermute | solution.py:22
  10.3 2.7 %collective-permute-done.2 = bf16[2,21504]{1,0:T(2,128)(2,1)S(1)} collective-permute-done((bf16[2,21504]{1,0:T(2,128)(2,1)S(1)}, bf16[2,21504]{1,0:T(2,128)(2,1)S(1)}, u32[]{:S(2)}, u32[]{:S(2)}) %collective-permute-start.2) | collective-permute-done | bytes 86048 | tf_op jit(solution)/shard_map/ppermute | solution.py:22
  15.6 2.5 %collective-permute-start.4 = (bf16[8,10752]{1,0:T(8,128)(2,1)S(1)}, bf16[8,10752]{1,0:T(8,128)(2,1)S(1)}, u32[]{:S(2)}, u32[]{:S(2)}) collective-permute-start(bf16[8,10752]{1,0:T(8,128)(2,1)S(1)} %get-tuple-element.64), channel_id=1, source_target_pairs={{0,8},{1,9},{2,10},{3,11},{4,12},{5,13},{6,14},{7,15},{8,0},{9,1},... | collective-permute-start | bytes 516104 | tf_op jit(solution)/shard_map/ppermute | solution.py:22
  19.7 2.6 %collective-permute-start.17 = (bf16[8,10752]{1,0:T(8,128)(2,1)S(1)}, bf16[8,10752]{1,0:T(8,128)(2,1)S(1)}, u32[]{:S(2)}, u32[]{:S(2)}) collective-permute-start(bf16[8,10752]{1,0:T(8,128)(2,1)S(1)} %get-tuple-element.65), channel_id=1, source_target_pairs={{0,32},{1,33},{2,34},{3,35},{4,36},{5,37},{6,38},{7,39},{8,40},{9,... | collective-permute-start | bytes 516104 | tf_op jit(solution)/shard_map/ppermute | solution.py:22
  25.9 1.9 %collective-permute-start.7 = (bf16[32,10752]{1,0:T(8,128)(2,1)S(1)}, bf16[32,10752]{1,0:T(8,128)(2,1)}, u32[]{:S(2)}, u32[]{:S(2)}) collective-permute-start(bf16[32,10752]{1,0:T(8,128)(2,1)S(1)} %pad_maximum_fusion.1.refs_0_), channel_id=1, source_target_pairs={{0,48},{1,49},{2,50},{3,51},{4,52},{5,53},{6,54},{7,55},{8,56},{9,... | collective-permute-start | bytes 2064392 | tf_op jit(solution)/shard_map/ppermute | solution.py:22
  28.9 2.6 %collective-permute-start.20 = (bf16[32,10752]{1,0:T(8,128)(2,1)S(1)}, bf16[32,10752]{1,0:T(8,128)(2,1)S(1)}, u32[]{:S(2)}, u32[]{:S(2)}) collective-permute-start(bf16[32,10752]{1,0:T(8,128)(2,1)S(1)} %pad_maximum_fusion.2.refs_0_), channel_id=1, source_target_pairs={{0,12},{1,13},{2,14},{3,15},{4,8},{5,9},{6,10},{7,11},{8,4},{9,5},... | collective-permute-start | bytes 2064392 | tf_op jit(solution)/shard_map/ppermute | solution.py:22
  32.8 8.1 %collective-permute-done.6.one.refs_1_ = bf16[32,10752]{1,0:T(8,128)(2,1)S(1)} collective-permute-done((bf16[32,10752]{1,0:T(8,128)(2,1)S(1)}, bf16[32,10752]{1,0:T(8,128)(2,1)S(1)}, u32[]{:S(2)}, u32[]{:S(2)}) %collective-permute-start.6) | collective-permute-done | bytes 688160 | tf_op jit(solution)/shard_map/ppermute | solution.py:22
  41.0 4.7 %collective-permute-done.7.three.refs_4_ = bf16[32,10752]{1,0:T(8,128)(2,1)} collective-permute-done((bf16[32,10752]{1,0:T(8,128)(2,1)S(1)}, bf16[32,10752]{1,0:T(8,128)(2,1)}, u32[]{:S(2)}, u32[]{:S(2)}) %collective-permute-start.7) | collective-permute-done | bytes 688160 | tf_op jit(solution)/shard_map/ppermute | solution.py:22
  51.5 3.3 %collective-permute-done.8.refs_2_ = bf16[16,10752]{1,0:T(8,128)(2,1)S(1)} collective-permute-done((bf16[16,10752]{1,0:T(8,128)(2,1)S(1)}, bf16[16,10752]{1,0:T(8,128)(2,1)S(1)}, u32[]{:S(2)}, u32[]{:S(2)}) %collective-permute-start.8) | collective-permute-done | bytes 344096 | tf_op jit(solution)/shard_map/ppermute | solution.py:22
  54.8 1.8 %collective-permute-done.9.refs_3_ = bf16[16,10752]{1,0:T(8,128)(2,1)S(1)} collective-permute-done((bf16[16,10752]{1,0:T(8,128)(2,1)S(1)}, bf16[16,10752]{1,0:T(8,128)(2,1)S(1)}, u32[]{:S(2)}, u32[]{:S(2)}) %collective-permute-start.9) | collective-permute-done | bytes 344096 | tf_op jit(solution)/shard_map/ppermute | solution.py:22
  56.6 6.3 %shard_map.122 = (bf16[7168,256]{1,0:T(8,128)(2,1)S(1)}, bf16[7168,256]{1,0:T(8,128)(2,1)S(1)}, bf16[256,7168]{1,0:T(8,128)(2,1)S(1)}, f32[128,256]{1,0:T(8,128)...) custom-call(bf16[32,10752]{1,0:T(8,128)(2,1)S(1)} %pad_maximum_fusio, ...), custom_call_target="tpu_custom_call" | custom-call | flops 10000000000 | bytes 10000000 | tf_op jit(solution)/shard_map/pallas_call | solution.py:183
  63.0 4.1 %shard_map.124 = (f32[32,7168]{1,0:T(8,128)S(1)}, bf16[16,7296]{1,0:T(8,128)(2,1)S(1)}, f32[16,7296]{1,0:T(8,128)S(1)}, bf16[16,7296]{1,0:T(8,128)(2,1)S(1)}, bf...) custom-call(bf16[32,10752]{1,0:T(8,128)(2,1)S(1)} %pad_maximum_fusion.2, ...), custom_call_target="tpu_custom_call" | custom-call | flops 10000000000 | bytes 10000000 | tf_op jit(solution)/shard_map/pallas_call | solution.py:253
  67.2 2.1 %collective-permute-start.11 = (bf16[32,7168]{1,0:T(8,128)(2,1)S(1)}, bf16[32,7168]{1,0:T(8,128)(2,1)S(1)}, u32[]{:S(2)}, u32[]{:S(2)}) collective-permute-start(bf16[32,7168]{1,0:T(8,128)(2,1)S(1)} %get-tuple-element.28), channel_id=1, source_target_pairs={{0,32},{1,33},{2,34},{3,35},{4,36},{5,37},{6,38},{7,39},{8,40},{9,... | collective-permute-start | bytes 1376264 | tf_op jit(solution)/shard_map/ppermute | solution.py:22
  71.1 2.2 %collective-permute-done.23 = bf16[16,7296]{1,0:T(8,128)(2,1)S(1)} collective-permute-done((bf16[16,7296]{1,0:T(8,128)(2,1)S(1)}, bf16[16,7296]{1,0:T(8,128)(2,1)S(1)}, u32[]{:S(2)}, u32[]{:S(2)}) %collective-permute-start.23) | collective-permute-done | bytes 233504 | tf_op jit(solution)/shard_map/ppermute | solution.py:22
  73.6 2.7 %collective-permute-done.25 = bf16[16,7296]{1,0:T(8,128)(2,1)S(1)} collective-permute-done((bf16[16,7296]{1,0:T(8,128)(2,1)S(1)}, bf16[16,7296]{1,0:T(8,128)(2,1)S(1)}, u32[]{:S(2)}, u32[]{:S(2)}) %collective-permute-start.25) | collective-permute-done | bytes 233504 | tf_op jit(solution)/shard_map/ppermute | solution.py:22
  76.6 2.7 %collective-permute-start.26 = (bf16[32,7296]{1,0:T(8,128)(2,1)S(1)}, bf16[32,7296]{1,0:T(8,128)(2,1)S(1)}, u32[]{:S(2)}, u32[]{:S(2)}) collective-permute-start(bf16[32,7296]{1,0:T(8,128)(2,1)S(1)} %pad_maximum_fusion.3), channel_id=1, source_target_pairs={{0,12},{1,13},{2,14},{3,15},{4,8},{5,9},{6,10},{7,11},{8,4},{9,5},... | collective-permute-start | bytes 1400840 | tf_op jit(solution)/shard_map/ppermute | solution.py:22
  79.2 5.5 %collective-permute-done.11 = bf16[32,7168]{1,0:T(8,128)(2,1)S(1)} collective-permute-done((bf16[32,7168]{1,0:T(8,128)(2,1)S(1)}, bf16[32,7168]{1,0:T(8,128)(2,1)S(1)}, u32[]{:S(2)}, u32[]{:S(2)}) %collective-permute-start.11) | collective-permute-done | bytes 458784 | tf_op jit(solution)/shard_map/ppermute | solution.py:22
  84.9 2.6 %collective-permute-start.13 = (bf16[8,7168]{1,0:T(8,128)(2,1)S(1)}, bf16[8,7168]{1,0:T(8,128)(2,1)S(1)}, u32[]{:S(2)}, u32[]{:S(2)}) collective-permute-start(bf16[8,7168]{1,0:T(8,128)(2,1)S(1)} %get-tuple-element.61), channel_id=1, source_target_pairs={{0,4},{1,5},{2,6},{3,7},{4,0},{5,1},{6,2},{7,3},{8,12},{9,13},{10,... | collective-permute-start | bytes 344072 | tf_op jit(solution)/shard_map/ppermute | solution.py:22
  87.5 5.3 %collective-permute-start.14 = (bf16[8,7168]{1,0:T(8,128)(2,1)S(1)}, bf16[8,7168]{1,0:T(8,128)(2,1)S(1)}, u32[]{:S(2)}, u32[]{:S(2)}) collective-permute-start(bf16[8,7168]{1,0:T(8,128)(2,1)S(1)} %get-tuple-element.63), channel_id=1, source_target_pairs={{0,8},{1,9},{2,10},{3,11},{4,12},{5,13},{6,14},{7,15},{8,0},{9,1},... | collective-permute-start | bytes 344072 | tf_op jit(solution)/shard_map/ppermute | solution.py:22
  94.0 3.6 %collective-permute-start.29 = (bf16[8,7296]{1,0:T(8,128)(2,1)S(1)}, bf16[8,7296]{1,0:T(8,128)(2,1)S(1)}, u32[]{:S(2)}, u32[]{:S(2)}) collective-permute-start(bf16[8,7296]{1,0:T(8,128)(2,1)S(1)} %get-tuple-element.56), channel_id=1, source_target_pairs={{0,48},{1,49},{2,50},{3,51},{4,52},{5,53},{6,54},{7,55},{8,56},{9,... | collective-permute-start | bytes 350216 | tf_op jit(solution)/shard_map/ppermute | solution.py:22
  101.0 4.5 %collective-permute-start.30 = (f32[2,14464]{1,0:T(2,128)S(1)}, f32[2,14464]{1,0:T(2,128)S(1)}, u32[]{:S(2)}, u32[]{:S(2)}) collective-permute-start(f32[2,14464]{1,0:T(2,128)S(1)} %get-tuple-element.58), channel_id=1, source_target_pairs={{0,1},{1,0},{2,3},{3,2},{4,5},{5,4},{6,7},{7,6},{8,9},{9,8},{10,11... | collective-permute-start | bytes 347144 | tf_op jit(solution)/shard_map/ppermute | solution.py:22
  108.0 4.5 %collective-permute-done.31 = f32[2,14464]{1,0:T(2,128)S(1)} collective-permute-done((f32[2,14464]{1,0:T(2,128)S(1)}, f32[2,14464]{1,0:T(2,128)S(1)}, u32[]{:S(2)}, u32[]{:S(2)}) %collective-permute-start.31) | collective-permute-done | bytes 115744 | tf_op jit(solution)/shard_map/ppermute | solution.py:22
  112.8 15.6 %collective-permute-start.33 = (bf16[2,7168]{1,0:T(2,128)(2,1)S(1)}, bf16[2,7168]{1,0:T(2,128)(2,1)S(1)}, u32[]{:S(2)}, u32[]{:S(2)}) collective-permute-start(bf16[2,7168]{1,0:T(2,128)(2,1)S(1)} %get-tuple-element.69), channel_id=1, source_target_pairs={{0,192},{64,128},{128,64},{192,0},{1,193},{65,129},{129,65},{193,1... | collective-permute-start | bytes 86024 | tf_op jit(solution)/shard_map/ppermute | solution.py:37
  (113 shorter events, 33.0 us)
Async XLA Ops:
  2.2 7.1 %collective-permute-start = (bf16[2,21504]{1,0:T(2,128)(2,1)S(1)}, bf16[2,21504]{1,0:T(2,128)(2,1)S(1)}, u32[]{:S(2)}, u32[]{:S(2)}) collective-permute-start(bf16[2,21504]{1,0:T(2,128)(2,1)S(1)} %pad_maximum_fusion.6), channel_id=1, source_target_pairs={{0,1},{1,0},{2,3},{3,2},{4,5},{5,4},{6,7},{7,6},{8,9},{9,8},{10,11... | collective-permute-start | bytes 258056 | tf_op jit(solution)/shard_map/ppermute | solution.py:22
  14.3 8.1 %collective-permute-start.3 = (bf16[8,10752]{1,0:T(8,128)(2,1)S(1)}, bf16[8,10752]{1,0:T(8,128)(2,1)S(1)}, u32[]{:S(2)}, u32[]{:S(2)}) collective-permute-start(bf16[8,10752]{1,0:T(8,128)(2,1)S(1)} %get-tuple-element.64), channel_id=1, source_target_pairs={{0,4},{1,5},{2,6},{3,7},{4,0},{5,1},{6,2},{7,3},{8,12},{9,13},{10,... | collective-permute-start | bytes 516104 | tf_op jit(solution)/shard_map/ppermute | solution.py:22
  15.6 7.5 %collective-permute-start.4 = (bf16[8,10752]{1,0:T(8,128)(2,1)S(1)}, bf16[8,10752]{1,0:T(8,128)(2,1)S(1)}, u32[]{:S(2)}, u32[]{:S(2)}) collective-permute-start(bf16[8,10752]{1,0:T(8,128)(2,1)S(1)} %get-tuple-element.64), channel_id=1, source_target_pairs={{0,8},{1,9},{2,10},{3,11},{4,12},{5,13},{6,14},{7,15},{8,0},{9,1},... | collective-permute-start | bytes 516104 | tf_op jit(solution)/shard_map/ppermute | solution.py:22
  18.3 9.5 %collective-permute-start.16 = (bf16[8,10752]{1,0:T(8,128)(2,1)S(1)}, bf16[8,10752]{1,0:T(8,128)(2,1)S(1)}, u32[]{:S(2)}, u32[]{:S(2)}) collective-permute-start(bf16[8,10752]{1,0:T(8,128)(2,1)S(1)} %get-tuple-element.65), channel_id=1, source_target_pairs={{0,16},{1,17},{2,18},{3,19},{4,20},{5,21},{6,22},{7,23},{8,24},{9,... | collective-permute-start | bytes 516104 | tf_op jit(solution)/shard_map/ppermute | solution.py:22
  19.7 8.1 %collective-permute-start.17 = (bf16[8,10752]{1,0:T(8,128)(2,1)S(1)}, bf16[8,10752]{1,0:T(8,128)(2,1)S(1)}, u32[]{:S(2)}, u32[]{:S(2)}) collective-permute-start(bf16[8,10752]{1,0:T(8,128)(2,1)S(1)} %get-tuple-element.65), channel_id=1, source_target_pairs={{0,32},{1,33},{2,34},{3,35},{4,36},{5,37},{6,38},{7,39},{8,40},{9,... | collective-permute-start | bytes 516104 | tf_op jit(solution)/shard_map/ppermute | solution.py:22
  24.5 16.4 %collective-permute-start.6 = (bf16[32,10752]{1,0:T(8,128)(2,1)S(1)}, bf16[32,10752]{1,0:T(8,128)(2,1)S(1)}, u32[]{:S(2)}, u32[]{:S(2)}) collective-permute-start(bf16[32,10752]{1,0:T(8,128)(2,1)S(1)} %pad_maximum_fusion.1.refs_0_), channel_id=1, source_target_pairs={{0,16},{1,17},{2,18},{3,19},{4,20},{5,21},{6,22},{7,23},{8,24},{9,... | collective-permute-start | bytes 2064392 | tf_op jit(solution)/shard_map/ppermute | solution.py:22
  25.9 19.7 %collective-permute-start.7 = (bf16[32,10752]{1,0:T(8,128)(2,1)S(1)}, bf16[32,10752]{1,0:T(8,128)(2,1)}, u32[]{:S(2)}, u32[]{:S(2)}) collective-permute-start(bf16[32,10752]{1,0:T(8,128)(2,1)S(1)} %pad_maximum_fusion.1.refs_0_), channel_id=1, source_target_pairs={{0,48},{1,49},{2,50},{3,51},{4,52},{5,53},{6,54},{7,55},{8,56},{9,... | collective-permute-start | bytes 2064392 | tf_op jit(solution)/shard_map/ppermute | solution.py:22
  28.8 19.8 %collective-permute-start.19 = (bf16[32,10752]{1,0:T(8,128)(2,1)S(1)}, bf16[32,10752]{1,0:T(8,128)(2,1)S(1)}, u32[]{:S(2)}, u32[]{:S(2)}) collective-permute-start(bf16[32,10752]{1,0:T(8,128)(2,1)S(1)} %pad_maximum_fusion.2.refs_0_), channel_id=1, source_target_pairs={{0,4},{1,5},{2,6},{3,7},{4,0},{5,1},{6,2},{7,3},{8,12},{9,13},{10,... | collective-permute-start | bytes 2064392 | tf_op jit(solution)/shard_map/ppermute | solution.py:22
  28.9 19.7 %collective-permute-start.20 = (bf16[32,10752]{1,0:T(8,128)(2,1)S(1)}, bf16[32,10752]{1,0:T(8,128)(2,1)S(1)}, u32[]{:S(2)}, u32[]{:S(2)}) collective-permute-start(bf16[32,10752]{1,0:T(8,128)(2,1)S(1)} %pad_maximum_fusion.2.refs_0_), channel_id=1, source_target_pairs={{0,12},{1,13},{2,14},{3,15},{4,8},{5,9},{6,10},{7,11},{8,4},{9,5},... | collective-permute-start | bytes 2064392 | tf_op jit(solution)/shard_map/ppermute | solution.py:22
  47.9 6.9 %collective-permute-start.8 = (bf16[16,10752]{1,0:T(8,128)(2,1)S(1)}, bf16[16,10752]{1,0:T(8,128)(2,1)S(1)}, u32[]{:S(2)}, u32[]{:S(2)}) collective-permute-start(bf16[16,10752]{1,0:T(8,128)(2,1)S(1)} %get-tuple-element.24), channel_id=1, source_target_pairs={{0,16},{1,17},{2,18},{3,19},{4,20},{5,21},{6,22},{7,23},{8,24},{9,... | collective-permute-start | bytes 1032200 | tf_op jit(solution)/shard_map/ppermute | solution.py:22
  48.4 8.2 %collective-permute-start.9 = (bf16[16,10752]{1,0:T(8,128)(2,1)S(1)}, bf16[16,10752]{1,0:T(8,128)(2,1)S(1)}, u32[]{:S(2)}, u32[]{:S(2)}) collective-permute-start(bf16[16,10752]{1,0:T(8,128)(2,1)S(1)} %get-tuple-element.25), channel_id=1, source_target_pairs={{0,48},{1,49},{2,50},{3,51},{4,52},{5,53},{6,54},{7,55},{8,56},{9,... | collective-permute-start | bytes 1032200 | tf_op jit(solution)/shard_map/ppermute | solution.py:22
  48.9 14.0 %collective-permute-start.21 = (bf16[16,10752]{1,0:T(8,128)(2,1)S(1)}, bf16[16,10752]{1,0:T(8,128)(2,1)S(1)}, u32[]{:S(2)}, u32[]{:S(2)}) collective-permute-start(bf16[16,10752]{1,0:T(8,128)(2,1)S(1)} %get-tuple-element.30), channel_id=1, source_target_pairs={{0,4},{1,5},{2,6},{3,7},{4,0},{5,1},{6,2},{7,3},{8,12},{9,13},{10,... | collective-permute-start | bytes 1032200 | tf_op jit(solution)/shard_map/ppermute | solution.py:22
  50.7 12.3 %collective-permute-start.22 = (bf16[16,10752]{1,0:T(8,128)(2,1)S(1)}, bf16[16,10752]{1,0:T(8,128)(2,1)S(1)}, u32[]{:S(2)}, u32[]{:S(2)}) collective-permute-start(bf16[16,10752]{1,0:T(8,128)(2,1)S(1)} %get-tuple-element.31), channel_id=1, source_target_pairs={{0,12},{1,13},{2,14},{3,15},{4,8},{5,9},{6,10},{7,11},{8,4},{9,5},... | collective-permute-start | bytes 1032200 | tf_op jit(solution)/shard_map/ppermute | solution.py:22
  67.1 12.1 %collective-permute-start.10 = (bf16[32,7168]{1,0:T(8,128)(2,1)S(1)}, bf16[32,7168]{1,0:T(8,128)(2,1)S(1)}, u32[]{:S(2)}, u32[]{:S(2)}) collective-permute-start(bf16[32,7168]{1,0:T(8,128)(2,1)S(1)} %get-tuple-element.27), channel_id=1, source_target_pairs={{0,16},{1,17},{2,18},{3,19},{4,20},{5,21},{6,22},{7,23},{8,24},{9,... | collective-permute-start | bytes 1376264 | tf_op jit(solution)/shard_map/ppermute | solution.py:22
  67.2 17.5 %collective-permute-start.11 = (bf16[32,7168]{1,0:T(8,128)(2,1)S(1)}, bf16[32,7168]{1,0:T(8,128)(2,1)S(1)}, u32[]{:S(2)}, u32[]{:S(2)}) collective-permute-start(bf16[32,7168]{1,0:T(8,128)(2,1)S(1)} %get-tuple-element.28), channel_id=1, source_target_pairs={{0,32},{1,33},{2,34},{3,35},{4,36},{5,37},{6,38},{7,39},{8,40},{9,... | collective-permute-start | bytes 1376264 | tf_op jit(solution)/shard_map/ppermute | solution.py:22
  69.3 15.4 %collective-permute-start.12 = (bf16[32,7168]{1,0:T(8,128)(2,1)S(1)}, bf16[32,7168]{1,0:T(8,128)(2,1)S(1)}, u32[]{:S(2)}, u32[]{:S(2)}) collective-permute-start(bf16[32,7168]{1,0:T(8,128)(2,1)S(1)} %get-tuple-element.29), channel_id=1, source_target_pairs={{0,48},{1,49},{2,50},{3,51},{4,52},{5,53},{6,54},{7,55},{8,56},{9,... | collective-permute-start | bytes 1376264 | tf_op jit(solution)/shard_map/ppermute | solution.py:22
  73.5 19.3 %collective-permute-start.24 = (bf16[32,7296]{1,0:T(8,128)(2,1)S(1)}, bf16[32,7296]{1,0:T(8,128)(2,1)S(1)}, u32[]{:S(2)}, u32[]{:S(2)}) collective-permute-start(bf16[32,7296]{1,0:T(8,128)(2,1)S(1)} %maximum_maximum_fusion), channel_id=1, source_target_pairs={{0,4},{1,5},{2,6},{3,7},{4,0},{5,1},{6,2},{7,3},{8,12},{9,13},{10,... | collective-permute-start | bytes 1400840 | tf_op jit(solution)/shard_map/ppermute | solution.py:22
  76.6 16.4 %collective-permute-start.26 = (bf16[32,7296]{1,0:T(8,128)(2,1)S(1)}, bf16[32,7296]{1,0:T(8,128)(2,1)S(1)}, u32[]{:S(2)}, u32[]{:S(2)}) collective-permute-start(bf16[32,7296]{1,0:T(8,128)(2,1)S(1)} %pad_maximum_fusion.3), channel_id=1, source_target_pairs={{0,12},{1,13},{2,14},{3,15},{4,8},{5,9},{6,10},{7,11},{8,4},{9,5},... | collective-permute-start | bytes 1400840 | tf_op jit(solution)/shard_map/ppermute | solution.py:22
  84.9 9.0 %collective-permute-start.13 = (bf16[8,7168]{1,0:T(8,128)(2,1)S(1)}, bf16[8,7168]{1,0:T(8,128)(2,1)S(1)}, u32[]{:S(2)}, u32[]{:S(2)}) collective-permute-start(bf16[8,7168]{1,0:T(8,128)(2,1)S(1)} %get-tuple-element.61), channel_id=1, source_target_pairs={{0,4},{1,5},{2,6},{3,7},{4,0},{5,1},{6,2},{7,3},{8,12},{9,13},{10,... | collective-permute-start | bytes 344072 | tf_op jit(solution)/shard_map/ppermute | solution.py:22
  87.5 10.1 %collective-permute-start.14 = (bf16[8,7168]{1,0:T(8,128)(2,1)S(1)}, bf16[8,7168]{1,0:T(8,128)(2,1)S(1)}, u32[]{:S(2)}, u32[]{:S(2)}) collective-permute-start(bf16[8,7168]{1,0:T(8,128)(2,1)S(1)} %get-tuple-element.63), channel_id=1, source_target_pairs={{0,8},{1,9},{2,10},{3,11},{4,12},{5,13},{6,14},{7,15},{8,0},{9,1},... | collective-permute-start | bytes 344072 | tf_op jit(solution)/shard_map/ppermute | solution.py:22
  101.0 7.0 %collective-permute-start.30 = (f32[2,14464]{1,0:T(2,128)S(1)}, f32[2,14464]{1,0:T(2,128)S(1)}, u32[]{:S(2)}, u32[]{:S(2)}) collective-permute-start(f32[2,14464]{1,0:T(2,128)S(1)} %get-tuple-element.58), channel_id=1, source_target_pairs={{0,1},{1,0},{2,3},{3,2},{4,5},{5,4},{6,7},{7,6},{8,9},{9,8},{10,11... | collective-permute-start | bytes 347144 | tf_op jit(solution)/shard_map/ppermute | solution.py:22
  105.5 7.0 %collective-permute-start.31 = (f32[2,14464]{1,0:T(2,128)S(1)}, f32[2,14464]{1,0:T(2,128)S(1)}, u32[]{:S(2)}, u32[]{:S(2)}) collective-permute-start(f32[2,14464]{1,0:T(2,128)S(1)} %get-tuple-element.60), channel_id=1, source_target_pairs={{0,2},{1,3},{2,0},{3,1},{4,6},{5,7},{6,4},{7,5},{8,10},{9,11},{10,... | collective-permute-start | bytes 347144 | tf_op jit(solution)/shard_map/ppermute | solution.py:22
  105.9 6.6 %collective-permute-start.32 = (f32[2,14464]{1,0:T(2,128)S(1)}, f32[2,14464]{1,0:T(2,128)S(1)}, u32[]{:S(2)}, u32[]{:S(2)}) collective-permute-start(f32[2,14464]{1,0:T(2,128)S(1)} %get-tuple-element.59), channel_id=1, source_target_pairs={{0,3},{1,2},{2,1},{3,0},{4,7},{5,6},{6,5},{7,4},{8,11},{9,10},{10,... | collective-permute-start | bytes 347144 | tf_op jit(solution)/shard_map/ppermute | solution.py:22
  112.8 17.9 %collective-permute-start.33 = (bf16[2,7168]{1,0:T(2,128)(2,1)S(1)}, bf16[2,7168]{1,0:T(2,128)(2,1)S(1)}, u32[]{:S(2)}, u32[]{:S(2)}) collective-permute-start(bf16[2,7168]{1,0:T(2,128)(2,1)S(1)} %get-tuple-element.69), channel_id=1, source_target_pairs={{0,192},{64,128},{128,64},{192,0},{1,193},{65,129},{129,65},{193,1... | collective-permute-start | bytes 86024 | tf_op jit(solution)/shard_map/ppermute | solution.py:37
  (17 other events, 120.9 us)

commit v4 on v2

--- a/solution.py
+++ b/solution.py
@@ -303,8 +303,6 @@
     ) = forward(a_parts, tab_f, w_gate[0], w_up[0], w_down[0])
     b_own, b_one, b_two, b_three, p_own = backward(b_parts, gate_b, up_b, tab_b, w_g, w_u, w_d)
 
-    f_two_lo, f_two_hi = after(f_two_lo, b_own), after(f_two_hi, b_own)
-
     f_three_lo = (f_three_lo + swap(f_two_lo, "y", 1).astype(F32)).astype(BF16)
     f_one_hi = (f_one_hi + swap(f_two_hi, "y", 3).astype(F32)).astype(BF16)
     sum_f = (
@@ -321,7 +319,7 @@
     sum_f = scattered(*cut(sum_f, BF16), "x")
     both = scattered(*cut(jnp.concatenate([sum_b, coded(sum_p)], axis=1), BF16), "y")
     sum_b, sum_p = both[:, :width], decoded(both[:, width:])
-    last = scattered(*cut(jnp.concatenate([sum_f, sum_b, coded(sum_p)], axis=1), F32), "z")
+    last = scattered(*cut(jnp.concatenate([sum_f, sum_b, coded(sum_p)], axis=1), BF16), "z")
 
     layer_out = (x_fwd.astype(F32) + last[:, :width]).astype(BF16)
     input_grad = (grad_out.astype(F32) + last[:, width : 2 * width]).astype(BF16)

time: 131 us -> 131 us (level)
  waiting for transfers between devices: 45.4 us -> 43 us
  starting transfers between devices: 61.9 us -> 63.3 us
    ppermute x33, waiting for transfers between devices: 44.4 us -> 42 us  [swap(): lax.ppermute(value, 'expert', [(i, i ^ by * STRIDE[along]) for i in range...]
    ppermute x33, starting transfers between devices: 46.9 us -> 48.8 us  [swap(): lax.ppermute(value, 'expert', [(i, i ^ by * STRIDE[along]) for i in range...]
  transfers between devices with their start and end apart: 35 -> 35, of which waited for: 18 -> 17; matrix products, arithmetic and copies ran while one was open for 3% -> 3% of each run, Pallas kernels for 5% -> 10%
where the time goes in v4:
time: 131 us
  starting transfers between devices  63.3 us (48%)
  waiting for transfers between devices  43 us (33%)
  Pallas kernels  13.1 us (10%)
  other arithmetic  6.71 us (5%)
  local copies, waits for them, and re-layouts  3.67 us (3%)
    ppermute x33, starting transfers between devices, swap(): lax.ppermute(value, 'expert', [(i, i ^ by * STRIDE[along]) for i in range...  48.8 us
    ppermute x33, waiting for transfers between devices, swap(): lax.ppermute(value, 'expert', [(i, i ^ by * STRIDE[along]) for i in range...  42 us
    ppermute x1, starting transfers between devices, handed_on(): got_far = lax.ppermute(jnp.where(even, back, forth), 'segment', far)  14.5 us
    pallas_call x1, Pallas kernels, forward(): pl.pallas_call(forward_kernel, out_shape=(out(w_g.shape, BF16), out(w_u.s...  6.53 us
    pallas_call x1, Pallas kernels, backward(): pl.pallas_call(backward_kernel, out_shape=(out((rows, width), F32), sent,...  4.06 us
  transfers between devices with their start and end apart: 35, of which 17 were waited for; matrix products, arithmetic and copies ran while one was open for 3% of the time, Pallas kernels for 10%

profile of v4, /device:TPU:1, one launch (start us, length us, event | category | flops | bytes accessed | tf_op | source)
XLA Modules:
  0.0 130.7 jit_solution(9250410428484318022)
XLA Ops:
  2.2 2.6 %collective-permute-start = (bf16[2,21504]{1,0:T(2,128)(2,1)S(1)}, bf16[2,21504]{1,0:T(2,128)(2,1)S(1)}, u32[]{:S(2)}, u32[]{:S(2)}) collective-permute-start(bf16[2,21504]{1,0:T(2,128)(2,1)S(1)} %pad_maximum_fusion.7), channel_id=1, source_target_pairs={{0,1},{1,0},{2,3},{3,2},{4,5},{5,4},{6,7},{7,6},{8,9},{9,8},{10,11... | collective-permute-start | bytes 258056 | tf_op jit(solution)/shard_map/ppermute | solution.py:22
  4.8 3.0 %collective-permute-start.1 = (bf16[2,21504]{1,0:T(2,128)(2,1)S(1)}, bf16[2,21504]{1,0:T(2,128)(2,1)S(1)}, u32[]{:S(2)}, u32[]{:S(2)}) collective-permute-start(bf16[2,21504]{1,0:T(2,128)(2,1)S(1)} %pad_maximum_fusion.7), channel_id=1, source_target_pairs={{0,2},{1,3},{2,0},{3,1},{4,6},{5,7},{6,4},{7,5},{8,10},{9,11},{10,... | collective-permute-start | bytes 258056 | tf_op jit(solution)/shard_map/ppermute | solution.py:22
  10.3 2.7 %collective-permute-done.2 = bf16[2,21504]{1,0:T(2,128)(2,1)S(1)} collective-permute-done((bf16[2,21504]{1,0:T(2,128)(2,1)S(1)}, bf16[2,21504]{1,0:T(2,128)(2,1)S(1)}, u32[]{:S(2)}, u32[]{:S(2)}) %collective-permute-start.2) | collective-permute-done | bytes 86048 | tf_op jit(solution)/shard_map/ppermute | solution.py:22
  15.6 2.5 %collective-permute-start.4 = (bf16[8,10752]{1,0:T(8,128)(2,1)S(1)}, bf16[8,10752]{1,0:T(8,128)(2,1)S(1)}, u32[]{:S(2)}, u32[]{:S(2)}) collective-permute-start(bf16[8,10752]{1,0:T(8,128)(2,1)S(1)} %get-tuple-element.59), channel_id=1, source_target_pairs={{0,8},{1,9},{2,10},{3,11},{4,12},{5,13},{6,14},{7,15},{8,0},{9,1},... | collective-permute-start | bytes 516104 | tf_op jit(solution)/shard_map/ppermute | solution.py:22
  19.7 2.6 %collective-permute-start.18 = (bf16[8,10752]{1,0:T(8,128)(2,1)S(1)}, bf16[8,10752]{1,0:T(8,128)(2,1)S(1)}, u32[]{:S(2)}, u32[]{:S(2)}) collective-permute-start(bf16[8,10752]{1,0:T(8,128)(2,1)S(1)} %get-tuple-element.60), channel_id=1, source_target_pairs={{0,32},{1,33},{2,34},{3,35},{4,36},{5,37},{6,38},{7,39},{8,40},{9,... | collective-permute-start | bytes 516104 | tf_op jit(solution)/shard_map/ppermute | solution.py:22
  25.9 1.9 %collective-permute-start.7 = (bf16[32,10752]{1,0:T(8,128)(2,1)S(1)}, bf16[32,10752]{1,0:T(8,128)(2,1)}, u32[]{:S(2)}, u32[]{:S(2)}) collective-permute-start(bf16[32,10752]{1,0:T(8,128)(2,1)S(1)} %pad_maximum_fusion.1.refs_0_), channel_id=1, source_target_pairs={{0,48},{1,49},{2,50},{3,51},{4,52},{5,53},{6,54},{7,55},{8,56},{9,... | collective-permute-start | bytes 2064392 | tf_op jit(solution)/shard_map/ppermute | solution.py:22
  28.9 2.6 %collective-permute-start.21 = (bf16[32,10752]{1,0:T(8,128)(2,1)S(1)}, bf16[32,10752]{1,0:T(8,128)(2,1)S(1)}, u32[]{:S(2)}, u32[]{:S(2)}) collective-permute-start(bf16[32,10752]{1,0:T(8,128)(2,1)S(1)} %pad_maximum_fusion.2.refs_0_), channel_id=1, source_target_pairs={{0,12},{1,13},{2,14},{3,15},{4,8},{5,9},{6,10},{7,11},{8,4},{9,5},... | collective-permute-start | bytes 2064392 | tf_op jit(solution)/shard_map/ppermute | solution.py:22
  32.9 8.1 %collective-permute-done.6.one.refs_1_ = bf16[32,10752]{1,0:T(8,128)(2,1)S(1)} collective-permute-done((bf16[32,10752]{1,0:T(8,128)(2,1)S(1)}, bf16[32,10752]{1,0:T(8,128)(2,1)S(1)}, u32[]{:S(2)}, u32[]{:S(2)}) %collective-permute-start.6) | collective-permute-done | bytes 688160 | tf_op jit(solution)/shard_map/ppermute | solution.py:22
  41.0 4.7 %collective-permute-done.7.three.refs_4_ = bf16[32,10752]{1,0:T(8,128)(2,1)} collective-permute-done((bf16[32,10752]{1,0:T(8,128)(2,1)S(1)}, bf16[32,10752]{1,0:T(8,128)(2,1)}, u32[]{:S(2)}, u32[]{:S(2)}) %collective-permute-start.7) | collective-permute-done | bytes 688160 | tf_op jit(solution)/shard_map/ppermute | solution.py:22
  46.5 2.2 %shard_map.121 = (bf16[16,10752]{1,0:T(8,128)(2,1)}, bf16[16,10752]{1,0:T(8,128)(2,1)}) custom-call(bf16[32,10752]{1,0:T(8,128)(2,1)} %collective-permute-done.7.three.refs_4_, bf16[32,10752]{1,0:T(8,128)(2,1)S(1)} %collective-permute-done.6.one.refs_1_, f32[128,1]{1,0:T(8,128)S(1)} %copy-done, f32[128,9]{1,0:T(8,128)S(1)} %copy.25.__.refs_7_), custom_call_target="tpu_custom_call" | custom-call | flops 1 | bytes 1000000 | tf_op jit(solution)/shard_map/pallas_call | solution.py:124
  53.1 2.8 %collective-permute-done.8.refs_2_ = bf16[16,10752]{1,0:T(8,128)(2,1)} collective-permute-done((bf16[16,10752]{1,0:T(8,128)(2,1)}, bf16[16,10752]{1,0:T(8,128)(2,1)}, u32[]{:S(2)}, u32[]{:S(2)}) %collective-permute-start.8) | collective-permute-done | bytes 344096 | tf_op jit(solution)/shard_map/ppermute | solution.py:22
  55.9 1.8 %collective-permute-done.9.refs_3_ = bf16[16,10752]{1,0:T(8,128)(2,1)} collective-permute-done((bf16[16,10752]{1,0:T(8,128)(2,1)}, bf16[16,10752]{1,0:T(8,128)(2,1)}, u32[]{:S(2)}, u32[]{:S(2)}) %collective-permute-start.9) | collective-permute-done | bytes 344096 | tf_op jit(solution)/shard_map/ppermute | solution.py:22
  57.7 6.5 %shard_map.122 = (bf16[7168,256]{1,0:T(8,128)(2,1)S(1)}, bf16[7168,256]{1,0:T(8,128)(2,1)S(1)}, bf16[256,7168]{1,0:T(8,128)(2,1)S(1)}, f32[128,256]{1,0:T(8,128)...) custom-call(bf16[32,10752]{1,0:T(8,128)(2,1)S(1)} %pad_maximum_fusio, ...), custom_call_target="tpu_custom_call" | custom-call | flops 10000000000 | bytes 10000000 | tf_op jit(solution)/shard_map/pallas_call | solution.py:188
  64.5 4.1 %shard_map.124 = (f32[32,7168]{1,0:T(8,128)S(1)}, bf16[32,7296]{1,0:T(8,128)(2,1)S(1)}, bf16[32,7296]{1,0:T(8,128)(2,1)S(1)}, bf16[32,7296]{1,0:T(8,128)(2,1)S(1)}, f32[32,8]{1,0:T(8,128)S(1)}) custom-call(bf16[32,10752]{1,0:T(8,128)(2,1)S(1)} %pad_maximum_fusion.2.refs_0_, bf16[32,10752]{1,0:T(8,128)(2,1)S(1)} %collective-permute-done.20.one.refs_1_, ...), custom_call_target="tpu_custom_call" | custom-call | flops 10000000000 | bytes 10000000 | tf_op jit(solution)/shard_map/pallas_call | solution.py:259
  68.6 2.0 %collective-permute-start.24 = (bf16[32,7296]{1,0:T(8,128)(2,1)S(1)}, bf16[32,7296]{1,0:T(8,128)(2,1)S(1)}, u32[]{:S(2)}, u32[]{:S(2)}) collective-permute-start(bf16[32,7296]{1,0:T(8,128)(2,1)S(1)} %get-tuple-element.43), channel_id=1, source_target_pairs={{0,4},{1,5},{2,6},{3,7},{4,0},{5,1},{6,2},{7,3},{8,12},{9,13},{10,... | collective-permute-start | bytes 1400840 | tf_op jit(solution)/shard_map/ppermute | solution.py:22
  71.0 2.1 %collective-permute-start.26 = (bf16[32,7296]{1,0:T(8,128)(2,1)S(1)}, bf16[32,7296]{1,0:T(8,128)(2,1)S(1)}, u32[]{:S(2)}, u32[]{:S(2)}) collective-permute-start(bf16[32,7296]{1,0:T(8,128)(2,1)S(1)} %get-tuple-element.45), channel_id=1, source_target_pairs={{0,12},{1,13},{2,14},{3,15},{4,8},{5,9},{6,10},{7,11},{8,4},{9,5},... | collective-permute-start | bytes 1400840 | tf_op jit(solution)/shard_map/ppermute | solution.py:22
  74.8 2.1 %collective-permute-start.13 = (bf16[32,7168]{1,0:T(8,128)(2,1)S(1)}, bf16[32,7168]{1,0:T(8,128)(2,1)S(1)}, u32[]{:S(2)}, u32[]{:S(2)}) collective-permute-start(bf16[32,7168]{1,0:T(8,128)(2,1)S(1)} %pad_maximum_fusion.5), channel_id=1, source_target_pairs={{0,48},{1,49},{2,50},{3,51},{4,52},{5,53},{6,54},{7,55},{8,56},{9,... | collective-permute-start | bytes 1376264 | tf_op jit(solution)/shard_map/ppermute | solution.py:22
  77.9 9.1 %collective-permute-done.25 = bf16[32,7296]{1,0:T(8,128)(2,1)S(1)} collective-permute-done((bf16[32,7296]{1,0:T(8,128)(2,1)S(1)}, bf16[32,7296]{1,0:T(8,128)(2,1)S(1)}, u32[]{:S(2)}, u32[]{:S(2)}) %collective-permute-start.25) | collective-permute-done | bytes 466976 | tf_op jit(solution)/shard_map/ppermute | solution.py:22
  89.3 2.8 %collective-permute-start.15 = (bf16[8,7168]{1,0:T(8,128)(2,1)S(1)}, bf16[8,7168]{1,0:T(8,128)(2,1)S(1)}, u32[]{:S(2)}, u32[]{:S(2)}) collective-permute-start(bf16[8,7168]{1,0:T(8,128)(2,1)S(1)} %get-tuple-element.58), channel_id=1, source_target_pairs={{0,8},{1,9},{2,10},{3,11},{4,12},{5,13},{6,14},{7,15},{8,0},{9,1},... | collective-permute-start | bytes 344072 | tf_op jit(solution)/shard_map/ppermute | solution.py:22
  97.1 2.0 %collective-permute-done.28 = bf16[8,7296]{1,0:T(8,128)(2,1)S(1)} collective-permute-done((bf16[8,7296]{1,0:T(8,128)(2,1)S(1)}, bf16[8,7296]{1,0:T(8,128)(2,1)S(1)}, u32[]{:S(2)}, u32[]{:S(2)}) %collective-permute-start.28) | collective-permute-done | bytes 116768 | tf_op jit(solution)/shard_map/ppermute | solution.py:22
  101.0 6.7 %collective-permute-start.30 = (bf16[2,14464]{1,0:T(2,128)(2,1)S(1)}, bf16[2,14464]{1,0:T(2,128)(2,1)S(1)}, u32[]{:S(2)}, u32[]{:S(2)}) collective-permute-start(bf16[2,14464]{1,0:T(2,128)(2,1)S(1)} %get-tuple-element.63), channel_id=1, source_target_pairs={{0,1},{1,0},{2,3},{3,2},{4,5},{5,4},{6,7},{7,6},{8,9},{9,8},{10,11... | collective-permute-start | bytes 173576 | tf_op jit(solution)/shard_map/ppermute | solution.py:22
  110.1 1.9 %collective-permute-done.31 = bf16[2,14464]{1,0:T(2,128)(2,1)S(1)} collective-permute-done((bf16[2,14464]{1,0:T(2,128)(2,1)S(1)}, bf16[2,14464]{1,0:T(2,128)(2,1)S(1)}, u32[]{:S(2)}, u32[]{:S(2)}) %collective-permute-start.31) | collective-permute-done | bytes 57888 | tf_op jit(solution)/shard_map/ppermute | solution.py:22
  112.0 1.8 %collective-permute-done.32 = bf16[2,14464]{1,0:T(2,128)(2,1)S(1)} collective-permute-done((bf16[2,14464]{1,0:T(2,128)(2,1)S(1)}, bf16[2,14464]{1,0:T(2,128)(2,1)S(1)}, u32[]{:S(2)}, u32[]{:S(2)}) %collective-permute-start.32) | collective-permute-done | bytes 57888 | tf_op jit(solution)/shard_map/ppermute | solution.py:22
  114.0 14.5 %collective-permute-start.33 = (bf16[2,7168]{1,0:T(2,128)(2,1)S(1)}, bf16[2,7168]{1,0:T(2,128)(2,1)S(1)}, u32[]{:S(2)}, u32[]{:S(2)}) collective-permute-start(bf16[2,7168]{1,0:T(2,128)(2,1)S(1)} %get-tuple-element.67), channel_id=1, source_target_pairs={{0,192},{64,128},{128,64},{192,0},{1,193},{65,129},{129,65},{193,1... | collective-permute-start | bytes 86024 | tf_op jit(solution)/shard_map/ppermute | solution.py:37
  (109 shorter events, 36.6 us)
Async XLA Ops:
  2.2 7.1 %collective-permute-start = (bf16[2,21504]{1,0:T(2,128)(2,1)S(1)}, bf16[2,21504]{1,0:T(2,128)(2,1)S(1)}, u32[]{:S(2)}, u32[]{:S(2)}) collective-permute-start(bf16[2,21504]{1,0:T(2,128)(2,1)S(1)} %pad_maximum_fusion.7), channel_id=1, source_target_pairs={{0,1},{1,0},{2,3},{3,2},{4,5},{5,4},{6,7},{7,6},{8,9},{9,8},{10,11... | collective-permute-start | bytes 258056 | tf_op jit(solution)/shard_map/ppermute | solution.py:22
  14.3 8.1 %collective-permute-start.3 = (bf16[8,10752]{1,0:T(8,128)(2,1)S(1)}, bf16[8,10752]{1,0:T(8,128)(2,1)S(1)}, u32[]{:S(2)}, u32[]{:S(2)}) collective-permute-start(bf16[8,10752]{1,0:T(8,128)(2,1)S(1)} %get-tuple-element.59), channel_id=1, source_target_pairs={{0,4},{1,5},{2,6},{3,7},{4,0},{5,1},{6,2},{7,3},{8,12},{9,13},{10,... | collective-permute-start | bytes 516104 | tf_op jit(solution)/shard_map/ppermute | solution.py:22
  15.6 7.5 %collective-permute-start.4 = (bf16[8,10752]{1,0:T(8,128)(2,1)S(1)}, bf16[8,10752]{1,0:T(8,128)(2,1)S(1)}, u32[]{:S(2)}, u32[]{:S(2)}) collective-permute-start(bf16[8,10752]{1,0:T(8,128)(2,1)S(1)} %get-tuple-element.59), channel_id=1, source_target_pairs={{0,8},{1,9},{2,10},{3,11},{4,12},{5,13},{6,14},{7,15},{8,0},{9,1},... | collective-permute-start | bytes 516104 | tf_op jit(solution)/shard_map/ppermute | solution.py:22
  18.3 9.5 %collective-permute-start.17 = (bf16[8,10752]{1,0:T(8,128)(2,1)S(1)}, bf16[8,10752]{1,0:T(8,128)(2,1)S(1)}, u32[]{:S(2)}, u32[]{:S(2)}) collective-permute-start(bf16[8,10752]{1,0:T(8,128)(2,1)S(1)} %get-tuple-element.60), channel_id=1, source_target_pairs={{0,16},{1,17},{2,18},{3,19},{4,20},{5,21},{6,22},{7,23},{8,24},{9,... | collective-permute-start | bytes 516104 | tf_op jit(solution)/shard_map/ppermute | solution.py:22
  19.7 8.1 %collective-permute-start.18 = (bf16[8,10752]{1,0:T(8,128)(2,1)S(1)}, bf16[8,10752]{1,0:T(8,128)(2,1)S(1)}, u32[]{:S(2)}, u32[]{:S(2)}) collective-permute-start(bf16[8,10752]{1,0:T(8,128)(2,1)S(1)} %get-tuple-element.60), channel_id=1, source_target_pairs={{0,32},{1,33},{2,34},{3,35},{4,36},{5,37},{6,38},{7,39},{8,40},{9,... | collective-permute-start | bytes 516104 | tf_op jit(solution)/shard_map/ppermute | solution.py:22
  24.5 16.4 %collective-permute-start.6 = (bf16[32,10752]{1,0:T(8,128)(2,1)S(1)}, bf16[32,10752]{1,0:T(8,128)(2,1)S(1)}, u32[]{:S(2)}, u32[]{:S(2)}) collective-permute-start(bf16[32,10752]{1,0:T(8,128)(2,1)S(1)} %pad_maximum_fusion.1.refs_0_), channel_id=1, source_target_pairs={{0,16},{1,17},{2,18},{3,19},{4,20},{5,21},{6,22},{7,23},{8,24},{9,... | collective-permute-start | bytes 2064392 | tf_op jit(solution)/shard_map/ppermute | solution.py:22
  25.9 19.7 %collective-permute-start.7 = (bf16[32,10752]{1,0:T(8,128)(2,1)S(1)}, bf16[32,10752]{1,0:T(8,128)(2,1)}, u32[]{:S(2)}, u32[]{:S(2)}) collective-permute-start(bf16[32,10752]{1,0:T(8,128)(2,1)S(1)} %pad_maximum_fusion.1.refs_0_), channel_id=1, source_target_pairs={{0,48},{1,49},{2,50},{3,51},{4,52},{5,53},{6,54},{7,55},{8,56},{9,... | collective-permute-start | bytes 2064392 | tf_op jit(solution)/shard_map/ppermute | solution.py:22
  28.8 20.6 %collective-permute-start.20 = (bf16[32,10752]{1,0:T(8,128)(2,1)S(1)}, bf16[32,10752]{1,0:T(8,128)(2,1)S(1)}, u32[]{:S(2)}, u32[]{:S(2)}) collective-permute-start(bf16[32,10752]{1,0:T(8,128)(2,1)S(1)} %pad_maximum_fusion.2.refs_0_), channel_id=1, source_target_pairs={{0,4},{1,5},{2,6},{3,7},{4,0},{5,1},{6,2},{7,3},{8,12},{9,13},{10,... | collective-permute-start | bytes 2064392 | tf_op jit(solution)/shard_map/ppermute | solution.py:22
  28.9 20.5 %collective-permute-start.21 = (bf16[32,10752]{1,0:T(8,128)(2,1)S(1)}, bf16[32,10752]{1,0:T(8,128)(2,1)S(1)}, u32[]{:S(2)}, u32[]{:S(2)}) collective-permute-start(bf16[32,10752]{1,0:T(8,128)(2,1)S(1)} %pad_maximum_fusion.2.refs_0_), channel_id=1, source_target_pairs={{0,12},{1,13},{2,14},{3,15},{4,8},{5,9},{6,10},{7,11},{8,4},{9,5},... | collective-permute-start | bytes 2064392 | tf_op jit(solution)/shard_map/ppermute | solution.py:22
  48.7 7.2 %collective-permute-start.8 = (bf16[16,10752]{1,0:T(8,128)(2,1)}, bf16[16,10752]{1,0:T(8,128)(2,1)}, u32[]{:S(2)}, u32[]{:S(2)}) collective-permute-start(bf16[16,10752]{1,0:T(8,128)(2,1)} %get-tuple-element.25), channel_id=1, source_target_pairs={{0,16},{1,17},{2,18},{3,19},{4,20},{5,21},{6,22},{7,23},{8,24},{9,... | collective-permute-start | bytes 1032200 | tf_op jit(solution)/shard_map/ppermute | solution.py:22
  49.2 8.6 %collective-permute-start.9 = (bf16[16,10752]{1,0:T(8,128)(2,1)}, bf16[16,10752]{1,0:T(8,128)(2,1)}, u32[]{:S(2)}, u32[]{:S(2)}) collective-permute-start(bf16[16,10752]{1,0:T(8,128)(2,1)} %get-tuple-element.26), channel_id=1, source_target_pairs={{0,48},{1,49},{2,50},{3,51},{4,52},{5,53},{6,54},{7,55},{8,56},{9,... | collective-permute-start | bytes 1032200 | tf_op jit(solution)/shard_map/ppermute | solution.py:22
  50.6 13.9 %collective-permute-start.22 = (bf16[16,10752]{1,0:T(8,128)(2,1)S(1)}, bf16[16,10752]{1,0:T(8,128)(2,1)S(1)}, u32[]{:S(2)}, u32[]{:S(2)}) collective-permute-start(bf16[16,10752]{1,0:T(8,128)(2,1)S(1)} %get-tuple-element.34), channel_id=1, source_target_pairs={{0,4},{1,5},{2,6},{3,7},{4,0},{5,1},{6,2},{7,3},{8,12},{9,13},{10,... | collective-permute-start | bytes 1032200 | tf_op jit(solution)/shard_map/ppermute | solution.py:22
  52.3 12.2 %collective-permute-start.23 = (bf16[16,10752]{1,0:T(8,128)(2,1)S(1)}, bf16[16,10752]{1,0:T(8,128)(2,1)S(1)}, u32[]{:S(2)}, u32[]{:S(2)}) collective-permute-start(bf16[16,10752]{1,0:T(8,128)(2,1)S(1)} %get-tuple-element.35), channel_id=1, source_target_pairs={{0,12},{1,13},{2,14},{3,15},{4,8},{5,9},{6,10},{7,11},{8,4},{9,5},... | collective-permute-start | bytes 1032200 | tf_op jit(solution)/shard_map/ppermute | solution.py:22
  64.3 8.8 %collective-permute-start.10 = (bf16[16,7168]{1,0:T(8,128)(2,1)S(1)}, bf16[16,7168]{1,0:T(8,128)(2,1)S(1)}, u32[]{:S(2)}, u32[]{:S(2)}) collective-permute-start(bf16[16,7168]{1,0:T(8,128)(2,1)S(1)} %get-tuple-element.30), channel_id=1, source_target_pairs={{0,48},{1,49},{2,50},{3,51},{4,52},{5,53},{6,54},{7,55},{8,56},{9,... | collective-permute-start | bytes 688136 | tf_op jit(solution)/shard_map/ppermute | solution.py:22
  64.4 10.4 %collective-permute-start.12 = (bf16[16,7168]{1,0:T(8,128)(2,1)S(1)}, bf16[16,7168]{1,0:T(8,128)(2,1)S(1)}, u32[]{:S(2)}, u32[]{:S(2)}) collective-permute-start(bf16[16,7168]{1,0:T(8,128)(2,1)S(1)} %get-tuple-element.32), channel_id=1, source_target_pairs={{0,16},{1,17},{2,18},{3,19},{4,20},{5,21},{6,22},{7,23},{8,24},{9,... | collective-permute-start | bytes 688136 | tf_op jit(solution)/shard_map/ppermute | solution.py:22
  68.6 9.3 %collective-permute-start.24 = (bf16[32,7296]{1,0:T(8,128)(2,1)S(1)}, bf16[32,7296]{1,0:T(8,128)(2,1)S(1)}, u32[]{:S(2)}, u32[]{:S(2)}) collective-permute-start(bf16[32,7296]{1,0:T(8,128)(2,1)S(1)} %get-tuple-element.43), channel_id=1, source_target_pairs={{0,4},{1,5},{2,6},{3,7},{4,0},{5,1},{6,2},{7,3},{8,12},{9,13},{10,... | collective-permute-start | bytes 1400840 | tf_op jit(solution)/shard_map/ppermute | solution.py:22
  70.6 16.4 %collective-permute-start.25 = (bf16[32,7296]{1,0:T(8,128)(2,1)S(1)}, bf16[32,7296]{1,0:T(8,128)(2,1)S(1)}, u32[]{:S(2)}, u32[]{:S(2)}) collective-permute-start(bf16[32,7296]{1,0:T(8,128)(2,1)S(1)} %get-tuple-element.44), channel_id=1, source_target_pairs={{0,8},{1,9},{2,10},{3,11},{4,12},{5,13},{6,14},{7,15},{8,0},{9,1},... | collective-permute-start | bytes 1400840 | tf_op jit(solution)/shard_map/ppermute | solution.py:22
  71.0 16.1 %collective-permute-start.26 = (bf16[32,7296]{1,0:T(8,128)(2,1)S(1)}, bf16[32,7296]{1,0:T(8,128)(2,1)S(1)}, u32[]{:S(2)}, u32[]{:S(2)}) collective-permute-start(bf16[32,7296]{1,0:T(8,128)(2,1)S(1)} %get-tuple-element.45), channel_id=1, source_target_pairs={{0,12},{1,13},{2,14},{3,15},{4,8},{5,9},{6,10},{7,11},{8,4},{9,5},... | collective-permute-start | bytes 1400840 | tf_op jit(solution)/shard_map/ppermute | solution.py:22
  73.2 14.2 %collective-permute-start.11 = (bf16[32,7168]{1,0:T(8,128)(2,1)S(1)}, bf16[32,7168]{1,0:T(8,128)(2,1)S(1)}, u32[]{:S(2)}, u32[]{:S(2)}) collective-permute-start(bf16[32,7168]{1,0:T(8,128)(2,1)S(1)} %pad_maximum_fusion.4), channel_id=1, source_target_pairs={{0,16},{1,17},{2,18},{3,19},{4,20},{5,21},{6,22},{7,23},{8,24},{9,... | collective-permute-start | bytes 1376264 | tf_op jit(solution)/shard_map/ppermute | solution.py:22
  74.8 12.6 %collective-permute-start.13 = (bf16[32,7168]{1,0:T(8,128)(2,1)S(1)}, bf16[32,7168]{1,0:T(8,128)(2,1)S(1)}, u32[]{:S(2)}, u32[]{:S(2)}) collective-permute-start(bf16[32,7168]{1,0:T(8,128)(2,1)S(1)} %pad_maximum_fusion.5), channel_id=1, source_target_pairs={{0,48},{1,49},{2,50},{3,51},{4,52},{5,53},{6,54},{7,55},{8,56},{9,... | collective-permute-start | bytes 1376264 | tf_op jit(solution)/shard_map/ppermute | solution.py:22
  87.6 8.1 %collective-permute-start.14 = (bf16[8,7168]{1,0:T(8,128)(2,1)S(1)}, bf16[8,7168]{1,0:T(8,128)(2,1)S(1)}, u32[]{:S(2)}, u32[]{:S(2)}) collective-permute-start(bf16[8,7168]{1,0:T(8,128)(2,1)S(1)} %get-tuple-element.56), channel_id=1, source_target_pairs={{0,4},{1,5},{2,6},{3,7},{4,0},{5,1},{6,2},{7,3},{8,12},{9,13},{10,... | collective-permute-start | bytes 344072 | tf_op jit(solution)/shard_map/ppermute | solution.py:22
  89.3 7.3 %collective-permute-start.15 = (bf16[8,7168]{1,0:T(8,128)(2,1)S(1)}, bf16[8,7168]{1,0:T(8,128)(2,1)S(1)}, u32[]{:S(2)}, u32[]{:S(2)}) collective-permute-start(bf16[8,7168]{1,0:T(8,128)(2,1)S(1)} %get-tuple-element.58), channel_id=1, source_target_pairs={{0,8},{1,9},{2,10},{3,11},{4,12},{5,13},{6,14},{7,15},{8,0},{9,1},... | collective-permute-start | bytes 344072 | tf_op jit(solution)/shard_map/ppermute | solution.py:22
  101.0 9.0 %collective-permute-start.30 = (bf16[2,14464]{1,0:T(2,128)(2,1)S(1)}, bf16[2,14464]{1,0:T(2,128)(2,1)S(1)}, u32[]{:S(2)}, u32[]{:S(2)}) collective-permute-start(bf16[2,14464]{1,0:T(2,128)(2,1)S(1)} %get-tuple-element.63), channel_id=1, source_target_pairs={{0,1},{1,0},{2,3},{3,2},{4,5},{5,4},{6,7},{7,6},{8,9},{9,8},{10,11... | collective-permute-start | bytes 173576 | tf_op jit(solution)/shard_map/ppermute | solution.py:22
  114.0 16.0 %collective-permute-start.33 = (bf16[2,7168]{1,0:T(2,128)(2,1)S(1)}, bf16[2,7168]{1,0:T(2,128)(2,1)S(1)}, u32[]{:S(2)}, u32[]{:S(2)}) collective-permute-start(bf16[2,7168]{1,0:T(2,128)(2,1)S(1)} %get-tuple-element.67), channel_id=1, source_target_pairs={{0,192},{64,128},{128,64},{192,0},{1,193},{65,129},{129,65},{193,1... | collective-permute-start | bytes 86024 | tf_op jit(solution)/shard_map/ppermute | solution.py:37
  (18 other events, 116.9 us)

commit v5 on v4

--- a/solution.py
+++ b/solution.py
@@ -39,19 +39,6 @@
     return jnp.where(even, got_far, got_near), jnp.where(even, got_near, got_far)
 
 
-def coded(value):
-    top = lax.reduce_precision(value, 8, 7)
-    return jnp.pad(jnp.concatenate([top, value - top], axis=1), ((0, 0), (0, LANES - 8)))
-
-
-def decoded(columns_of):
-    return columns_of[:, :4] + columns_of[:, 4:8]
-
-
-def after(value, *earlier):
-    return lax.optimization_barrier((value,) + earlier)[0]
-
-
 def gathered(value, along):
     return jnp.concatenate([value] + [swap(value, along, j) for j in range(1, SIDE)], axis=0)
 
@@ -126,7 +113,6 @@
         out_shape=(out, out),
         in_specs=[vmem, vmem, there, there],
         out_specs=(vmem, vmem),
-        cost_estimate=pl.CostEstimate(flops=1, bytes_accessed=10**6, transcendentals=0),
         scratch_shapes=[pltpu.SemaphoreType.DMA((2,))],
         compiler_params=pltpu.CompilerParams(vmem_limit_bytes=16 * 2**20),
     )(three, one, *earlier)
@@ -205,7 +191,9 @@
         out_specs=(vmem,) * 12,
         scratch_shapes=[pltpu.SemaphoreType.DMA((3, LOAD_CHUNKS))],
         compiler_params=pltpu.CompilerParams(vmem_limit_bytes=36 * 2**20),
-        cost_estimate=pl.CostEstimate(flops=10**10, bytes_accessed=10**7, transcendentals=0),
+        cost_estimate=pl.CostEstimate(
+            flops=2 * count * width * hidden * 4, bytes_accessed=6 * width * hidden, transcendentals=0
+        ),
     )(*parts, table, w_g, w_u, w_d)
 
 
@@ -261,7 +249,6 @@
         out_shape=(out((rows, width), F32), sent, sent, sent, out((rows, 8), F32)),
         in_specs=[vmem] * 11,
         out_specs=(vmem,) * 5,
-        cost_estimate=pl.CostEstimate(flops=10**10, bytes_accessed=10**7, transcendentals=0),
         compiler_params=pltpu.CompilerParams(vmem_limit_bytes=24 * 2**20),
     )(*parts, gate_b, up_b, table, w_g, w_u, w_d)
 
@@ -310,16 +297,18 @@
         + swap(jnp.concatenate([f_one_lo, f_one_hi], axis=0), "y", 1).astype(F32)
         + swap(jnp.concatenate([f_three_lo, f_three_hi], axis=0), "y", 3).astype(F32)
     )
-    sum_b, sum_p = after(b_own, sum_f), p_own[:, :4]
+    sum_b, sum_p = b_own, p_own[:, :4]
     for j, block in enumerate((b_one, b_two, b_three), 1):
         got = swap(block, "x", j).astype(F32)
         sum_b = sum_b + got[:, :width]
         sum_p = sum_p + got[:, width : width + 4] + got[:, width + 4 : width + 8]
 
     sum_f = scattered(*cut(sum_f, BF16), "x")
-    both = scattered(*cut(jnp.concatenate([sum_b, coded(sum_p)], axis=1), BF16), "y")
-    sum_b, sum_p = both[:, :width], decoded(both[:, width:])
-    last = scattered(*cut(jnp.concatenate([sum_f, sum_b, coded(sum_p)], axis=1), BF16), "z")
+    top = lax.reduce_precision(sum_p, 8, 7)
+    coded = jnp.pad(jnp.concatenate([top, sum_p - top], axis=1), ((0, 0), (0, LANES - 8)))
+    both = scattered(*cut(jnp.concatenate([sum_b, coded], axis=1), BF16), "y")
+    sum_b, coded = both[:, :width], both[:, width:]
+    last = scattered(*cut(jnp.concatenate([sum_f, sum_b, coded], axis=1), F32), "z")
 
     layer_out = (x_fwd.astype(F32) + last[:, :width]).astype(BF16)
     input_grad = (grad_out.astype(F32) + last[:, width : 2 * width]).astype(BF16)

time: 131 us -> 130 us (level)
  waiting for transfers between devices: 43 us -> 46.2 us
  starting transfers between devices: 63.3 us -> 61 us
    ppermute x33, waiting for transfers between devices: 42 us -> 44.4 us  [swap(): lax.ppermute(value, 'expert', [(i, i ^ by * STRIDE[along]) for i in range...]
    ppermute x1, starting transfers between devices: 14.5 us -> 12.4 us  [handed_on(): got_far = lax.ppermute(jnp.where(even, back, forth), 'segment', far)]
  transfers between devices with their start and end apart: 35 -> 35, of which waited for: 17 -> 16; matrix products, arithmetic and copies ran while one was open for 3% -> 4% of each run, Pallas kernels for 10% -> 9%
where the time goes in v5:
time: 130 us
  starting transfers between devices  61 us (47%)
  waiting for transfers between devices  46.2 us (36%)
  Pallas kernels  12.1 us (9%)
  other arithmetic  6.69 us (5%)
  local copies, waits for them, and re-layouts  2.64 us (2%)
    ppermute x33, starting transfers between devices, swap(): lax.ppermute(value, 'expert', [(i, i ^ by * STRIDE[along]) for i in range...  48.6 us
    ppermute x33, waiting for transfers between devices, swap(): lax.ppermute(value, 'expert', [(i, i ^ by * STRIDE[along]) for i in range...  44.4 us
    ppermute x1, starting transfers between devices, handed_on(): got_far = lax.ppermute(jnp.where(even, back, forth), 'segment', far)  12.4 us
    pallas_call x1, Pallas kernels, forward(): pl.pallas_call(forward_kernel, out_shape=(out(w_g.shape, BF16), out(w_u.s...  6.37 us
    pallas_call x1, Pallas kernels, backward(): pl.pallas_call(backward_kernel, out_shape=(out((rows, width), F32), sent,...  4.09 us
  transfers between devices with their start and end apart: 35, of which 16 were waited for; matrix products, arithmetic and copies ran while one was open for 4% of the time, Pallas kernels for 9%

profile of v5, /device:TPU:1, one launch (start us, length us, event | category | flops | bytes accessed | tf_op | source)
XLA Modules:
  0.0 129.6 jit_solution(12717984434108762062)
XLA Ops:
  2.2 2.6 %collective-permute-start = (bf16[2,21504]{1,0:T(2,128)(2,1)S(1)}, bf16[2,21504]{1,0:T(2,128)(2,1)S(1)}, u32[]{:S(2)}, u32[]{:S(2)}) collective-permute-start(bf16[2,21504]{1,0:T(2,128)(2,1)S(1)} %pad_maximum_fusion.7), channel_id=1, source_target_pairs={{0,1},{1,0},{2,3},{3,2},{4,5},{5,4},{6,7},{7,6},{8,9},{9,8},{10,11... | collective-permute-start | bytes 258056 | tf_op jit(solution)/shard_map/ppermute | solution.py:22
  4.8 3.0 %collective-permute-start.1 = (bf16[2,21504]{1,0:T(2,128)(2,1)S(1)}, bf16[2,21504]{1,0:T(2,128)(2,1)S(1)}, u32[]{:S(2)}, u32[]{:S(2)}) collective-permute-start(bf16[2,21504]{1,0:T(2,128)(2,1)S(1)} %pad_maximum_fusion.7), channel_id=1, source_target_pairs={{0,2},{1,3},{2,0},{3,1},{4,6},{5,7},{6,4},{7,5},{8,10},{9,11},{10,... | collective-permute-start | bytes 258056 | tf_op jit(solution)/shard_map/ppermute | solution.py:22
  10.3 2.7 %collective-permute-done.2 = bf16[2,21504]{1,0:T(2,128)(2,1)S(1)} collective-permute-done((bf16[2,21504]{1,0:T(2,128)(2,1)S(1)}, bf16[2,21504]{1,0:T(2,128)(2,1)S(1)}, u32[]{:S(2)}, u32[]{:S(2)}) %collective-permute-start.2) | collective-permute-done | bytes 86048 | tf_op jit(solution)/shard_map/ppermute | solution.py:22
  15.6 2.5 %collective-permute-start.4 = (bf16[8,10752]{1,0:T(8,128)(2,1)S(1)}, bf16[8,10752]{1,0:T(8,128)(2,1)S(1)}, u32[]{:S(2)}, u32[]{:S(2)}) collective-permute-start(bf16[8,10752]{1,0:T(8,128)(2,1)S(1)} %get-tuple-element.60), channel_id=1, source_target_pairs={{0,8},{1,9},{2,10},{3,11},{4,12},{5,13},{6,14},{7,15},{8,0},{9,1},... | collective-permute-start | bytes 516104 | tf_op jit(solution)/shard_map/ppermute | solution.py:22
  19.7 2.6 %collective-permute-start.18 = (bf16[8,10752]{1,0:T(8,128)(2,1)S(1)}, bf16[8,10752]{1,0:T(8,128)(2,1)S(1)}, u32[]{:S(2)}, u32[]{:S(2)}) collective-permute-start(bf16[8,10752]{1,0:T(8,128)(2,1)S(1)} %get-tuple-element.61), channel_id=1, source_target_pairs={{0,32},{1,33},{2,34},{3,35},{4,36},{5,37},{6,38},{7,39},{8,40},{9,... | collective-permute-start | bytes 516104 | tf_op jit(solution)/shard_map/ppermute | solution.py:22
  25.9 1.9 %collective-permute-start.7 = (bf16[32,10752]{1,0:T(8,128)(2,1)S(1)}, bf16[32,10752]{1,0:T(8,128)(2,1)}, u32[]{:S(2)}, u32[]{:S(2)}) collective-permute-start(bf16[32,10752]{1,0:T(8,128)(2,1)S(1)} %pad_maximum_fusion.1.refs_0_), channel_id=1, source_target_pairs={{0,48},{1,49},{2,50},{3,51},{4,52},{5,53},{6,54},{7,55},{8,56},{9,... | collective-permute-start | bytes 2064392 | tf_op jit(solution)/shard_map/ppermute | solution.py:22
  28.9 2.6 %collective-permute-start.21 = (bf16[32,10752]{1,0:T(8,128)(2,1)S(1)}, bf16[32,10752]{1,0:T(8,128)(2,1)S(1)}, u32[]{:S(2)}, u32[]{:S(2)}) collective-permute-start(bf16[32,10752]{1,0:T(8,128)(2,1)S(1)} %pad_maximum_fusion.2.refs_0_), channel_id=1, source_target_pairs={{0,12},{1,13},{2,14},{3,15},{4,8},{5,9},{6,10},{7,11},{8,4},{9,5},... | collective-permute-start | bytes 2064392 | tf_op jit(solution)/shard_map/ppermute | solution.py:22
  32.8 8.1 %collective-permute-done.6.one.refs_1_ = bf16[32,10752]{1,0:T(8,128)(2,1)S(1)} collective-permute-done((bf16[32,10752]{1,0:T(8,128)(2,1)S(1)}, bf16[32,10752]{1,0:T(8,128)(2,1)S(1)}, u32[]{:S(2)}, u32[]{:S(2)}) %collective-permute-start.6) | collective-permute-done | bytes 688160 | tf_op jit(solution)/shard_map/ppermute | solution.py:22
  41.0 4.7 %collective-permute-done.7.three.refs_4_ = bf16[32,10752]{1,0:T(8,128)(2,1)} collective-permute-done((bf16[32,10752]{1,0:T(8,128)(2,1)S(1)}, bf16[32,10752]{1,0:T(8,128)(2,1)}, u32[]{:S(2)}, u32[]{:S(2)}) %collective-permute-start.7) | collective-permute-done | bytes 688160 | tf_op jit(solution)/shard_map/ppermute | solution.py:22
  51.5 3.3 %collective-permute-done.8.refs_2_ = bf16[16,10752]{1,0:T(8,128)(2,1)S(1)} collective-permute-done((bf16[16,10752]{1,0:T(8,128)(2,1)S(1)}, bf16[16,10752]{1,0:T(8,128)(2,1)S(1)}, u32[]{:S(2)}, u32[]{:S(2)}) %collective-permute-start.8) | collective-permute-done | bytes 344096 | tf_op jit(solution)/shard_map/ppermute | solution.py:22
  54.8 1.8 %collective-permute-done.9.refs_3_ = bf16[16,10752]{1,0:T(8,128)(2,1)S(1)} collective-permute-done((bf16[16,10752]{1,0:T(8,128)(2,1)S(1)}, bf16[16,10752]{1,0:T(8,128)(2,1)S(1)}, u32[]{:S(2)}, u32[]{:S(2)}) %collective-permute-start.9) | collective-permute-done | bytes 344096 | tf_op jit(solution)/shard_map/ppermute | solution.py:22
  56.6 6.4 %shard_map.122 = (bf16[7168,256]{1,0:T(8,128)(2,1)S(1)}, bf16[7168,256]{1,0:T(8,128)(2,1)S(1)}, bf16[256,7168]{1,0:T(8,128)(2,1)S(1)}, f32[128,256]{1,0:T(8,128)...) custom-call(bf16[32,10752]{1,0:T(8,128)(2,1)S(1)} %pad_maximum_fusio, ...), custom_call_target="tpu_custom_call" | custom-call | flops 1879048192 | bytes 11010048 | tf_op jit(solution)/shard_map/pallas_call | solution.py:174
  63.2 4.1 %shard_map.124 = (f32[32,7168]{1,0:T(8,128)S(1)}, bf16[32,7296]{1,0:T(8,128)(2,1)S(1)}, bf16[32,7296]{1,0:T(8,128)(2,1)S(1)}, bf16[32,7296]{1,0:T(8,128)(2,1)S(1)}, f32[32,8]{1,0:T(8,128)S(1)}) custom-call(bf16[32,10752]{1,0:T(8,128)(2,1)S(1)} %pad_maximum_fusion.2.refs_0_, bf16[32,10752]{1,0:T(8,128)(2,1)S(1)} %collective-permute-done.20.one.refs_1_, ...), custom_call_target="tpu_custom_call" | custom-call | tf_op jit(solution)/shard_map/pallas_call | solution.py:247
  67.3 2.0 %collective-permute-start.24 = (bf16[32,7296]{1,0:T(8,128)(2,1)S(1)}, bf16[32,7296]{1,0:T(8,128)(2,1)S(1)}, u32[]{:S(2)}, u32[]{:S(2)}) collective-permute-start(bf16[32,7296]{1,0:T(8,128)(2,1)S(1)} %get-tuple-element.41), channel_id=1, source_target_pairs={{0,4},{1,5},{2,6},{3,7},{4,0},{5,1},{6,2},{7,3},{8,12},{9,13},{10,... | collective-permute-start | bytes 1400840 | tf_op jit(solution)/shard_map/ppermute | solution.py:22
  69.7 2.1 %collective-permute-start.26 = (bf16[32,7296]{1,0:T(8,128)(2,1)S(1)}, bf16[32,7296]{1,0:T(8,128)(2,1)S(1)}, u32[]{:S(2)}, u32[]{:S(2)}) collective-permute-start(bf16[32,7296]{1,0:T(8,128)(2,1)S(1)} %get-tuple-element.43), channel_id=1, source_target_pairs={{0,12},{1,13},{2,14},{3,15},{4,8},{5,9},{6,10},{7,11},{8,4},{9,5},... | collective-permute-start | bytes 1400840 | tf_op jit(solution)/shard_map/ppermute | solution.py:22
  73.6 2.1 %collective-permute-start.13 = (bf16[32,7168]{1,0:T(8,128)(2,1)S(1)}, bf16[32,7168]{1,0:T(8,128)(2,1)S(1)}, u32[]{:S(2)}, u32[]{:S(2)}) collective-permute-start(bf16[32,7168]{1,0:T(8,128)(2,1)S(1)} %pad_maximum_fusion.4), channel_id=1, source_target_pairs={{0,48},{1,49},{2,50},{3,51},{4,52},{5,53},{6,54},{7,55},{8,56},{9,... | collective-permute-start | bytes 1376264 | tf_op jit(solution)/shard_map/ppermute | solution.py:22
  76.7 9.1 %collective-permute-done.25 = bf16[32,7296]{1,0:T(8,128)(2,1)S(1)} collective-permute-done((bf16[32,7296]{1,0:T(8,128)(2,1)S(1)}, bf16[32,7296]{1,0:T(8,128)(2,1)S(1)}, u32[]{:S(2)}, u32[]{:S(2)}) %collective-permute-start.25) | collective-permute-done | bytes 466976 | tf_op jit(solution)/shard_map/ppermute | solution.py:22
  88.3 2.0 %collective-permute-start.29 = (bf16[8,7296]{1,0:T(8,128)(2,1)S(1)}, bf16[8,7296]{1,0:T(8,128)(2,1)S(1)}, u32[]{:S(2)}, u32[]{:S(2)}) collective-permute-start(bf16[8,7296]{1,0:T(8,128)(2,1)S(1)} %get-tuple-element.52), channel_id=1, source_target_pairs={{0,48},{1,49},{2,50},{3,51},{4,52},{5,53},{6,54},{7,55},{8,56},{9,... | collective-permute-start | bytes 350216 | tf_op jit(solution)/shard_map/ppermute | solution.py:22
  90.6 1.9 %collective-permute-start.14 = (bf16[8,7168]{1,0:T(8,128)(2,1)S(1)}, bf16[8,7168]{1,0:T(8,128)(2,1)S(1)}, u32[]{:S(2)}, u32[]{:S(2)}) collective-permute-start(bf16[8,7168]{1,0:T(8,128)(2,1)S(1)} %get-tuple-element.57), channel_id=1, source_target_pairs={{0,4},{1,5},{2,6},{3,7},{4,0},{5,1},{6,2},{7,3},{8,12},{9,13},{10,... | collective-permute-start | bytes 344072 | tf_op jit(solution)/shard_map/ppermute | solution.py:22
  92.5 2.8 %collective-permute-start.15 = (bf16[8,7168]{1,0:T(8,128)(2,1)S(1)}, bf16[8,7168]{1,0:T(8,128)(2,1)S(1)}, u32[]{:S(2)}, u32[]{:S(2)}) collective-permute-start(bf16[8,7168]{1,0:T(8,128)(2,1)S(1)} %get-tuple-element.59), channel_id=1, source_target_pairs={{0,8},{1,9},{2,10},{3,11},{4,12},{5,13},{6,14},{7,15},{8,0},{9,1},... | collective-permute-start | bytes 344072 | tf_op jit(solution)/shard_map/ppermute | solution.py:22
  95.5 3.3 %collective-permute-done.15 = bf16[8,7168]{1,0:T(8,128)(2,1)S(1)} collective-permute-done((bf16[8,7168]{1,0:T(8,128)(2,1)S(1)}, bf16[8,7168]{1,0:T(8,128)(2,1)S(1)}, u32[]{:S(2)}, u32[]{:S(2)}) %collective-permute-start.15) | collective-permute-done | bytes 114720 | tf_op jit(solution)/shard_map/ppermute | solution.py:22
  100.4 6.0 %collective-permute-start.30 = (f32[2,14464]{1,0:T(2,128)S(1)}, f32[2,14464]{1,0:T(2,128)S(1)}, u32[]{:S(2)}, u32[]{:S(2)}) collective-permute-start(f32[2,14464]{1,0:T(2,128)S(1)} %get-tuple-element.54), channel_id=1, source_target_pairs={{0,1},{1,0},{2,3},{3,2},{4,5},{5,4},{6,7},{7,6},{8,9},{9,8},{10,11... | collective-permute-start | bytes 347144 | tf_op jit(solution)/shard_map/ppermute | solution.py:22
  111.0 3.1 %collective-permute-done.32 = f32[2,14464]{1,0:T(2,128)S(1)} collective-permute-done((f32[2,14464]{1,0:T(2,128)S(1)}, f32[2,14464]{1,0:T(2,128)S(1)}, u32[]{:S(2)}, u32[]{:S(2)}) %collective-permute-start.32) | collective-permute-done | bytes 115744 | tf_op jit(solution)/shard_map/ppermute | solution.py:22
  114.2 12.4 %collective-permute-start.33 = (bf16[2,7168]{1,0:T(2,128)(2,1)S(1)}, bf16[2,7168]{1,0:T(2,128)(2,1)S(1)}, u32[]{:S(2)}, u32[]{:S(2)}) collective-permute-start(bf16[2,7168]{1,0:T(2,128)(2,1)S(1)} %get-tuple-element.63), channel_id=1, source_target_pairs={{0,192},{64,128},{128,64},{192,0},{1,193},{65,129},{129,65},{193,1... | collective-permute-start | bytes 86024 | tf_op jit(solution)/shard_map/ppermute | solution.py:37
  (102 shorter events, 35.5 us)
Async XLA Ops:
  2.2 7.1 %collective-permute-start = (bf16[2,21504]{1,0:T(2,128)(2,1)S(1)}, bf16[2,21504]{1,0:T(2,128)(2,1)S(1)}, u32[]{:S(2)}, u32[]{:S(2)}) collective-permute-start(bf16[2,21504]{1,0:T(2,128)(2,1)S(1)} %pad_maximum_fusion.7), channel_id=1, source_target_pairs={{0,1},{1,0},{2,3},{3,2},{4,5},{5,4},{6,7},{7,6},{8,9},{9,8},{10,11... | collective-permute-start | bytes 258056 | tf_op jit(solution)/shard_map/ppermute | solution.py:22
  14.3 8.1 %collective-permute-start.3 = (bf16[8,10752]{1,0:T(8,128)(2,1)S(1)}, bf16[8,10752]{1,0:T(8,128)(2,1)S(1)}, u32[]{:S(2)}, u32[]{:S(2)}) collective-permute-start(bf16[8,10752]{1,0:T(8,128)(2,1)S(1)} %get-tuple-element.60), channel_id=1, source_target_pairs={{0,4},{1,5},{2,6},{3,7},{4,0},{5,1},{6,2},{7,3},{8,12},{9,13},{10,... | collective-permute-start | bytes 516104 | tf_op jit(solution)/shard_map/ppermute | solution.py:22
  15.6 7.5 %collective-permute-start.4 = (bf16[8,10752]{1,0:T(8,128)(2,1)S(1)}, bf16[8,10752]{1,0:T(8,128)(2,1)S(1)}, u32[]{:S(2)}, u32[]{:S(2)}) collective-permute-start(bf16[8,10752]{1,0:T(8,128)(2,1)S(1)} %get-tuple-element.60), channel_id=1, source_target_pairs={{0,8},{1,9},{2,10},{3,11},{4,12},{5,13},{6,14},{7,15},{8,0},{9,1},... | collective-permute-start | bytes 516104 | tf_op jit(solution)/shard_map/ppermute | solution.py:22
  18.3 9.5 %collective-permute-start.17 = (bf16[8,10752]{1,0:T(8,128)(2,1)S(1)}, bf16[8,10752]{1,0:T(8,128)(2,1)S(1)}, u32[]{:S(2)}, u32[]{:S(2)}) collective-permute-start(bf16[8,10752]{1,0:T(8,128)(2,1)S(1)} %get-tuple-element.61), channel_id=1, source_target_pairs={{0,16},{1,17},{2,18},{3,19},{4,20},{5,21},{6,22},{7,23},{8,24},{9,... | collective-permute-start | bytes 516104 | tf_op jit(solution)/shard_map/ppermute | solution.py:22
  19.7 8.1 %collective-permute-start.18 = (bf16[8,10752]{1,0:T(8,128)(2,1)S(1)}, bf16[8,10752]{1,0:T(8,128)(2,1)S(1)}, u32[]{:S(2)}, u32[]{:S(2)}) collective-permute-start(bf16[8,10752]{1,0:T(8,128)(2,1)S(1)} %get-tuple-element.61), channel_id=1, source_target_pairs={{0,32},{1,33},{2,34},{3,35},{4,36},{5,37},{6,38},{7,39},{8,40},{9,... | collective-permute-start | bytes 516104 | tf_op jit(solution)/shard_map/ppermute | solution.py:22
  24.5 16.4 %collective-permute-start.6 = (bf16[32,10752]{1,0:T(8,128)(2,1)S(1)}, bf16[32,10752]{1,0:T(8,128)(2,1)S(1)}, u32[]{:S(2)}, u32[]{:S(2)}) collective-permute-start(bf16[32,10752]{1,0:T(8,128)(2,1)S(1)} %pad_maximum_fusion.1.refs_0_), channel_id=1, source_target_pairs={{0,16},{1,17},{2,18},{3,19},{4,20},{5,21},{6,22},{7,23},{8,24},{9,... | collective-permute-start | bytes 2064392 | tf_op jit(solution)/shard_map/ppermute | solution.py:22
  25.9 19.7 %collective-permute-start.7 = (bf16[32,10752]{1,0:T(8,128)(2,1)S(1)}, bf16[32,10752]{1,0:T(8,128)(2,1)}, u32[]{:S(2)}, u32[]{:S(2)}) collective-permute-start(bf16[32,10752]{1,0:T(8,128)(2,1)S(1)} %pad_maximum_fusion.1.refs_0_), channel_id=1, source_target_pairs={{0,48},{1,49},{2,50},{3,51},{4,52},{5,53},{6,54},{7,55},{8,56},{9,... | collective-permute-start | bytes 2064392 | tf_op jit(solution)/shard_map/ppermute | solution.py:22
  28.8 19.8 %collective-permute-start.20 = (bf16[32,10752]{1,0:T(8,128)(2,1)S(1)}, bf16[32,10752]{1,0:T(8,128)(2,1)S(1)}, u32[]{:S(2)}, u32[]{:S(2)}) collective-permute-start(bf16[32,10752]{1,0:T(8,128)(2,1)S(1)} %pad_maximum_fusion.2.refs_0_), channel_id=1, source_target_pairs={{0,4},{1,5},{2,6},{3,7},{4,0},{5,1},{6,2},{7,3},{8,12},{9,13},{10,... | collective-permute-start | bytes 2064392 | tf_op jit(solution)/shard_map/ppermute | solution.py:22
  28.9 19.7 %collective-permute-start.21 = (bf16[32,10752]{1,0:T(8,128)(2,1)S(1)}, bf16[32,10752]{1,0:T(8,128)(2,1)S(1)}, u32[]{:S(2)}, u32[]{:S(2)}) collective-permute-start(bf16[32,10752]{1,0:T(8,128)(2,1)S(1)} %pad_maximum_fusion.2.refs_0_), channel_id=1, source_target_pairs={{0,12},{1,13},{2,14},{3,15},{4,8},{5,9},{6,10},{7,11},{8,4},{9,5},... | collective-permute-start | bytes 2064392 | tf_op jit(solution)/shard_map/ppermute | solution.py:22
  48.4 8.2 %collective-permute-start.9 = (bf16[16,10752]{1,0:T(8,128)(2,1)S(1)}, bf16[16,10752]{1,0:T(8,128)(2,1)S(1)}, u32[]{:S(2)}, u32[]{:S(2)}) collective-permute-start(bf16[16,10752]{1,0:T(8,128)(2,1)S(1)} %get-tuple-element.25), channel_id=1, source_target_pairs={{0,48},{1,49},{2,50},{3,51},{4,52},{5,53},{6,54},{7,55},{8,56},{9,... | collective-permute-start | bytes 1032200 | tf_op jit(solution)/shard_map/ppermute | solution.py:22
  48.9 14.3 %collective-permute-start.22 = (bf16[16,10752]{1,0:T(8,128)(2,1)S(1)}, bf16[16,10752]{1,0:T(8,128)(2,1)S(1)}, u32[]{:S(2)}, u32[]{:S(2)}) collective-permute-start(bf16[16,10752]{1,0:T(8,128)(2,1)S(1)} %get-tuple-element.33), channel_id=1, source_target_pairs={{0,4},{1,5},{2,6},{3,7},{4,0},{5,1},{6,2},{7,3},{8,12},{9,13},{10,... | collective-permute-start | bytes 1032200 | tf_op jit(solution)/shard_map/ppermute | solution.py:22
  50.7 12.5 %collective-permute-start.23 = (bf16[16,10752]{1,0:T(8,128)(2,1)S(1)}, bf16[16,10752]{1,0:T(8,128)(2,1)S(1)}, u32[]{:S(2)}, u32[]{:S(2)}) collective-permute-start(bf16[16,10752]{1,0:T(8,128)(2,1)S(1)} %get-tuple-element.34), channel_id=1, source_target_pairs={{0,12},{1,13},{2,14},{3,15},{4,8},{5,9},{6,10},{7,11},{8,4},{9,5},... | collective-permute-start | bytes 1032200 | tf_op jit(solution)/shard_map/ppermute | solution.py:22
  63.0 8.9 %collective-permute-start.10 = (bf16[16,7168]{1,0:T(8,128)(2,1)S(1)}, bf16[16,7168]{1,0:T(8,128)(2,1)S(1)}, u32[]{:S(2)}, u32[]{:S(2)}) collective-permute-start(bf16[16,7168]{1,0:T(8,128)(2,1)S(1)} %get-tuple-element.29), channel_id=1, source_target_pairs={{0,48},{1,49},{2,50},{3,51},{4,52},{5,53},{6,54},{7,55},{8,56},{9,... | collective-permute-start | bytes 688136 | tf_op jit(solution)/shard_map/ppermute | solution.py:22
  63.1 10.4 %collective-permute-start.12 = (bf16[16,7168]{1,0:T(8,128)(2,1)S(1)}, bf16[16,7168]{1,0:T(8,128)(2,1)S(1)}, u32[]{:S(2)}, u32[]{:S(2)}) collective-permute-start(bf16[16,7168]{1,0:T(8,128)(2,1)S(1)} %get-tuple-element.31), channel_id=1, source_target_pairs={{0,16},{1,17},{2,18},{3,19},{4,20},{5,21},{6,22},{7,23},{8,24},{9,... | collective-permute-start | bytes 688136 | tf_op jit(solution)/shard_map/ppermute | solution.py:22
  67.3 9.3 %collective-permute-start.24 = (bf16[32,7296]{1,0:T(8,128)(2,1)S(1)}, bf16[32,7296]{1,0:T(8,128)(2,1)S(1)}, u32[]{:S(2)}, u32[]{:S(2)}) collective-permute-start(bf16[32,7296]{1,0:T(8,128)(2,1)S(1)} %get-tuple-element.41), channel_id=1, source_target_pairs={{0,4},{1,5},{2,6},{3,7},{4,0},{5,1},{6,2},{7,3},{8,12},{9,13},{10,... | collective-permute-start | bytes 1400840 | tf_op jit(solution)/shard_map/ppermute | solution.py:22
  69.3 16.4 %collective-permute-start.25 = (bf16[32,7296]{1,0:T(8,128)(2,1)S(1)}, bf16[32,7296]{1,0:T(8,128)(2,1)S(1)}, u32[]{:S(2)}, u32[]{:S(2)}) collective-permute-start(bf16[32,7296]{1,0:T(8,128)(2,1)S(1)} %get-tuple-element.42), channel_id=1, source_target_pairs={{0,8},{1,9},{2,10},{3,11},{4,12},{5,13},{6,14},{7,15},{8,0},{9,1},... | collective-permute-start | bytes 1400840 | tf_op jit(solution)/shard_map/ppermute | solution.py:22
  69.7 16.1 %collective-permute-start.26 = (bf16[32,7296]{1,0:T(8,128)(2,1)S(1)}, bf16[32,7296]{1,0:T(8,128)(2,1)S(1)}, u32[]{:S(2)}, u32[]{:S(2)}) collective-permute-start(bf16[32,7296]{1,0:T(8,128)(2,1)S(1)} %get-tuple-element.43), channel_id=1, source_target_pairs={{0,12},{1,13},{2,14},{3,15},{4,8},{5,9},{6,10},{7,11},{8,4},{9,5},... | collective-permute-start | bytes 1400840 | tf_op jit(solution)/shard_map/ppermute | solution.py:22
  71.9 18.5 %collective-permute-start.11 = (bf16[32,7168]{1,0:T(8,128)(2,1)S(1)}, bf16[32,7168]{1,0:T(8,128)(2,1)S(1)}, u32[]{:S(2)}, u32[]{:S(2)}) collective-permute-start(bf16[32,7168]{1,0:T(8,128)(2,1)S(1)} %pad_maximum_fusion.3), channel_id=1, source_target_pairs={{0,16},{1,17},{2,18},{3,19},{4,20},{5,21},{6,22},{7,23},{8,24},{9,... | collective-permute-start | bytes 1376264 | tf_op jit(solution)/shard_map/ppermute | solution.py:22
  73.6 16.8 %collective-permute-start.13 = (bf16[32,7168]{1,0:T(8,128)(2,1)S(1)}, bf16[32,7168]{1,0:T(8,128)(2,1)S(1)}, u32[]{:S(2)}, u32[]{:S(2)}) collective-permute-start(bf16[32,7168]{1,0:T(8,128)(2,1)S(1)} %pad_maximum_fusion.4), channel_id=1, source_target_pairs={{0,48},{1,49},{2,50},{3,51},{4,52},{5,53},{6,54},{7,55},{8,56},{9,... | collective-permute-start | bytes 1376264 | tf_op jit(solution)/shard_map/ppermute | solution.py:22
  86.4 8.9 %collective-permute-start.27 = (bf16[8,7296]{1,0:T(8,128)(2,1)S(1)}, bf16[8,7296]{1,0:T(8,128)(2,1)S(1)}, u32[]{:S(2)}, u32[]{:S(2)}) collective-permute-start(bf16[8,7296]{1,0:T(8,128)(2,1)S(1)} %get-tuple-element.51), channel_id=1, source_target_pairs={{0,16},{1,17},{2,18},{3,19},{4,20},{5,21},{6,22},{7,23},{8,24},{9,... | collective-permute-start | bytes 350216 | tf_op jit(solution)/shard_map/ppermute | solution.py:22
  87.7 7.6 %collective-permute-start.28 = (bf16[8,7296]{1,0:T(8,128)(2,1)S(1)}, bf16[8,7296]{1,0:T(8,128)(2,1)S(1)}, u32[]{:S(2)}, u32[]{:S(2)}) collective-permute-start(bf16[8,7296]{1,0:T(8,128)(2,1)S(1)} %get-tuple-element.53), channel_id=1, source_target_pairs={{0,32},{1,33},{2,34},{3,35},{4,36},{5,37},{6,38},{7,39},{8,40},{9,... | collective-permute-start | bytes 350216 | tf_op jit(solution)/shard_map/ppermute | solution.py:22
  88.3 7.0 %collective-permute-start.29 = (bf16[8,7296]{1,0:T(8,128)(2,1)S(1)}, bf16[8,7296]{1,0:T(8,128)(2,1)S(1)}, u32[]{:S(2)}, u32[]{:S(2)}) collective-permute-start(bf16[8,7296]{1,0:T(8,128)(2,1)S(1)} %get-tuple-element.52), channel_id=1, source_target_pairs={{0,48},{1,49},{2,50},{3,51},{4,52},{5,53},{6,54},{7,55},{8,56},{9,... | collective-permute-start | bytes 350216 | tf_op jit(solution)/shard_map/ppermute | solution.py:22
  100.4 8.9 %collective-permute-start.30 = (f32[2,14464]{1,0:T(2,128)S(1)}, f32[2,14464]{1,0:T(2,128)S(1)}, u32[]{:S(2)}, u32[]{:S(2)}) collective-permute-start(f32[2,14464]{1,0:T(2,128)S(1)} %get-tuple-element.54), channel_id=1, source_target_pairs={{0,1},{1,0},{2,3},{3,2},{4,5},{5,4},{6,7},{7,6},{8,9},{9,8},{10,11... | collective-permute-start | bytes 347144 | tf_op jit(solution)/shard_map/ppermute | solution.py:22
  114.2 14.7 %collective-permute-start.33 = (bf16[2,7168]{1,0:T(2,128)(2,1)S(1)}, bf16[2,7168]{1,0:T(2,128)(2,1)S(1)}, u32[]{:S(2)}, u32[]{:S(2)}) collective-permute-start(bf16[2,7168]{1,0:T(2,128)(2,1)S(1)} %get-tuple-element.63), channel_id=1, source_target_pairs={{0,192},{64,128},{128,64},{192,0},{1,193},{65,129},{129,65},{193,1... | collective-permute-start | bytes 86024 | tf_op jit(solution)/shard_map/ppermute | solution.py:37
  (17 other events, 134.9 us)
